TPU v7x, 128 devices: a whole 4x4x4 slice. The times are simulated.
128 devices in a mesh: ctx: 32 (over z_lo, x, y), wt: 4 (over z_hi, core).
Axes of the slice: x: 4, y: 4, z: 4 (z_hi: 2, z_lo: 2; z = z_hi * 2 + z_lo), core: 2. Of those that a mesh axis runs over, the one named last changes fastest.
Arguments:
- tokens: bfloat16 [4, 4096, 2048], P('wt', 'ctx'), may hold values from -6 to 6
- cotangent: bfloat16 [4, 4096, 2048], P('wt', 'ctx'), may hold values from -6 to 6
- block_map: int32 [64], replicated, may hold values from 0 to 63, as said below
- document_ids: int32 [4, 4096], P('wt'), may hold values from 0 to 2, as said below
- positions: int32 [4, 4096], P('wt', 'ctx'), may hold values from 0 to 8190, as said below
- first_gain: float32 [2048], replicated, may hold values from 0.1 to 1.9
- query_weight: bfloat16 [2048, 1536], P(('ctx', 'wt')), may hold values from -0.125 to 0.125
- key_weight: bfloat16 [2048, 384], P(('ctx', 'wt')), may hold values from -0.125 to 0.125
- value_weight: bfloat16 [2048, 384], P(('ctx', 'wt')), may hold values from -0.125 to 0.125
- out_weight: bfloat16 [2048, 1536], P(('ctx', 'wt')), may hold values from -6 to 6
- query_gain: float32 [64], replicated, may hold values from 0.1 to 1.9
- key_gain: float32 [64], replicated, may hold values from 0.1 to 1.9
- second_gain: float32 [2048], replicated, may hold values from 0.1 to 1.9
- gate_weight: bfloat16 [2048, 4864], P(('ctx', 'wt')), may hold values from -0.125 to 0.125
- up_weight: bfloat16 [2048, 4864], P(('ctx', 'wt')), may hold values from -0.125 to 0.125
- down_weight: bfloat16 [2048, 4864], P(('ctx', 'wt')), may hold values from -0.078125 to 0.078125
Outputs:
- activations: bfloat16 [4, 4096, 2048], P('wt', 'ctx')
- token_grad: bfloat16 [4, 4096, 2048], P('wt', 'ctx')
- first_gain_grad: float32 [2048], replicated
- query_weight_grad: float32 [2048, 1536], P(('ctx', 'wt'))
- key_weight_grad: float32 [2048, 384], P(('ctx', 'wt'))
- value_weight_grad: float32 [2048, 384], P(('ctx', 'wt'))
- out_weight_grad: float32 [2048, 1536], P(('ctx', 'wt'))
- query_gain_grad: float32 [64], replicated
- key_gain_grad: float32 [64], replicated
- second_gain_grad: float32 [2048], replicated
- gate_weight_grad: float32 [2048, 4864], P(('ctx', 'wt'))
- up_weight_grad: float32 [2048, 4864], P(('ctx', 'wt'))
- down_weight_grad: float32 [2048, 4864], P(('ctx', 'wt'))
Inputs may be any that keep to these rules, and one draw needn't show every extreme that they name: `block_map`: entry s is the initial block held by stored slot s (stored rows s * 64 to (s + 1) * 64 - 1). Slots 2c and 2c + 1 hold blocks m_c and 63 - m_c, and the m_c form a permutation of 0 to 31. `document_ids`: in initial order (block b holds positions b * 64 to (b + 1) * 64 - 1) the ids never fall; 0, 1 and 2 all occur; document 0 holds at least 3968 tokens. `positions`: within a document the position rises by one per initial position; documents 1 and 2 start at 0, document 0 ends at 8190.
All inputs are finite; a program needn't handle non-finite values.
Results may differ from a plain program's by a relative error of at most 0.015.
Values may be sent and summed in bfloat16 or wider, within the bound.
A program may use at most 384 MiB of HBM per device.

v0:
```python
import math

import jax
import jax.numpy as jnp
from jax import lax
from jax.sharding import PartitionSpec as P

EPSILON = 1e-06
ROPE_BASE = 10000.0


def norm_forward(values, gain):
    inverse = lax.rsqrt(jnp.mean(values * values, axis=-1, keepdims=True) + EPSILON)
    normed = values * inverse
    return (normed * gain, normed, inverse)


def norm_backward(grads, gain, normed, inverse):
    scaled = grads * gain
    back = inverse * (scaled - normed * jnp.mean(scaled * normed, axis=-1, keepdims=True))
    return (back, grads * normed)


def rotate(values, cosine, sine):
    halfway = values.shape[-1] // 2
    first = values[..., :halfway]
    second = values[..., halfway:]
    return jnp.concatenate(
        [first * cosine - second * sine, second * cosine + first * sine], axis=-1
    )


def unrotate(grads, cosine, sine):
    halfway = grads.shape[-1] // 2
    first = grads[..., :halfway]
    second = grads[..., halfway:]
    return jnp.concatenate(
        [first * cosine + second * sine, second * cosine - first * sine], axis=-1
    )


def add_into(source, pieces):
    return tuple((jnp.dot(source, piece, preferred_element_type=jnp.float32) for piece in pieces))


def write_into(sources, pieces):
    update = sum(
        (
            lax.dot_general(
                source, piece, (((1,), (1,)), ((), ())), preferred_element_type=jnp.float32
            )
            for source, piece in zip(sources, pieces)
        )
    )
    return update


def body(
    tokens,
    cotangent,
    block_map,
    document_ids,
    positions,
    first_gain,
    query_weight,
    key_weight,
    value_weight,
    out_weight,
    query_gain,
    key_gain,
    second_gain,
    gate_weight,
    up_weight,
    down_weight,
):
    rows = tokens[0].astype(jnp.float32)
    local_rows = rows.shape[0]
    block_rows = local_rows // 2
    head_size = query_gain.shape[0]
    query_width = query_weight.shape[1]
    kv_width = key_weight.shape[1]
    kv_heads = kv_width // head_size
    query_heads = query_width // head_size
    group = query_heads // kv_heads
    hidden = gate_weight.shape[1]
    ctx_count = lax.axis_size("ctx")
    length = local_rows * ctx_count
    scale = 1.0 / math.sqrt(head_size)
    offsets = jnp.arange(block_rows, dtype=jnp.int32)
    own_blocks = lax.dynamic_slice_in_dim(block_map, lax.axis_index("ctx") * 2, 2)
    query_anchor = (own_blocks[:, None] * block_rows + offsets[None, :]).reshape(local_rows)
    key_anchor = (block_map[:, None] * block_rows + offsets[None, :]).reshape(length)
    doc_table = document_ids[0]
    places = jnp.arange(length, dtype=jnp.int32)
    query_doc = jnp.sum(
        jnp.where(query_anchor[:, None] == places[None, :], doc_table[None, :], 0), axis=1
    )
    doc_start = jnp.sum((doc_table[None, :] < query_doc[:, None]).astype(jnp.int32), axis=1)
    halfway = head_size // 2
    inverse_freq = ROPE_BASE ** (-(jnp.arange(halfway, dtype=jnp.float32) * 2.0) / head_size)
    angle = positions[0].astype(jnp.float32)[:, None] * inverse_freq[None, :]
    cosine = jnp.cos(angle)[:, None, :]
    sine = jnp.sin(angle)[:, None, :]
    first_out, first_hat, first_inv = norm_forward(rows, first_gain)
    first_low = first_out.astype(jnp.bfloat16)
    query_pre, key_pre, value_pre = add_into(
        first_low,
        (
            lax.all_gather(query_weight, ("ctx", "wt"), axis=0, tiled=True),
            lax.all_gather(key_weight, ("ctx", "wt"), axis=0, tiled=True),
            lax.all_gather(value_weight, ("ctx", "wt"), axis=0, tiled=True),
        ),
    )
    query_heads_in = query_pre.reshape(local_rows, query_heads, head_size)
    query_normed, query_hat, query_inv = norm_forward(query_heads_in, query_gain)
    query_low = (
        rotate(query_normed, cosine, sine)
        .astype(jnp.bfloat16)
        .reshape(local_rows, kv_heads, group, head_size)
    )
    key_heads_in = key_pre.reshape(local_rows, kv_heads, head_size)
    key_normed, key_hat, key_inv = norm_forward(key_heads_in, key_gain)
    key_low = rotate(key_normed, cosine, sine).astype(jnp.bfloat16).reshape(local_rows, kv_width)
    value_low = value_pre.astype(jnp.bfloat16)
    key_all, value_all = (
        lax.all_gather(key_low, "ctx", axis=0, tiled=True),
        lax.all_gather(value_low, "ctx", axis=0, tiled=True),
    )
    key_block = min(512, length)
    block_count = length // key_block
    keys_split = key_all.reshape(block_count, key_block, kv_heads, head_size)
    values_split = value_all.reshape(block_count, key_block, kv_heads, head_size)
    anchor_split = key_anchor.reshape(block_count, key_block)

    def scores_for(key_piece, anchor_piece):
        raw_scores = (
            jnp.einsum("qhgd,khd->hgqk", query_low, key_piece, preferred_element_type=jnp.float32)
            * scale
        )
        allowed = (anchor_piece[None, :] <= query_anchor[:, None]) & (
            anchor_piece[None, :] >= doc_start[:, None]
        )
        return jnp.where(allowed[None, None], raw_scores, -1e30)

    def max_step(carried, items):
        running_top, running_sum = carried
        key_piece, anchor_piece = items
        scores = scores_for(key_piece, anchor_piece)
        new_top = jnp.maximum(running_top, jnp.max(scores, axis=-1))
        running_sum = running_sum * jnp.exp(running_top - new_top) + jnp.sum(
            jnp.exp(scores - new_top[..., None]), axis=-1
        )
        return ((new_top, running_sum), None)

    start_top = jnp.full((kv_heads, group, local_rows), -1e30, jnp.float32)
    start_sum = jnp.zeros((kv_heads, group, local_rows), jnp.float32)
    (final_top, final_sum), _ = lax.scan(
        max_step, (start_top, start_sum), (keys_split, anchor_split)
    )
    log_total = final_top + jnp.log(final_sum)

    def value_step(carried, items):
        rounded_sum, exact_sum = carried
        key_piece, value_piece, anchor_piece = items
        weights = jnp.exp(scores_for(key_piece, anchor_piece) - log_total[..., None])
        rounded_sum = rounded_sum + jnp.einsum(
            "hgqk,khd->qhgd",
            weights.astype(jnp.bfloat16),
            value_piece,
            preferred_element_type=jnp.float32,
        )
        exact_sum = exact_sum + jnp.einsum(
            "hgqk,khd->qhgd",
            weights,
            value_piece.astype(jnp.float32),
            preferred_element_type=jnp.float32,
        )
        return ((rounded_sum, exact_sum), None)

    zero_heads = jnp.zeros((local_rows, kv_heads, group, head_size), jnp.float32)
    (attended, exact_out), _ = lax.scan(
        value_step, (zero_heads, zero_heads), (keys_split, values_split, anchor_split)
    )
    merged = attended.reshape(local_rows, query_width).astype(jnp.bfloat16)
    attn_branch = write_into(
        (merged,), (lax.all_gather(out_weight, ("ctx", "wt"), axis=0, tiled=True),)
    )
    mixed = rows + attn_branch
    second_out, second_hat, second_inv = norm_forward(mixed, second_gain)
    second_low = second_out.astype(jnp.bfloat16)
    gate, upward = add_into(
        second_low,
        (
            lax.all_gather(gate_weight, ("ctx", "wt"), axis=0, tiled=True),
            lax.all_gather(up_weight, ("ctx", "wt"), axis=0, tiled=True),
        ),
    )
    product = (jax.nn.silu(gate) * upward).astype(jnp.bfloat16)
    ffn_branch = write_into(
        (product,), (lax.all_gather(down_weight, ("ctx", "wt"), axis=0, tiled=True),)
    )
    activations = (mixed + ffn_branch).astype(jnp.bfloat16)[None]
    grad_out = cotangent[0]
    (grad_product,) = add_into(
        grad_out, (lax.all_gather(down_weight, ("ctx", "wt"), axis=0, tiled=True),)
    )
    sigmoid_gate = jax.nn.sigmoid(gate)
    grad_gate = (grad_product * upward * sigmoid_gate * (1.0 + gate * (1.0 - sigmoid_gate))).astype(
        jnp.bfloat16
    )
    grad_upward = (grad_product * gate * sigmoid_gate).astype(jnp.bfloat16)
    grad_second = write_into(
        (grad_gate, grad_upward),
        (
            lax.all_gather(gate_weight, ("ctx", "wt"), axis=0, tiled=True),
            lax.all_gather(up_weight, ("ctx", "wt"), axis=0, tiled=True),
        ),
    )
    second_back, second_terms = norm_backward(grad_second, second_gain, second_hat, second_inv)
    grad_mixed = grad_out.astype(jnp.float32) + second_back
    grad_branch = grad_mixed.astype(jnp.bfloat16)
    (grad_merged,) = add_into(
        grad_branch, (lax.all_gather(out_weight, ("ctx", "wt"), axis=0, tiled=True),)
    )
    grad_heads = grad_merged.astype(jnp.bfloat16).reshape(local_rows, kv_heads, group, head_size)
    delta = jnp.einsum("qhgd,qhgd->hgq", grad_heads.astype(jnp.float32), exact_out)

    def backward_step(grad_query, items):
        key_piece, value_piece, anchor_piece = items
        weights = jnp.exp(scores_for(key_piece, anchor_piece) - log_total[..., None])
        grad_weights = jnp.einsum(
            "qhgd,khd->hgqk", grad_heads, value_piece, preferred_element_type=jnp.float32
        )
        grad_scores = (weights * (grad_weights - delta[..., None])).astype(jnp.bfloat16)
        grad_query = (
            grad_query
            + jnp.einsum(
                "hgqk,khd->qhgd", grad_scores, key_piece, preferred_element_type=jnp.float32
            )
            * scale
        )
        grad_keys = (
            jnp.einsum("hgqk,qhgd->khd", grad_scores, query_low, preferred_element_type=jnp.float32)
            * scale
        )
        grad_values = jnp.einsum(
            "hgqk,qhgd->khd",
            weights.astype(jnp.bfloat16),
            grad_heads,
            preferred_element_type=jnp.float32,
        )
        return (grad_query, (grad_keys, grad_values))

    grad_query_rot, (keys_grads, values_grads) = lax.scan(
        backward_step, zero_heads, (keys_split, values_split, anchor_split)
    )
    own_key_grad, own_value_grad = (
        lax.psum_scatter(
            keys_grads.reshape(length, kv_width), "ctx", scatter_dimension=0, tiled=True
        ),
        lax.psum_scatter(
            values_grads.reshape(length, kv_width), "ctx", scatter_dimension=0, tiled=True
        ),
    )
    query_unrot = unrotate(grad_query_rot.reshape(local_rows, query_heads, head_size), cosine, sine)
    query_back, query_terms = norm_backward(query_unrot, query_gain, query_hat, query_inv)
    grad_query = query_back.reshape(local_rows, query_width).astype(jnp.bfloat16)
    key_unrot = unrotate(own_key_grad.reshape(local_rows, kv_heads, head_size), cosine, sine)
    key_back, key_terms = norm_backward(key_unrot, key_gain, key_hat, key_inv)
    grad_key = key_back.reshape(local_rows, kv_width).astype(jnp.bfloat16)
    grad_value = own_value_grad.astype(jnp.bfloat16)
    grad_first = write_into(
        (grad_query, grad_key, grad_value),
        (
            lax.all_gather(query_weight, ("ctx", "wt"), axis=0, tiled=True),
            lax.all_gather(key_weight, ("ctx", "wt"), axis=0, tiled=True),
            lax.all_gather(value_weight, ("ctx", "wt"), axis=0, tiled=True),
        ),
    )
    first_back, first_terms = norm_backward(grad_first, first_gain, first_hat, first_inv)
    token_grad = (grad_mixed + first_back).astype(jnp.bfloat16)[None]

    def outer(left, right):
        return lax.dot_general(
            left, right, (((0,), (0,)), ((), ())), preferred_element_type=jnp.float32
        )

    packed = lax.psum_scatter(
        jnp.concatenate(
            [
                outer(first_low, grad_query),
                outer(first_low, grad_key),
                outer(first_low, grad_value),
                outer(grad_branch, merged),
                outer(second_low, grad_gate),
                outer(second_low, grad_upward),
                outer(grad_out, product),
            ],
            axis=1,
        ),
        ("ctx", "wt"),
        scatter_dimension=0,
        tiled=True,
    )
    bounds = [0, query_width, kv_width, kv_width, query_width, hidden, hidden, hidden]
    edges = [sum(bounds[: index + 1]) for index in range(len(bounds))]
    pieces_out = [packed[:, edges[index] : edges[index + 1]] for index in range(7)]
    first_gain_grad, second_gain_grad, query_gain_grad, key_gain_grad = lax.psum(
        (
            jnp.sum(first_terms, axis=0),
            jnp.sum(second_terms, axis=0),
            jnp.sum(query_terms, axis=(0, 1)),
            jnp.sum(key_terms, axis=(0, 1)),
        ),
        ("ctx", "wt"),
    )
    return (
        activations,
        token_grad,
        first_gain_grad,
        pieces_out[0],
        pieces_out[1],
        pieces_out[2],
        pieces_out[3],
        query_gain_grad,
        key_gain_grad,
        second_gain_grad,
        pieces_out[4],
        pieces_out[5],
        pieces_out[6],
    )


def solution(mesh):
    in_specs = (
        P("wt", "ctx", None),
        P("wt", "ctx", None),
        P(),
        P("wt", None),
        P("wt", "ctx"),
        P(),
        P(("ctx", "wt"), None),
        P(("ctx", "wt"), None),
        P(("ctx", "wt"), None),
        P(("ctx", "wt"), None),
        P(),
        P(),
        P(),
        P(("ctx", "wt"), None),
        P(("ctx", "wt"), None),
        P(("ctx", "wt"), None),
    )
    out_specs = (
        P("wt", "ctx", None),
        P("wt", "ctx", None),
        P(),
        P(("ctx", "wt"), None),
        P(("ctx", "wt"), None),
        P(("ctx", "wt"), None),
        P(("ctx", "wt"), None),
        P(),
        P(),
        P(),
        P(("ctx", "wt"), None),
        P(("ctx", "wt"), None),
        P(("ctx", "wt"), None),
    )
    return jax.shard_map(body, mesh=mesh, in_specs=in_specs, out_specs=out_specs, check_vma=False)
```

profile of v0, /device:TPU:1, one launch (start us, length us, event | category | flops | bytes accessed | tf_op | source)
XLA Modules:
  0.0 4275.2 jit_solution(3772273014028191435)
XLA Ops:
  10.0 196.2 %all-gather.10.cloned.1.call-done = bf16[2048,384]{1,0:T(8,128)(2,1)} async-done(((bf16[16,384]{1,0:T(8,128)(2,1)}), bf16[2048,384]{1,0:T(8,128)(2,1)}) %all-gather.10.cloned.1.call-update) | async-done | bytes 1572880 | tf_op jit(solution)/shard_map/all_gather | solution.py:111
  209.8 190.0 %all-gather.14.cloned.1.call-done = bf16[2048,384]{1,0:T(8,128)(2,1)} async-done(((bf16[16,384]{1,0:T(8,128)(2,1)}), bf16[2048,384]{1,0:T(8,128)(2,1)}) %all-gather.14.cloned.1.call-update) | async-done | bytes 1572880 | tf_op jit(solution)/shard_map/all_gather | solution.py:110
  411.3 124.5 %all-gather.12.cloned.1.call-done = bf16[4096,384]{1,0:T(8,128)(2,1)} async-done(((bf16[128,384]{1,0:T(8,128)(2,1)}), bf16[4096,384]{1,0:T(8,128)(2,1)}) %all-gather.12.cloned.1.call-update) | async-done | bytes 3145744 | tf_op jit(solution)/shard_map/all_gather | solution.py:127
  535.8 4.7 copy.70
  546.6 126.2 %all-gather.16.cloned.1.call-done = bf16[4096,384]{0,1:T(8,128)(2,1)} async-done(((bf16[128,384]{0,1:T(8,128)(2,1)}), bf16[4096,384]{0,1:T(8,128)(2,1)}) %all-gather.16.cloned.1.call-update) | async-done | bytes 3145744 | tf_op jit(solution)/shard_map/all_gather | solution.py:126
  678.9 213.0 %all-gather.18.cloned.1.call-done = bf16[2048,1536]{1,0:T(8,128)(2,1)} async-done(((bf16[16,1536]{1,0:T(8,128)(2,1)}), bf16[2048,1536]{1,0:T(8,128)(2,1)}) %all-gather.18.cloned.1.call-update) | async-done | bytes 6291472 | tf_op jit(solution)/shard_map/all_gather | solution.py:109
  891.9 8.8 copy.72
  906.4 39.9 while.41
  946.9 72.6 %while.42 = (s32[]{:T(128)}, f32[128,6,4,64]{0,3,2,1:T(8,128)S(1)}, f32[128,6,4,64]{0,3,2,1:T(8,128)S(1)}, bf16[8,512,6,64]{1,3,2,0:T(8,128)(2,1)}, s32[8,512]{1...) while((s32[]{:T(128)}, f32[128,6,4,64]{0,3,2,1:T(8,128)S(1)}, ...), condition=%wide.region_10.11_spmd.clone, body=%wide.region_9.10_spmd.clone.sunk | while | flops 615972992 | bytes 23823008 | solution.py:181
  1021.8 71.5 %all-gather.20.cloned.1.call-done = bf16[2048,1536]{1,0:T(8,128)(2,1)} async-done(((bf16[16,1536]{1,0:T(8,128)(2,1)}), bf16[2048,1536]{1,0:T(8,128)(2,1)}) %all-gather.20.cloned.1.call-update) | async-done | bytes 6291472 | tf_op jit(solution)/shard_map/all_gather | solution.py:186
  1093.3 5.0 multiply_reduce_fusion.2
  1098.6 214.8 %all-gather.24.cloned.1.call-done = bf16[2048,4864]{1,0:T(8,128)(2,1)} async-done(((bf16[16,4864]{1,0:T(8,128)(2,1)}), bf16[2048,4864]{1,0:T(8,128)(2,1)}) %all-gather.24.cloned.1.call-update) | async-done | bytes 19922960 | tf_op jit(solution)/shard_map/all_gather | solution.py:195
  1313.4 10.9 fusion.120
  1324.4 209.6 %all-gather.22.cloned.1.call-done = bf16[2048,4864]{1,0:T(8,128)(2,1)} async-done(((bf16[16,4864]{1,0:T(8,128)(2,1)}), bf16[2048,4864]{1,0:T(8,128)(2,1)}) %all-gather.22.cloned.1.call-update) | async-done | bytes 19922960 | tf_op jit(solution)/shard_map/all_gather | solution.py:194
  1534.0 10.9 fusion.119
  1544.8 209.4 %all-gather.26.cloned.1.call-done = bf16[2048,4864]{1,0:T(8,128)(2,1)} async-done(((bf16[16,4864]{1,0:T(8,128)(2,1)}), bf16[2048,4864]{1,0:T(8,128)(2,1)}) %all-gather.26.cloned.1.call-update) | async-done | bytes 19922960 | tf_op jit(solution)/shard_map/all_gather | solution.py:200
  1754.3 13.6 multiply_convert_fusion
  1767.9 14.6 fusion.121
  1782.5 11.8 multiply_reduce_fusion
  1802.8 376.1 %while.43 = (s32[]{:T(128)}, f32[128,6,4,64]{0,3,2,1:T(8,128)S(1)}, f32[8,512,6,64]{1,0,3,2:T(8,128)}, f32[8,512,6,64]{1,0,3,2:T(8,128)}, bf16[8,512,6,64]{1,3,2...) while((s32[]{:T(128)}, f32[128,6,4,64]{0,3,2,1:T(8,128)S(1)}, ...), condition=%wide.region_14.15_spmd.clone, body=%wide.region_13.14_spmd.clone.sunk | while | flops 1023344768 | bytes 40743612 | solution.py:254
  1816.5 16.7 dynamic_update_slice.11
  1833.2 16.7 dynamic_update_slice.12
  1863.5 16.7 dynamic_update_slice.11
  1880.2 16.7 dynamic_update_slice.12
  1910.5 16.7 dynamic_update_slice.11
  1927.1 16.7 dynamic_update_slice.12
  1957.5 16.7 dynamic_update_slice.11
  1974.1 16.7 dynamic_update_slice.12
  2004.5 16.7 dynamic_update_slice.11
  2021.1 16.7 dynamic_update_slice.12
  2051.5 16.7 dynamic_update_slice.11
  2068.1 16.7 dynamic_update_slice.12
  2098.4 16.7 dynamic_update_slice.11
  2115.1 16.7 dynamic_update_slice.12
  2145.4 16.7 dynamic_update_slice.11
  2162.1 16.7 dynamic_update_slice.12
  2178.9 11.3 copy.130
  2190.6 11.3 copy.131
  2203.7 6.5 convolution_dynamic-update-slice_fusion.3
  2210.2 131.3 %reduce-scatter.4.cloned.1.call-done = f32[128,384]{0,1:T(8,128)} async-done(((f32[4096,384]{0,1:T(8,128)}), f32[128,384]{0,1:T(8,128)}) %reduce-scatter.4.cloned.1.call-update) | async-done | bytes 196624 | tf_op jit(solution)/shard_map/reduce_scatter | solution.py:258
  2345.1 169.8 %reduce-scatter.6.cloned.1.call-done = f32[128,384]{0,1:T(8,128)} async-done(((f32[4096,384]{0,1:T(8,128)}), f32[128,384]{0,1:T(8,128)}) %reduce-scatter.6.cloned.1.call-update) | async-done | bytes 196624 | tf_op jit(solution)/shard_map/reduce_scatter | solution.py:261
  2518.2 6.5 convolution_dynamic-update-slice_fusion.2
  2524.7 15.6 convolution_dynamic-update-slice_fusion.1
  2540.3 15.5 convolution_dynamic-update-slice_fusion
  2555.9 15.5 bitcast_dynamic-update-slice_fusion
  2571.4 5.1 fusion.122
  2576.6 11.5 fusion.78
  2589.5 1672.4 %all-reduce = (f32[2048]{0:T(1024)}, f32[64]{0:T(128)}, f32[64]{0:T(128)}, f32[2048]{0:T(1024)}) all-reduce(f32[2048]{0:T(1024)S(1)} %get-tuple-element.385, f32[64]{0:T(128)S(1)} %get-tuple-element.383, f32[64]{0:T(128)S(1)} %get-tuple-element.387, f32[2048]{0:T(1024)S(1)} %copy-done.38), channel_id=1, replica_groups=mesh['ctx'=32,'wt'=4] {'ctx','wt'}, use_global_device_ids=true, to_apply=%region_21.22 | all-reduce | flops 4224 | bytes 33792 | tf_op jit(solution)/shard_map/psum | solution.py:308
  (401 shorter events, 283.9 us)
Async XLA Ops:
  7.2 396.2 %copy-start.43 = (f32[64]{0:T(128)S(1)}, f32[64]{0:T(128)}, u32[]{:S(2)}) copy-start(f32[64]{0:T(128)} %param.33) | copy-start | bytes 772
  7.2 401.0 %copy-start.46 = (s32[64]{0:T(128)S(1)}, s32[64]{0:T(128)}, u32[]{:S(2)}) copy-start(s32[64]{0:T(128)} %param.24) | copy-start | bytes 772
  7.2 402.7 %copy-start.37 = (s32[1,4096]{1,0:T(1,128)S(1)}, s32[1,4096]{1,0:T(1,128)}, u32[]{:S(2)}) copy-start(s32[1,4096]{1,0:T(1,128)} %param.25) | copy-start | bytes 49156
  7.2 199.0 %all-gather.10.cloned.1.call-start = ((), (), s32[]{:S(2)}) async-start(), calls=%async_computation.3 | async-start | bytes 1585152 | tf_op jit(solution)/shard_map/all_gather | solution.py:111
  7.9 391.9 %all-gather.14.cloned.1.call-start = ((), (), s32[]{:S(2)}) async-start(), calls=%async_computation.5 | async-start | bytes 1585152 | tf_op jit(solution)/shard_map/all_gather | solution.py:110
  8.7 527.1 %all-gather.12.cloned.1.call-start = ((), (), s32[]{:S(2)}) async-start(), calls=%async_computation.4 | async-start | bytes 3244032 | tf_op jit(solution)/shard_map/all_gather | solution.py:127
  10.0 890.7 %copy-start.39 = (f32[128]{0:T(128)}, f32[128]{0:T(128)S(1)}, u32[]{:S(2)}) copy-start(f32[128]{0:T(128)S(1)} %add_rsqrt_fusion.3) | copy-start | bytes 1540
  208.9 463.9 %all-gather.16.cloned.1.call-start = ((), (), s32[]{:S(2)}) async-start(), calls=%async_computation.6 | async-start | bytes 3244032 | tf_op jit(solution)/shard_map/all_gather | solution.py:126
  209.8 695.9 %copy-start.27 = (f32[128,32]{0,1:T(8,128)}, f32[128,32]{0,1:T(8,128)S(1)}, u32[]{:S(2)}) copy-start(f32[128,32]{0,1:T(8,128)S(1)} %get-tuple-element.475) | copy-start | bytes 49156
  209.8 695.9 %copy-start.29 = (f32[128,32]{0,1:T(8,128)}, f32[128,32]{0,1:T(8,128)S(1)}, u32[]{:S(2)}) copy-start(f32[128,32]{0,1:T(8,128)S(1)} %get-tuple-element.476) | copy-start | bytes 49156
  403.3 140.5 %copy-start.18 = (f32[128,6,64]{0,2,1:T(8,128)}, f32[128,6,64]{0,2,1:T(8,128)S(1)}, u32[]{:S(2)}) copy-start(f32[128,6,64]{0,2,1:T(8,128)S(1)} %get-tuple-element.478) | copy-start | bytes 589828
  404.7 487.2 %all-gather.18.cloned.1.call-start = ((), (), s32[]{:S(2)}) async-start(), calls=%async_computation.7 | async-start | bytes 6340608 | tf_op jit(solution)/shard_map/all_gather | solution.py:109
  405.2 688.1 %all-gather.20.cloned.1.call-start = ((), (), s32[]{:S(2)}) async-start(), calls=%async_computation.8 | async-start | bytes 6340608 | tf_op jit(solution)/shard_map/all_gather | solution.py:186
  405.8 907.6 %all-gather.24.cloned.1.call-start = ((), (), s32[]{:S(2)}) async-start(), calls=%async_computation.10 | async-start | bytes 20078592 | tf_op jit(solution)/shard_map/all_gather | solution.py:195
  406.6 1127.4 %all-gather.22.cloned.1.call-start = ((), (), s32[]{:S(2)}) async-start(), calls=%async_computation.9 | async-start | bytes 20078592 | tf_op jit(solution)/shard_map/all_gather | solution.py:194
  407.3 1346.9 %all-gather.26.cloned.1.call-start = ((), (), s32[]{:S(2)}) async-start(), calls=%async_computation.11 | async-start | bytes 20078592 | tf_op jit(solution)/shard_map/all_gather | solution.py:200
  408.1 1933.4 %reduce-scatter.4.cloned.1.call-start = ((), (), s32[]{:S(2)}) async-start(), calls=%async_computation.12 | async-start | bytes 6488064 | tf_op jit(solution)/shard_map/reduce_scatter | solution.py:258
  891.9 8.8 copy-start
  891.9 8.8 copy-start.25
  900.7 4.8 copy-start.41
  1020.3 73.0 %copy-start.22 = (f32[128,6,4,64]{0,3,2,1:T(8,128)}, f32[128,6,4,64]{0,3,2,1:T(8,128)S(1)}, u32[]{:S(2)}) copy-start(f32[128,6,4,64]{0,3,2,1:T(8,128)S(1)} %get-tuple-element.181) | copy-start | bytes 2359300
  1020.3 78.1 %copy-start.33 = (f32[2048]{0:T(1024)S(1)}, f32[2048]{0:T(1024)}, u32[]{:S(2)}) copy-start(f32[2048]{0:T(1024)} %param.34) | copy-start | bytes 24580
  1021.8 76.5 %copy-start.14 = (bf16[128,6,4,64]{0,3,2,1:T(8,128)(2,1)}, bf16[128,6,4,64]{0,3,2,1:T(8,128)(2,1)S(1)}, u32[]{:S(2)}) copy-start(bf16[128,6,4,64]{0,3,2,1:T(8,128)(2,1)S(1)} %convert_element_type.118) | copy-start | bytes 1179652
  1098.4 696.0 %copy-start.1 = (f32[128,2048]{1,0:T(8,128)}, f32[128,2048]{1,0:T(8,128)S(1)}, u32[]{:S(2)}) copy-start(f32[128,2048]{1,0:T(8,128)S(1)} %get-tuple-element.482) | copy-start | bytes 3145732
  1098.4 684.1 %copy-start.45 = (f32[128]{0:T(128)}, f32[128]{0:T(128)S(1)}, u32[]{:S(2)}) copy-start(f32[128]{0:T(128)S(1)} %add_rsqrt_fusion.2) | copy-start | bytes 1540
  1098.6 435.4 %copy-start.5 = (bf16[128,2048]{1,0:T(8,128)(2,1)}, bf16[128,2048]{1,0:T(8,128)(2,1)S(1)}, u32[]{:S(2)}) copy-start(bf16[128,2048]{1,0:T(8,128)(2,1)S(1)} %multiply_convert_fusion.3) | copy-start | bytes 1572868
  1782.5 11.8 copy-start.16
  1782.5 11.8 copy-start.34
  1794.3 6.8 copy-start.23
  2190.3 324.5 %reduce-scatter.6.cloned.1.call-start = ((), (), s32[]{:S(2)}) async-start(), calls=%async_computation.13 | async-start | bytes 6488064 | tf_op jit(solution)/shard_map/reduce_scatter | solution.py:261
  2202.0 1.6 copy-start.26
  2202.0 1.6 copy-start.40
  2202.0 2061.0 %reduce-scatter.8.cloned.1.call-start = ((), (), s32[]{:S(2)}) async-start(), calls=%async_computation.14 | async-start | bytes 152174592 | tf_op jit(solution)/shard_map/reduce_scatter | solution.py:288
  2203.6 138.7 %copy-start.19 = (f32[128,6,64]{0,2,1:T(8,128)S(1)}, f32[128,6,64]{0,2,1:T(8,128)}, u32[]{:S(2)}) copy-start(f32[128,6,64]{0,2,1:T(8,128)} %copy-done.18) | copy-start | bytes 589828
  2203.7 138.7 %copy-start.36 = (f32[128,6]{0,1:T(8,128)S(1)}, f32[128,6]{0,1:T(8,128)}, u32[]{:S(2)}) copy-start(f32[128,6]{0,1:T(8,128)} %copy-done.35) | copy-start | bytes 9220
  2203.7 138.7 %copy-start.44 = (f32[64]{0:T(128)S(1)}, f32[64]{0:T(128)}, u32[]{:S(2)}) copy-start(f32[64]{0:T(128)} %param.33) | copy-start | bytes 772
  2210.2 308.0 %copy-start.4 = (f32[128,2048]{1,0:T(8,128)S(1)}, f32[128,2048]{1,0:T(8,128)}, u32[]{:S(2)}) copy-start(f32[128,2048]{1,0:T(8,128)} %copy-done.3) | copy-start | bytes 3145732
  2210.2 308.0 %copy-start.15 = (bf16[128,6,4,64]{0,3,2,1:T(8,128)(2,1)S(1)}, bf16[128,6,4,64]{0,3,2,1:T(8,128)(2,1)}, u32[]{:S(2)}) copy-start(bf16[128,6,4,64]{0,3,2,1:T(8,128)(2,1)} %copy-done.14) | copy-start | bytes 1179652
  2518.2 6.5 copy-start.6
  2518.2 6.5 copy-start.13
  2524.7 15.6 copy-start.11
  2540.3 15.5 copy-start.9
  2540.3 15.5 copy-start.17
  2571.4 5.1 copy-start.2
  2571.4 5.1 copy-start.10
  2576.6 11.5 copy-start.12
  2576.6 12.1 copy-start.20
  2576.6 12.1 copy-start.21
  (11 other events, 10.7 us)
Sparse Core Ops, SparseCore 0:
  9.8 196.3 all-gather.9
  207.9 191.9 all-gather.13
  402.1 133.6 all-gather.11
  537.8 135.0 all-gather.15
  674.4 217.4 all-gather.17
  893.5 199.7 all-gather.19
  1095.0 218.3 all-gather.23
  1315.1 218.7 all-gather.21
  1535.7 218.5 all-gather.25
  2190.4 150.9 reduce-scatter.3
  2343.8 170.9 reduce-scatter.5
  2571.5 1638.3 reduce-scatter.7
where the time goes:
time: 4290 us; the launch traced here: 4280 us
  waiting for transfers between devices  1860 us (43%)
  blocking collectives  1670 us (39%)
  local copies, waits for them, and re-layouts  342 us (8%)
  matrix products  322 us (8%)
  other arithmetic  60 us (1%)
    psum x1, blocking collectives, body(): lax.psum((jnp.sum(first_terms, axis=0), jnp.sum(second_terms, axis=0), jn...  1670 us
    dynamic_update_slice x32, local copies, waits for them, and re-layouts, body(): lax.scan(backward_step, zero_heads, (keys_split, values_split, anchor_spl...  279 us
    all_gather x1, waiting for transfers between devices, body(): lax.all_gather(up_weight, ('ctx', 'wt'), axis=0, tiled=True)  215 us
    all_gather x1, waiting for transfers between devices, body(): lax.all_gather(query_weight, ('ctx', 'wt'), axis=0, tiled=True)  213 us
    all_gather x1, waiting for transfers between devices, body(): lax.all_gather(gate_weight, ('ctx', 'wt'), axis=0, tiled=True)  210 us
    all_gather x1, waiting for transfers between devices, body(): lax.all_gather(down_weight, ('ctx', 'wt'), axis=0, tiled=True)  209 us
    all_gather x1, waiting for transfers between devices, body(): lax.all_gather(value_weight, ('ctx', 'wt'), axis=0, tiled=True)  196 us
    all_gather x1, waiting for transfers between devices, body(): lax.all_gather(key_weight, ('ctx', 'wt'), axis=0, tiled=True)  190 us
  transfers between devices with their start and end apart: 12, of which 11 were waited for; matrix products, arithmetic and copies ran while one was open for 5% of the time, Pallas kernels for 0%

commit v1 on v0

v1 whole, which is shorter than its diff:
```python
import functools
import math

import jax
import jax.numpy as jnp
from jax import lax
from jax.experimental import pallas as pl
from jax.experimental.pallas import tpu as pltpu
from jax.sharding import PartitionSpec as P

EPSILON = 1e-06
ROPE_BASE = 10000.0
MESH = pl.DeviceIdType.MESH
BF16 = jnp.bfloat16
F32 = jnp.float32
ANY = pl.BlockSpec(memory_space=pl.ANY)
WEIGHT_DIMS = ("zl", "x", "y", "zh")
KEY_DIMS = ("zl", "x", "y")
SIZES = {"zl": 2, "x": 4, "y": 4, "zh": 2}
SPAN = {"x": 4, "y": 4, "z": 4, "p": 2, "k": 2}
GATHER_ORDERS = (("x", "y", "z"), ("y", "z", "x"), ("z", "x", "y"))
SCATTER_ORDERS = (("z", "y", "x"), ("x", "z", "y"), ("y", "x", "z"))
KEY_GATHER_ORDERS = (("p", "x", "y"), ("p", "y", "x"))
KEY_SCATTER_ORDERS = (("y", "x", "p"), ("x", "y", "p"))


class Spot:
    def __init__(self):
        ctx, wt = lax.axis_index("ctx"), lax.axis_index("wt")
        low, high = lax.div(ctx, 16), lax.div(wt, 2)
        self.at = {
            "x": lax.rem(lax.div(ctx, 4), 4),
            "y": lax.rem(ctx, 4),
            "z": high * 2 + low,
            "k": lax.rem(wt, 2),
            "p": low,
            "zl": low,
            "zh": high,
        }

    def device(self, axis, value):
        at = dict(self.at)
        if axis == "z":
            at["zl"], at["zh"] = lax.rem(value, 2), lax.div(value, 2)
        elif axis == "p":
            at["zl"] = value
        else:
            at[axis] = value
        return (at["zl"] * 16 + at["x"] * 4 + at["y"], at["zh"] * 2 + at["k"])

    def turn(self, axis, by):
        return lax.rem(self.at[axis] + by, SPAN[axis])

    def greet(self, reach):
        barrier = pltpu.get_barrier_semaphore()
        count = 0
        for axis, steps in reach:
            for by in steps:
                pl.semaphore_signal(
                    barrier,
                    inc=1,
                    device_id=self.device(axis, self.turn(axis, by)),
                    device_id_type=MESH,
                )
                count += 1
        pl.semaphore_wait(barrier, count)

    def slab(self, dims, full, axis, value):
        index = []
        for dim in dims:
            name = "z" if dim == "zh" or (dim == "zl" and "zh" in dims) else "p" if dim == "zl" else dim
            if name in full:
                index.append(slice(None))
            elif name == axis:
                index.append(
                    value if name != "z" else lax.rem(value, 2) if dim == "zl" else lax.div(value, 2)
                )
            else:
                index.append(self.at[dim])
        return tuple(index)


class Wires:
    def __init__(self, send, recv, local):
        self.send, self.recv, self.local = send, recv, local
        self.remotes = self.locals = 0

    def remote(self, source, target, device):
        at = self.remotes
        self.remotes += 1
        return pltpu.make_async_remote_copy(
            src_ref=source,
            dst_ref=target,
            send_sem=self.send.at[at],
            recv_sem=self.recv.at[at],
            device_id=device,
            device_id_type=MESH,
        )

    def copy(self, source, target):
        at = self.locals
        self.locals += 1
        return pltpu.make_async_copy(source, target, self.local.at[at])


def start(copies):
    for copy in copies:
        copy.start()
    return copies


def run(threads):
    threads = list(threads)
    while threads:
        for thread in list(threads):
            if next(thread, "end") == "end":
                threads.remove(thread)


def gather_lane(spot, wires, dims, order, parts, rows):
    sent = []
    for phase, axis in enumerate(order):
        full = order[:phase]
        me = spot.at[axis]

        def slab(part, value, first, count):
            ref, columns = part
            return ref.at[spot.slab(dims, full, axis, value) + (pl.ds(first, count), columns)]

        if SPAN[axis] == 2:
            other = spot.turn(axis, 1)
            copies = []
            for part in parts:
                mine = slab(part, me, 0, rows)
                copies.append(wires.remote(mine, mine, spot.device(axis, other)))
            sent += start(copies)
            yield
            for copy in copies:
                copy.wait_recv()
            continue
        right, left = spot.turn(axis, 1), spot.turn(axis, 3)
        copies = []
        for part in parts:
            mine = slab(part, me, 0, rows)
            copies.append(wires.remote(mine, mine, spot.device(axis, right)))
            copies.append(wires.remote(mine, mine, spot.device(axis, left)))
        sent += start(copies)
        yield
        for copy in copies:
            copy.wait_recv()
        copies = []
        for part in parts:
            one = slab(part, left, 0, rows // 2)
            two = slab(part, right, rows // 2, rows // 2)
            copies.append(wires.remote(one, one, spot.device(axis, right)))
            copies.append(wires.remote(two, two, spot.device(axis, left)))
        sent += start(copies)
        yield
        for copy in copies:
            copy.wait_recv()
    for copy in sent:
        copy.wait_send()


def each_block(shape, body):
    total = math.prod(shape)

    def one(step, _):
        index, rest = [], step
        for size in reversed(shape):
            index.append(lax.rem(rest, size))
            rest = lax.div(rest, size)
        body(tuple(reversed(index)))
        return 0

    lax.fori_loop(0, total, one, 0)


def slab_shape(dims, full):
    names = {"zl": "z" if "zh" in dims else "p", "zh": "z", "x": "x", "y": "y"}
    return tuple(SIZES[dim] if names[dim] in full else 1 for dim in dims)


def landing_shapes(dims, order, rows, width):
    shapes = []
    for phase, axis in enumerate(order):
        lead = slab_shape(dims, order[phase + 1 :])
        if SPAN[axis] == 2:
            shapes.append(lead + (rows, width))
        else:
            shapes += [lead + (rows // 2, width)] * 2 + [lead + (rows, width)] * 2
    return shapes


def scatter_lane(spot, wires, dims, order, source, held, landing, final, rows):
    landing = list(landing)
    sent = []
    half = rows // 2
    first_axis, first_full = order[0], order[1:]
    loads = []
    for by in [0, 1, 3] if SPAN[first_axis] == 4 else [0]:
        index = spot.slab(dims, first_full, first_axis, spot.turn(first_axis, by))
        loads.append(wires.copy(source.at[index], held.at[index]))
    start(loads)
    for phase, axis in enumerate(order):
        full = order[phase + 1 :]
        lead = slab_shape(dims, full)
        flat = tuple(slice(None) if size > 1 else 0 for size in lead)
        me = spot.at[axis]
        origin = source if phase == 0 else held

        def at(value, index):
            spots = spot.slab(dims, full, axis, value)
            return tuple(
                index[n] if isinstance(place, slice) else place for n, place in enumerate(spots)
            )

        last = phase == len(order) - 1
        if SPAN[axis] == 2:
            other = spot.turn(axis, 1)
            (whole,) = [landing.pop(0)]
            copy = wires.remote(
                origin.at[spot.slab(dims, full, axis, other)],
                whole.at[flat],
                spot.device(axis, other),
            )
            sent += start([copy])
            yield
            if phase == 0:
                for load in loads:
                    load.wait()
            copy.wait_recv()
            arrived = [whole]
        else:
            right, left = spot.turn(axis, 1), spot.turn(axis, 3)
            across = origin.at[spot.slab(dims, full, axis, spot.turn(axis, 2))]
            half_left, half_right, whole_left, whole_right = [landing.pop(0) for _ in range(4)]
            tail = (slice(None),) * sum(size > 1 for size in lead)
            copies = [
                wires.remote(
                    across.at[tail + (pl.ds(0, half),)], half_left.at[flat], spot.device(axis, right)
                ),
                wires.remote(
                    across.at[tail + (pl.ds(half, half),)],
                    half_right.at[flat],
                    spot.device(axis, left),
                ),
            ]
            sent += start(copies)
            yield
            if phase == 0:
                for load in loads:
                    load.wait()
            later = []
            for copy, arrived, value, rows_at, whole in (
                (copies[0], half_left, right, pl.ds(0, half), whole_left),
                (copies[1], half_right, left, pl.ds(half, half), whole_right),
            ):
                copy.wait_recv()

                def add(index):
                    place = at(value, index) + (rows_at,)
                    held[place] = held[place] + arrived[index]

                each_block(lead, add)
                onward = wires.remote(
                    held.at[spot.slab(dims, full, axis, value)],
                    whole.at[flat],
                    spot.device(axis, value),
                )
                later += start([onward])
            sent += later
            yield
            for copy in later:
                copy.wait_recv()
            arrived = [whole_left, whole_right]

        def total(index):
            place = at(me, index)
            value = held[place].astype(F32)
            for piece in arrived:
                value = value + piece[index].astype(F32)
            if last:
                final[...] = value
            else:
                held[place] = value.astype(BF16)

        each_block(lead, total)
    for copy in sent:
        copy.wait_send()


RING = (1, 2, 3)


def weight_gather_kernel(widths, lanes, *refs):
    count = len(widths)
    sources, pairs_in = refs[:count], refs[count : count + 2]
    outs, pairs_out = refs[count + 2 : 2 * count + 2], refs[2 * count + 2 : 2 * count + 4]
    spot, wires = Spot(), Wires(*refs[2 * count + 4 :])
    spot.greet((("x", (1, 3)), ("y", (1, 3)), ("z", (1, 3)), ("k", (1,))))
    core = spot.at["k"]
    sibling = spot.device("k", 1 - core)
    rows = pl.ds(pl.multiple_of(core * 16, 16), 16)
    own = tuple(spot.at[dim] for dim in WEIGHT_DIMS)
    local, remote, swaps = [], [], []
    for source, out, width in zip(sources, outs, widths):
        target = out.at[own + (rows,)]
        mine = pl.ds(pl.multiple_of(core * width, 128), width)
        theirs = pl.ds(pl.multiple_of((1 - core) * width, 128), width)
        local.append(wires.copy(source.at[:, mine], target))
        remote.append(wires.remote(source.at[:, theirs], target, sibling))
    for source, out in zip(pairs_in, pairs_out):
        local.append(wires.copy(source, out.at[core]))
        swaps.append(wires.remote(source, out.at[core], sibling))
    start(local + remote + swaps)
    for copy in local:
        copy.wait()
    for copy in remote:
        copy.wait()
    run(
        gather_lane(
            spot,
            wires,
            WEIGHT_DIMS,
            order,
            [(outs[at], pl.ds(first, wide)) for at, first, wide in parts],
            32,
        )
        for order, parts in zip(GATHER_ORDERS, lanes)
    )
    for copy in swaps:
        copy.wait()


def gather_weights(sources, pairs, lanes):
    widths = [source.shape[1] // 2 for source in sources]
    remotes = len(sources) + 2 + sum(len(parts) for parts in lanes) * 12
    out = [jax.ShapeDtypeStruct((2, 4, 4, 2, 32, width), BF16) for width in widths]
    out += [jax.ShapeDtypeStruct((2,) + pair.shape, pair.dtype) for pair in pairs]
    gathered = pl.pallas_call(
        functools.partial(weight_gather_kernel, widths, lanes),
        out_shape=out,
        in_specs=[ANY] * (len(sources) + 2),
        out_specs=[ANY] * len(out),
        scratch_shapes=[
            pltpu.SemaphoreType.DMA((remotes,)),
            pltpu.SemaphoreType.DMA((remotes,)),
            pltpu.SemaphoreType.DMA((len(sources) + 2,)),
        ],
        compiler_params=pltpu.CompilerParams(collective_id=0, has_side_effects=True),
    )(*sources, *pairs)
    weights = [g.reshape(2048, g.shape[-1]) for g in gathered[: len(sources)]]
    return weights, gathered[len(sources) :]


def key_gather_kernel(source, out, send, recv, local):
    spot, wires = Spot(), Wires(send, recv, local)
    spot.greet((("x", (1, 3)), ("y", (1, 3)), ("p", (1,))))
    own = tuple(spot.at[dim] for dim in KEY_DIMS)
    copies = start([wires.copy(source.at[s], out.at[(s,) + own]) for s in range(2)])
    for copy in copies:
        copy.wait()
    whole = pl.ds(0, source.shape[-1])
    run(
        gather_lane(spot, wires, KEY_DIMS, order, [(out.at[s], whole)], source.shape[1])
        for s, order in enumerate(KEY_GATHER_ORDERS)
    )


def gather_keys(packed):
    _, rows, width = packed.shape
    out = pl.pallas_call(
        key_gather_kernel,
        out_shape=jax.ShapeDtypeStruct((2, 2, 4, 4, rows, width), BF16),
        in_specs=[ANY],
        out_specs=ANY,
        scratch_shapes=[
            pltpu.SemaphoreType.DMA((18,)),
            pltpu.SemaphoreType.DMA((18,)),
            pltpu.SemaphoreType.DMA((2,)),
        ],
        compiler_params=pltpu.CompilerParams(collective_id=1, has_side_effects=True),
    )(packed)
    return out.reshape(2, 32 * rows, width)


def key_scatter_kernel(source, out, *refs):
    send, recv, local = refs[:3]
    buffers = list(refs[3:])
    spot, wires = Spot(), Wires(send, recv, local)
    spot.greet((("x", (1, 3)), ("y", (1, 3)), ("p", (1,))))
    rows, width = source.shape[-2:]
    lanes = []
    for s, order in enumerate(KEY_SCATTER_ORDERS):
        count = len(landing_shapes(KEY_DIMS, order, rows, width))
        held, landing = buffers[0], buffers[1 : 1 + count]
        del buffers[: 1 + count]
        lanes.append(
            scatter_lane(
                spot, wires, KEY_DIMS, order, source.at[s], held, landing, out.at[s], rows
            )
        )
    run(lanes)


def scatter_keys(grads):
    rows, width = grads.shape[-2:]
    scratch = [
        pltpu.SemaphoreType.DMA((18,)),
        pltpu.SemaphoreType.DMA((18,)),
        pltpu.SemaphoreType.DMA((6,)),
    ]
    for order in KEY_SCATTER_ORDERS:
        shapes = [(2, 4, 4, rows, width)] + landing_shapes(KEY_DIMS, order, rows, width)
        scratch += [pltpu.VMEM(shape, BF16) for shape in shapes]
    return pl.pallas_call(
        key_scatter_kernel,
        out_shape=jax.ShapeDtypeStruct((2, rows, width), F32),
        in_specs=[ANY],
        out_specs=pl.BlockSpec(memory_space=pltpu.VMEM),
        scratch_shapes=scratch,
        compiler_params=pltpu.CompilerParams(
            collective_id=2, has_side_effects=True, vmem_limit_bytes=48 << 20
        ),
    )(grads)


def total_lane(spot, wires, vector, slots, out):
    value = vector[...]
    sent = []
    for phase, axis in enumerate(("k", "x", "y", "z")):
        me = spot.at[axis]
        slots[phase, me] = value
        copies = start(
            [
                wires.remote(
                    slots.at[phase, me],
                    slots.at[phase, me],
                    spot.device(axis, spot.turn(axis, by)),
                )
                for by in range(1, SPAN[axis])
            ]
        )
        sent += copies
        yield
        for copy in copies:
            copy.wait_recv()
        value = slots[phase, 0]
        for place in range(1, SPAN[axis]):
            value = value + slots[phase, place]
    out[...] = value
    for copy in sent:
        copy.wait_send()


def weight_scatter_kernel(widths, chunks, *refs):
    refs = list(refs)

    def take(count):
        taken = refs[:count]
        del refs[:count]
        return taken

    count = len(widths)
    sources, (vector,) = take(count), take(1)
    outs, (vector_out,) = take(count), take(1)
    send, recv, local, slots = take(4)
    held = [take(3), take(3)]
    spot, wires = Spot(), Wires(send, recv, local)
    spot.greet((("x", RING), ("y", RING), ("z", RING), ("k", (1,))))
    core = spot.at["k"]
    sibling = spot.device("k", 1 - core)
    mine = pl.ds(pl.multiple_of(core * 16, 16), 16)
    theirs = pl.ds(pl.multiple_of((1 - core) * 16, 16), 16)

    def finish(at, first, wide, final):
        columns = pl.ds(pl.multiple_of(core * widths[at] + first, 128), wide)
        copies = [
            wires.copy(final.at[mine], outs[at].at[:, columns]),
            wires.remote(final.at[theirs], outs[at].at[:, columns], sibling),
        ]
        start(copies)
        yield
        for copy in copies:
            copy.wait()

    def chunk(lane, part, buffer):
        order = SCATTER_ORDERS[lane]
        at, first, wide = part
        landing = take(len(landing_shapes(WEIGHT_DIMS, order, 32, wide)))
        (final,) = take(1)
        lead = (slice(None),) * 5
        yield from scatter_lane(
            spot,
            wires,
            WEIGHT_DIMS,
            order,
            sources[at].at[lead + (pl.ds(first, wide),)],
            buffer.at[lead + (pl.ds(0, wide),)],
            landing,
            final,
            32,
        )
        yield from finish(at, first, wide, final)

    def series(parity):
        for number in range(parity, len(chunks), 2):
            threads = [
                chunk(lane, part, held[parity][lane]) for lane, part in enumerate(chunks[number])
            ]
            while threads:
                for thread in list(threads):
                    if next(thread, "end") == "end":
                        threads.remove(thread)
                yield

    run([series(0), series(1), total_lane(spot, wires, vector, slots, vector_out)])


def scatter_weights(sources, vector, chunks):
    widths = [source.shape[1] for source in sources]
    sources = [source.reshape(2, 4, 4, 2, 32, source.shape[1]) for source in sources]
    remotes = 10 + sum(13 * len(parts) for parts in chunks)
    locals_ = sum(4 * len(parts) for parts in chunks)
    scratch = [
        pltpu.SemaphoreType.DMA((remotes,)),
        pltpu.SemaphoreType.DMA((remotes,)),
        pltpu.SemaphoreType.DMA((locals_,)),
        pltpu.VMEM((4, 4) + vector.shape, F32),
    ]
    for parity in range(2):
        for lane in range(3):
            wide = max(parts[lane][2] for parts in chunks[parity::2])
            scratch.append(pltpu.VMEM((2, 4, 4, 2, 32, wide), BF16))
    order = []
    waves = [list(range(0, len(chunks), 2)), list(range(1, len(chunks), 2))]
    order = [n for pair in zip(*waves) for n in pair]
    order += waves[0][len(waves[1]) :]
    for number in order:
        for lane, (_, _, wide) in enumerate(chunks[number]):
            shapes = landing_shapes(WEIGHT_DIMS, SCATTER_ORDERS[lane], 32, wide)
            scratch += [pltpu.VMEM(shape, BF16) for shape in shapes]
            scratch.append(pltpu.VMEM((32, wide), F32))
    in_vmem = pl.BlockSpec(memory_space=pltpu.VMEM)
    return pl.pallas_call(
        functools.partial(weight_scatter_kernel, widths, chunks),
        out_shape=[jax.ShapeDtypeStruct((16, 2 * width), F32) for width in widths]
        + [jax.ShapeDtypeStruct(vector.shape, F32)],
        in_specs=[ANY] * len(sources) + [in_vmem],
        out_specs=[ANY] * len(sources) + [in_vmem],
        scratch_shapes=scratch,
        compiler_params=pltpu.CompilerParams(
            collective_id=3, has_side_effects=True, vmem_limit_bytes=62 << 20
        ),
    )(*sources, vector)


def contract(left, right, dims):
    return lax.dot_general(left, right, (dims, ((), ())), preferred_element_type=F32)


def key_chunk(slot_ref, kv_ref, chunk):
    return jnp.concatenate(
        [
            kv_ref[pl.ds(pl.multiple_of(slot_ref[chunk * 4 + n] * 64, 64), 64), :]
            for n in range(4)
        ],
        axis=0,
    )


def allowed_in(chunk, anchor, first):
    key = chunk * 256 + lax.broadcasted_iota(jnp.int32, (256, 256), 0)
    return (key <= anchor) & (key >= first)


def attention_kernel(slot_ref, low_ref, kv_ref, q_ref, anchor_ref, first_ref, o_ref, lse_ref, acc, norm):
    acc[...] = jnp.zeros_like(acc)
    norm[...] = jnp.zeros_like(norm)
    low_chunks = lax.div(low_ref[0], 4) + 1

    def step(item, _):
        is_low = item < low_chunks
        block = jnp.where(is_low, 0, 1)
        chunk = jnp.where(is_low, item, item - low_chunks)
        kv = key_chunk(slot_ref, kv_ref, chunk)
        scores = contract(kv, q_ref[block], ((1,), (1,)))
        weights = jnp.where(
            allowed_in(chunk, anchor_ref[block], first_ref[block]), jnp.exp(scores), 0.0
        )
        norm[block] += jnp.sum(weights, axis=0, keepdims=True)
        acc[block] += contract(kv, weights.astype(BF16), ((0,), (0,)))
        return 0

    lax.fori_loop(0, 17, step, 0)
    for block in range(2):
        total = norm[block]
        o_ref[block] = acc[block, 64:, :] / total
        lse_ref[block] = jnp.log(total)


def attention_specs():
    per_head = pl.BlockSpec((None, None, 2, 256, 128), lambda s, h, *_: (s, h, 0, 0, 0))
    row = pl.BlockSpec((None, None, 2, 1, 256), lambda s, h, *_: (s, h, 0, 0, 0))
    tall = pl.BlockSpec((None, None, 2, 64, 256), lambda s, h, *_: (s, h, 0, 0, 0))
    keys = pl.BlockSpec((None, 4096, 128), lambda s, h, *_: (s, 0, h))
    places = pl.BlockSpec((None, 2, 1, 256), lambda s, h, *_: (s, 0, 0, 0))
    return per_head, row, tall, keys, places


def attention(slots, low, kv, q, anchor, first):
    per_head, row, tall, keys, places = attention_specs()
    return pl.pallas_call(
        attention_kernel,
        grid_spec=pltpu.PrefetchScalarGridSpec(
            num_scalar_prefetch=2,
            grid=(2, 3),
            in_specs=[keys, per_head, places, places],
            out_specs=[tall, row],
            scratch_shapes=[pltpu.VMEM((2, 128, 256), F32), pltpu.VMEM((2, 1, 256), F32)],
        ),
        out_shape=[
            jax.ShapeDtypeStruct((2, 3, 2, 64, 256), F32),
            jax.ShapeDtypeStruct((2, 3, 2, 1, 256), F32),
        ],
        compiler_params=pltpu.CompilerParams(vmem_limit_bytes=32 << 20),
    )(slots, low, kv, q, anchor, first)


def attention_back_kernel(
    slot_ref, low_ref, map_ref, kv_ref, q_ref, d_ref, anchor_ref, first_ref, lse_ref, delta_ref, dq_ref, dkv_ref, acc, sums
):
    acc[...] = jnp.zeros_like(acc)
    sums[...] = jnp.zeros_like(sums)
    low_chunks = lax.div(low_ref[0], 4) + 1

    def step(item, _):
        is_low = item < low_chunks
        block = jnp.where(is_low, 0, 1)
        chunk = jnp.where(is_low, item, item - low_chunks)
        kv = key_chunk(slot_ref, kv_ref, chunk)
        q, d = q_ref[block], d_ref[block]
        scores = contract(kv, q, ((1,), (1,)))
        toward = contract(kv, d, ((1,), (1,)))
        weights = jnp.where(
            allowed_in(chunk, anchor_ref[block], first_ref[block]),
            jnp.exp(scores - lse_ref[block]),
            0.0,
        )
        grads = (weights * (toward - delta_ref[block])).astype(BF16)
        acc[block] += contract(kv, grads, ((0,), (0,)))
        sums[chunk] += contract(grads, q, ((1,), (0,))) + contract(
            weights.astype(BF16), d, ((1,), (0,))
        )
        return 0

    lax.fori_loop(0, 17, step, 0)
    for block in range(2):
        dq_ref[block] = acc[block, :64, :]

    def place(slot, _):
        block = map_ref[slot]
        rows = pl.ds(pl.multiple_of(lax.rem(block, 4) * 64, 64), 64)
        dkv_ref[pl.ds(pl.multiple_of(slot * 64, 64), 64), :] = sums[
            lax.div(block, 4), rows, :
        ].astype(BF16)
        return 0

    lax.fori_loop(0, 64, place, 0)


def attention_back(slots, low, block_map, kv, q, d, anchor, first, lse, delta):
    per_head, row, tall, keys, places = attention_specs()
    return pl.pallas_call(
        attention_back_kernel,
        grid_spec=pltpu.PrefetchScalarGridSpec(
            num_scalar_prefetch=3,
            grid=(2, 3),
            in_specs=[keys, per_head, per_head, places, places, row, row],
            out_specs=[tall, keys],
            scratch_shapes=[pltpu.VMEM((2, 128, 256), F32), pltpu.VMEM((16, 256, 128), F32)],
        ),
        out_shape=[
            jax.ShapeDtypeStruct((2, 3, 2, 64, 256), F32),
            jax.ShapeDtypeStruct(kv.shape, BF16),
        ],
        compiler_params=pltpu.CompilerParams(vmem_limit_bytes=32 << 20),
    )(slots, low, block_map, kv, q, d, anchor, first, lse, delta)


def swap(array):
    return lax.ppermute(array, "wt", [(0, 1), (1, 0), (2, 3), (3, 2)])


def share(array, core):
    other = swap(array)
    first = core == 0
    return jnp.concatenate(
        [jnp.where(first, array, other), jnp.where(first, other, array)], axis=0
    )


def total_rows(partial, core):
    half = partial.shape[0] // 2
    mine = lax.dynamic_slice_in_dim(partial, core * half, half)
    theirs = lax.dynamic_slice_in_dim(partial, (1 - core) * half, half)
    return mine + swap(theirs)


def norm_forward(values, gain):
    inverse = lax.rsqrt(jnp.mean(values * values, axis=-1, keepdims=True) + EPSILON)
    normed = values * inverse
    return (normed * gain, normed, inverse)


def norm_backward(grads, gain, normed, inverse):
    scaled = grads * gain
    back = inverse * (scaled - normed * jnp.mean(scaled * normed, axis=-1, keepdims=True))
    return (back, grads * normed)


def rotate(values, cosine, sine):
    halfway = values.shape[-1] // 2
    first = values[..., :halfway]
    second = values[..., halfway:]
    return jnp.concatenate(
        [first * cosine - second * sine, second * cosine + first * sine], axis=-1
    )


def unrotate(grads, cosine, sine):
    return rotate(grads, cosine, -sine)


def halves(array):
    return array.reshape(array.shape[0], 2, array.shape[1] // 2)


def to_blocks(heads):
    depth = heads.shape[-1]
    split = heads.reshape(2, 2, 64, 3, 4, depth)
    return split.transpose(0, 3, 1, 4, 2, 5).reshape(2, 3, 2, 256, depth)


def from_blocks(tall):
    depth = tall.shape[3]
    split = tall.reshape(2, 3, 2, depth, 4, 64)
    return split.transpose(0, 2, 5, 1, 4, 3).reshape(256, 12, depth)


def body(
    tokens,
    cotangent,
    block_map,
    document_ids,
    positions,
    first_gain,
    query_weight,
    key_weight,
    value_weight,
    out_weight,
    query_gain,
    key_gain,
    second_gain,
    gate_weight,
    up_weight,
    down_weight,
):
    core = lax.rem(lax.axis_index("wt"), 2)
    ctx = lax.axis_index("ctx")
    kv_halves = jnp.stack(
        [key_weight.reshape(16, 2, 3, 64), value_weight.reshape(16, 2, 3, 64)], axis=3
    ).reshape(16, 2, 384)
    qkv_pack = jnp.concatenate([halves(query_weight), kv_halves], axis=2).reshape(16, 2304)
    lanes = [
        [(0, lane * 384, 384), (1, lane * 256, 256), (2 + lane, 0, 2432)] for lane in range(3)
    ]
    (qkv_w, out_w, gate_w, up_w, down_w), (tokens_all, grad_out_all) = gather_weights(
        [qkv_pack, out_weight, gate_weight, up_weight, down_weight],
        [tokens[0], cotangent[0]],
        lanes,
    )
    grad_out_all = grad_out_all.reshape(256, 2048)
    rows = tokens[0].astype(F32)

    offsets = jnp.arange(64, dtype=jnp.int32)
    own_blocks = lax.dynamic_slice_in_dim(block_map, ctx * 2, 2)
    anchor = (own_blocks[:, None] * 64 + offsets[None, :]).reshape(128)
    doc_table = document_ids[0]
    places = jnp.arange(4096, dtype=jnp.int32)
    query_doc = jnp.sum(
        jnp.where(anchor[:, None] == places[None, :], doc_table[None, :], 0), axis=1
    )
    doc_start = jnp.sum((doc_table[None, :] < query_doc[:, None]).astype(jnp.int32), axis=1)
    layout = share(jnp.stack([positions[0], doc_start]).reshape(1, 2, 128), core)
    position_all, start_all = layout[:, 0], layout[:, 1]

    def over_heads(values):
        values = jnp.broadcast_to(values, (2, 128)).reshape(2, 2, 1, 1, 64)
        return jnp.broadcast_to(values, (2, 2, 1, 4, 64)).reshape(2, 2, 1, 256)

    anchor_rows, start_rows = over_heads(anchor), over_heads(start_all)
    blocks = jnp.arange(64, dtype=jnp.int32)
    slots = jnp.sum(jnp.where(block_map[None, :] == blocks[:, None], blocks[None, :], 0), axis=1)
    low_block = own_blocks[:1]

    inverse_freq = ROPE_BASE ** (-(jnp.arange(32, dtype=F32) * 2.0) / 64)
    angle = position_all.reshape(256).astype(F32)[:, None] * inverse_freq[None, :]
    cosine, sine = jnp.cos(angle)[:, None, :], jnp.sin(angle)[:, None, :]

    first_all, _, _ = norm_forward(tokens_all.reshape(256, 2048).astype(F32), first_gain)
    first_low = first_all.astype(BF16)
    _, first_hat, first_inv = norm_forward(rows, first_gain)
    qkv_pre = jnp.dot(first_low, qkv_w, preferred_element_type=F32)
    query_normed, query_hat, query_inv = norm_forward(
        qkv_pre[:, :768].reshape(256, 12, 64), query_gain
    )
    query_low = rotate(query_normed, cosine, sine).astype(BF16)
    kv_pre = qkv_pre[:, 768:].reshape(256, 3, 2, 64)
    key_normed, key_hat, key_inv = norm_forward(kv_pre[:, :, 0], key_gain)
    key_low = rotate(key_normed, cosine, sine).astype(BF16)
    kv_low = jnp.stack([key_low, kv_pre[:, :, 1].astype(BF16)], axis=2)
    kv_all = gather_keys(kv_low.reshape(2, 128, 384))
    query_blocks = jnp.pad(
        to_blocks(query_low * jnp.asarray(0.125, BF16)), ((0, 0),) * 4 + ((0, 64),)
    )
    attended, lse = attention(slots, low_block, kv_all, query_blocks, anchor_rows, start_rows)
    attended = from_blocks(attended)
    merged = attended.reshape(256, 768).astype(BF16)
    mixed = rows + total_rows(contract(merged, out_w, ((1,), (1,))), core)

    second_out, second_hat, second_inv = norm_forward(mixed, second_gain)
    second_low = share(second_out.astype(BF16), core)
    gate = jnp.dot(second_low, gate_w, preferred_element_type=F32)
    upward = jnp.dot(second_low, up_w, preferred_element_type=F32)
    sigmoid_gate = jax.nn.sigmoid(gate)
    product = (gate * sigmoid_gate * upward).astype(BF16)
    activations = (
        mixed + total_rows(contract(product, down_w, ((1,), (1,))), core)
    ).astype(BF16)[None]

    grad_product = jnp.dot(grad_out_all, down_w, preferred_element_type=F32)
    grad_gate = (grad_product * upward * sigmoid_gate * (1.0 + gate * (1.0 - sigmoid_gate))).astype(
        BF16
    )
    grad_upward = (grad_product * gate * sigmoid_gate).astype(BF16)
    grad_second = total_rows(
        contract(grad_gate, gate_w, ((1,), (1,))) + contract(grad_upward, up_w, ((1,), (1,))), core
    )
    second_back, second_terms = norm_backward(grad_second, second_gain, second_hat, second_inv)
    grad_mixed = cotangent[0].astype(F32) + second_back
    grad_branch = share(grad_mixed.astype(BF16), core)
    grad_merged = jnp.dot(grad_branch, out_w, preferred_element_type=F32).astype(BF16)
    grad_heads = grad_merged.reshape(256, 12, 64)
    delta = jnp.sum(grad_heads.astype(F32) * attended, axis=-1, keepdims=True)
    delta_rows = to_blocks(delta).reshape(2, 3, 2, 1, 256)
    grad_blocks = jnp.pad(to_blocks(grad_heads), ((0, 0),) * 4 + ((64, 0),))
    grad_query_tall, grad_kv = attention_back(
        slots,
        low_block,
        block_map,
        kv_all,
        query_blocks,
        grad_blocks,
        anchor_rows,
        start_rows,
        lse,
        delta_rows,
    )
    own_kv = scatter_keys(grad_kv.reshape(2, 2, 4, 4, 128, 384)).reshape(256, 3, 2, 64)
    query_unrot = unrotate(from_blocks(grad_query_tall) * 0.125, cosine, sine)
    query_back, query_terms = norm_backward(query_unrot, query_gain, query_hat, query_inv)
    key_unrot = unrotate(own_kv[:, :, 0], cosine, sine)
    key_back, key_terms = norm_backward(key_unrot, key_gain, key_hat, key_inv)
    grad_kv_low = jnp.stack([key_back, own_kv[:, :, 1]], axis=2).reshape(256, 384)
    grad_qkv = jnp.concatenate([query_back.reshape(256, 768), grad_kv_low], axis=1).astype(BF16)
    grad_first = total_rows(contract(grad_qkv, qkv_w, ((1,), (1,))), core)
    first_back, first_terms = norm_backward(grad_first, first_gain, first_hat, first_inv)
    token_grad = (grad_mixed + first_back).astype(BF16)[None]

    def outer(left, right):
        return contract(left, right, ((0,), (0,))).astype(BF16)

    gains = jnp.concatenate(
        [
            jnp.sum(first_terms, axis=0),
            jnp.sum(second_terms, axis=0),
            jnp.sum(query_terms, axis=(0, 1)),
            jnp.sum(key_terms, axis=(0, 1)),
            jnp.zeros((896,), F32),
        ]
    ).reshape(8, 640)
    ffn = [[(2 + lane, first, wide) for lane in range(3)] for first, wide in
           ((0, 640), (640, 640), (1280, 640), (1920, 512))]
    chunks = ffn + [[(at, lane * wide, wide) for lane in range(3)] for at, wide in ((0, 384), (1, 256))]
    qkv_g, out_g, gate_g, up_g, down_g, gains = scatter_weights(
        [
            outer(first_low, grad_qkv),
            outer(grad_branch, merged),
            outer(second_low, grad_gate),
            outer(second_low, grad_upward),
            outer(grad_out_all, product),
        ],
        gains,
        chunks,
    )
    gains = gains.reshape(5120)
    qkv_g = qkv_g.reshape(16, 2, 1152)
    query_g = qkv_g[:, :, :768].reshape(16, 1536)
    kv_g = qkv_g[:, :, 768:].reshape(16, 2, 3, 2, 64)
    key_g, value_g = kv_g[:, :, :, 0].reshape(16, 384), kv_g[:, :, :, 1].reshape(16, 384)
    return (
        activations,
        token_grad,
        gains[:2048],
        query_g,
        key_g,
        value_g,
        out_g,
        gains[4096:4160],
        gains[4160:4224],
        gains[2048:4096],
        gate_g,
        up_g,
        down_g,
    )


def solution(mesh):
    rows = P("wt", "ctx", None)
    weight = P(("ctx", "wt"), None)
    whole = P()
    in_specs = (
        rows,
        rows,
        whole,
        P("wt", None),
        P("wt", "ctx"),
        whole,
        weight,
        weight,
        weight,
        weight,
        whole,
        whole,
        whole,
        weight,
        weight,
        weight,
    )
    out_specs = (
        rows,
        rows,
        whole,
        weight,
        weight,
        weight,
        weight,
        whole,
        whole,
        whole,
        weight,
        weight,
        weight,
    )
    return jax.shard_map(body, mesh=mesh, in_specs=in_specs, out_specs=out_specs, check_vma=False)
```

time: 4290 us -> 742 us (0.17)
  waiting for transfers between devices: 1860 us -> 0.11 us
  blocking collectives: 1670 us -> 0 us
  Pallas kernels: 0 us -> 551 us
  local copies, waits for them, and re-layouts: 342 us -> 59.9 us
  matrix products: 322 us -> 73.7 us
    psum x1 -> x0, blocking collectives: 1670 us -> none  [body(): lax.psum((jnp.sum(first_terms, axis=0), jnp.sum(second_terms, axis=0), jn...]
    all_gather x9 -> x0, waiting for transfers between devices: 1560 us -> none  [the longest x1 215 us: body(): lax.all_gather(up_weight, ('ctx', 'wt'), axis=0, tiled=True)]
    pallas_call x0 -> x6, Pallas kernels: none -> 551 us  [the longest x1 189 us: gather_weights(): pl.pallas_call(functools.partial(weight_gather_kernel, widths, lanes), ou...]
    reduce_scatter x3 -> x0, waiting for transfers between devices: 301 us -> none  [the longest x1 170 us: body(): lax.psum_scatter(values_grads.reshape(length, kv_width), 'ctx', scatter_d...]
    dynamic_update_slice x32 -> x0, local copies, waits for them, and re-layouts: 279 us -> none  [body(): lax.scan(backward_step, zero_heads, (keys_split, values_split, anchor_spl...]
    dot_general x93 -> x15, matrix products: 322 us -> 73.7 us  [the longest x10 48.1 us: contract(): lax.dot_general(left, right, (dims, ((), ())), preferred_element_type=F32)]
  transfers between devices with their start and end apart: 12 -> 7, of which waited for: 11 -> 1; matrix products, arithmetic and copies ran while one was open for 5% -> 13% of each run, Pallas kernels for 0% -> 63%
where the time goes in v1:
time: 742 us; the launch traced here: 732 us
  Pallas kernels  551 us (74%)
  matrix products  73.7 us (10%)
  local copies, waits for them, and re-layouts  59.9 us (8%)
  other arithmetic  28.6 us (4%)
  starting transfers between devices  16.5 us (2%)
    pallas_call x1, Pallas kernels, gather_weights(): pl.pallas_call(functools.partial(weight_gather_kernel, widths, lanes), ou...  189 us
    pallas_call x1, Pallas kernels, scatter_weights(): pl.pallas_call(functools.partial(weight_scatter_kernel, widths, chunks),...  175 us
    pallas_call x1, Pallas kernels, attention_back(): pl.pallas_call(attention_back_kernel, grid_spec=pltpu.PrefetchScalarGridS...  56.3 us
    dot_general x10, matrix products, contract(): lax.dot_general(left, right, (dims, ((), ())), preferred_element_type=F32)  48.1 us
    pallas_call x1, Pallas kernels, gather_keys(): pl.pallas_call(key_gather_kernel, out_shape=jax.ShapeDtypeStruct((2, 2, 4...  47.1 us
    pallas_call x1, Pallas kernels, scatter_keys(): pl.pallas_call(key_scatter_kernel, out_shape=jax.ShapeDtypeStruct((2, row...  42.7 us
    pallas_call x1, Pallas kernels, attention(): pl.pallas_call(attention_kernel, grid_spec=pltpu.PrefetchScalarGridSpec(n...  40.4 us
    unnamed x123, local copies, waits for them, and re-layouts  18.8 us
  transfers between devices with their start and end apart: 7, of which 1 were waited for; matrix products, arithmetic and copies ran while one was open for 13% of the time, Pallas kernels for 63%

profile of v1, /device:TPU:1, one launch (start us, length us, event | category | flops | bytes accessed | tf_op | source)
XLA Modules:
  0.0 731.9 jit_solution(3450869210381898419)
XLA Ops:
  4.4 1.4 collective-permute-start
  10.0 189.2 %shard_map.255 = (bf16[2,4,4,2,32,1152]{5,4,3,2,1,0:T(8,128)(2,1)}, bf16[2,4,4,2,32,768]{5,4,3,2,1,0:T(8,128)(2,1)}, bf16[2,4,4,2,32,2432]{5,4,3,2,1,0:T(8,128)(...) custom-call(bf16[16,2304]{1,0:T(8,128)(2,1)} %bitcast.184, ...), custom_call_target="tpu_custom_call" | custom-call | tf_op jit(solution)/shard_map/pallas_call | solution.py:341
  199.2 1.5 multiply_reduce_fusion
  200.8 1.5 multiply_convert_fusion.3
  202.3 3.9 fusion.40
  208.9 47.1 %shard_map.256 = bf16[2,2,4,4,128,384]{5,4,3,2,1,0:T(8,128)(2,1)} custom-call(bf16[2,128,384]{2,1,0:T(8,128)(2,1)} %copy.111.source), custom_call_target="tpu_custom_call" | custom-call | tf_op jit(solution)/shard_map/pallas_call | solution.py:373
  256.5 1.3 fusion.13
  259.0 2.8 copy-done
  261.8 40.4 %shard_map.257 = (f32[2,3,2,64,256]{4,3,2,1,0:T(8,128)S(1)}, f32[2,3,2,1,256]{4,3,2,1,0:T(1,128)S(1)}) custom-call(s32[64]{0:T(128)S(1)} %select_reduce_fusion.1.slot_ref, s32[1]{0:T(128)S(1)} %bitcast.149, bf16[2,4096,384]{2,1,0:T(8,128)(2,1)S(1)} %bitcast.146, bf16[2,3,2,256,128]{4,3,2,1,0:T(8,128)(2,1)S(1)} %pad.8.q_ref, ...), custom_call_target="tpu_custom_call" | custom-call | tf_op jit(solution)/shard_map/pallas_call | solution.py:614
  302.2 1.8 reshape.420
  304.0 1.8 copy.114
  306.1 1.2 convert_element_type.112
  307.3 3.0 fusion.41
  310.3 1.3 copy-done.9
  312.7 8.5 %collective-permute-start.1 = (f32[128,2048]{1,0:T(8,128)}, f32[128,2048]{1,0:T(8,128)}, u32[]{:S(2)}, u32[]{:S(2)}) collective-permute-start(f32[128,2048]{1,0:T(8,128)} %constant_dynamic-slice_fusion.3), channel_id=1, source_target_pairs={{0,1},{1,0},{2,3},{3,2},{4,5},{5,4},{6,7},{7,6},{8,9},{9,8},{10,11... | collective-permute-start | bytes 3145736 | tf_op jit(solution)/shard_map/ppermute | solution.py:693
  323.1 6.1 fusion.43
  329.3 1.6 multiply_reduce_fusion.3
  331.2 1.3 fusion.1
  333.5 6.1 fusion.34
  339.6 7.6 %multiply_convert_fusion = (bf16[256,2432]{1,0:T(8,128)(2,1)S(1)}, bf16[256,2432]{1,0:T(8,128)(2,1)S(1)}, bf16[256,2432]{1,0:T(8,128)(2,1)S(1)}) fusion(f32[256,2432]{1,0:T(8,128)S(1)} %fusion.43, f32[256,2432]{1,0:T(8,128)S(1)} %fusion.34, bf16[2048,2432]{1,0:T(8,128)(2,1)} %bitcast.196, bf16[128,2048]{1,0:T(8,128)(2,1)S(1)} %get-tuple-element.69, ...), kind=kOutput, calls=%fused_computation.6 | convolution fusion | flops 2562195456 | bytes 19726336 | tf_op jit(solution)/shard_map/dot_general | solution.py:835
  347.3 6.0 fusion.44
  353.3 5.6 convolution_add_fusion
  359.4 5.5 fusion.42
  366.3 5.4 convolution_convert_fusion.2
  374.6 5.3 convolution_convert_fusion
  381.0 1.7 convolution_convert_fusion.5
  382.8 2.6 reshape_reshape.7
  385.3 3.0 fusion.2
  388.9 1.2 copy.116
  390.2 2.8 copy-done.1
  393.0 56.3 %shard_map.258 = (f32[2,3,2,64,256]{4,3,2,1,0:T(8,128)S(1)}, bf16[2,4096,384]{2,1,0:T(8,128)(2,1)S(1)}) custom-call(s32[64]{0:T(128)S(1)} %select_reduce_fusion.1.slot_ref, s32[1]{0:T(128)S(1)} %bitcast.150, s32[64]{0:T(128)S(1)} %copy-done.3, bf16[2,4096,384]{2,1,0:T(8,128)(2,1)S(1)} %bitcast.147, bf16[2,3,2,256,128]{4,3,2,1,0:T(8,128)(2,1)S(1)} %pad.8.q_ref, ...), custom_call_target="tpu_custom_call" | custom-call | tf_op jit(solution)/shard_map/pallas_call | solution.py:675
  449.3 2.6 copy-done.2
  452.0 42.7 %shard_map.259 = f32[2,128,384]{2,1,0:T(8,128)S(1)} custom-call(bf16[2,2,4,4,128,384]{5,4,3,2,1,0:T(8,128)(2,1)} %bitcast.148), custom_call_target="tpu_custom_call" | custom-call | tf_op jit(solution)/shard_map/pallas_call | solution.py:417
  500.3 1.9 mul.514
  502.2 2.4 copy.142
  504.5 2.9 mul.516
  508.6 2.4 copy.118
  512.0 2.3 copy.120
  514.3 1.6 multiply_reduce_fusion.4
  516.0 4.0 fusion.16
  520.0 1.3 copy-done.26
  522.4 5.2 collective-permute-start.6
  527.7 5.5 convolution_convert_fusion.1
  533.3 4.0 convolution_convert_fusion.4
  537.4 3.7 convolution_convert_fusion.3
  541.1 2.6 fusion.11
  544.3 175.3 %shard_map.260 = (f32[16,2304]{1,0:T(8,128)}, f32[16,1536]{1,0:T(8,128)}, f32[16,4864]{1,0:T(8,128)}, f32[16,4864]{1,0:T(8,128)}, f32[16,4864]{1,0:T(8,128)}, /*index=5*/f32[8,640]{1,0:T(8,128)}) custom-call(bf16[2,4,4,2,32,1152]{5,4,3,2,1,0:T(8,128)(2,1)} %bitcast.154, bf16[2,4,4,2,32,768]{5,4,3,2,1,0:T(8,128)(2,1)} %bitcast.167, ...), custom_call_target="tpu_custom_call" | custom-call | tf_op jit(solution)/shard_map/pallas_call | solution.py:546
  725.0 3.7 fusion.15
  (227 shorter events, 40.6 us)
Async XLA Ops:
  0.6 200.1 %copy-start.43 = (f32[2048]{0:T(1024)S(1)}, f32[2048]{0:T(1024)}, u32[]{:S(2)}) copy-start(f32[2048]{0:T(1024)} %param.21) | copy-start | bytes 24580
  4.4 203.2 %collective-permute-start = (s32[1,2,128]{2,1,0:T(2,128)S(1)}, s32[1,2,128]{2,1,0:T(2,128)S(1)}, u32[]{:S(2)}, u32[]{:S(2)}) collective-permute-start(s32[1,2,128]{2,1,0:T(2,128)S(1)} %add_bitcast_fusion), channel_id=1, source_target_pairs={{0,1},{1,0},{2,3},{3,2},{4,5},{5,4},{6,7},{7,6},{8,9},{9,8},{10,11... | collective-permute-start | bytes 3080 | tf_op jit(solution)/shard_map/ppermute | solution.py:693
  259.0 2.8 copy-start
  312.7 16.6 %collective-permute-start.1 = (f32[128,2048]{1,0:T(8,128)}, f32[128,2048]{1,0:T(8,128)}, u32[]{:S(2)}, u32[]{:S(2)}) collective-permute-start(f32[128,2048]{1,0:T(8,128)} %constant_dynamic-slice_fusion.3), channel_id=1, source_target_pairs={{0,1},{1,0},{2,3},{3,2},{4,5},{5,4},{6,7},{7,6},{8,9},{9,8},{10,11... | collective-permute-start | bytes 3145736 | tf_op jit(solution)/shard_map/ppermute | solution.py:693
  323.1 6.2 copy-start.10
  323.1 6.2 copy-start.11
  329.2 2.0 copy-start.8
  330.9 41.8 %copy-start.47 = (f32[128]{0:T(128)}, f32[128]{0:T(128)S(1)}, u32[]{:S(2)}) copy-start(f32[128]{0:T(128)S(1)} %add_rsqrt_fusion.4) | copy-start | bytes 1540
  331.1 2.0 collective-permute-start.2
  333.4 32.8 %copy-start.15 = (bf16[128,2048]{1,0:T(8,128)(2,1)}, bf16[128,2048]{1,0:T(8,128)(2,1)S(1)}, u32[]{:S(2)}) copy-start(bf16[128,2048]{1,0:T(8,128)(2,1)S(1)} %get-tuple-element.68) | copy-start | bytes 1572868
  333.5 32.8 %copy-start.17 = (bf16[128,2048]{1,0:T(8,128)(2,1)}, bf16[128,2048]{1,0:T(8,128)(2,1)S(1)}, u32[]{:S(2)}) copy-start(bf16[128,2048]{1,0:T(8,128)(2,1)S(1)} %get-tuple-element.69) | copy-start | bytes 1572868
  347.2 6.0 copy-start.33
  359.0 12.7 %collective-permute-start.4 = (f32[128,2048]{1,0:T(8,128)S(1)}, f32[128,2048]{1,0:T(8,128)S(1)}, u32[]{:S(2)}, u32[]{:S(2)}) collective-permute-start(f32[128,2048]{1,0:T(8,128)S(1)} %constant_dynamic-slice_fusion.1), channel_id=1, source_target_pairs={{0,1},{1,0},{2,3},{3,2},{4,5},{5,4},{6,7},{7,6},{8,9},{9,8},{10,11... | collective-permute-start | bytes 3145736 | tf_op jit(solution)/shard_map/ppermute | solution.py:693
  365.0 6.7 copy-start.28
  366.2 358.8 %collective-permute-start.3 = (f32[128,2048]{1,0:T(8,128)}, f32[128,2048]{1,0:T(8,128)}, u32[]{:S(2)}, u32[]{:S(2)}) collective-permute-start(f32[128,2048]{1,0:T(8,128)} %constant_dynamic-slice_fusion.2), channel_id=1, source_target_pairs={{0,1},{1,0},{2,3},{3,2},{4,5},{5,4},{6,7},{7,6},{8,9},{9,8},{10,11... | collective-permute-start | bytes 3145736 | tf_op jit(solution)/shard_map/ppermute | solution.py:693
  372.7 7.3 copy-start.54
  374.0 6.0 collective-permute-start.5
  374.6 6.4 copy-start.25
  385.3 3.0 copy-start.13
  390.2 2.8 copy-start.1
  449.3 2.7 copy-start.2
  494.7 3.5 copy-start.21
  494.7 3.5 copy-start.50
  504.5 3.0 copy-start.5
  504.5 3.0 copy-start.52
  508.6 5.7 copy-start.23
  508.6 5.7 copy-start.24
  508.6 5.7 copy-start.46
  515.9 4.1 copy-start.30
  516.0 11.7 %copy-start.34 = (bf16[256,2432]{1,0:T(8,128)(2,1)S(1)}, bf16[256,2432]{1,0:T(8,128)(2,1)}, u32[]{:S(2)}) copy-start(bf16[256,2432]{1,0:T(8,128)(2,1)} %copy-done.33) | copy-start | bytes 3735556
  521.3 6.3 copy-start.16
  521.3 6.3 copy-start.18
  522.4 10.8 %copy-start.32 = (bf16[256,768]{1,0:T(8,128)(2,1)S(1)}, bf16[256,768]{1,0:T(8,128)(2,1)}, u32[]{:S(2)}) copy-start(bf16[256,768]{1,0:T(8,128)(2,1)} %convert_element_type.112) | copy-start | bytes 1179652
  522.4 18.6 %collective-permute-start.6 = (f32[128,2048]{1,0:T(8,128)}, f32[128,2048]{1,0:T(8,128)}, u32[]{:S(2)}, u32[]{:S(2)}) collective-permute-start(f32[128,2048]{1,0:T(8,128)} %constant_dynamic-slice_fusion), channel_id=1, source_target_pairs={{0,1},{1,0},{2,3},{3,2},{4,5},{5,4},{6,7},{7,6},{8,9},{9,8},{10,11... | collective-permute-start | bytes 3145736 | tf_op jit(solution)/shard_map/ppermute | solution.py:693
  533.3 4.1 copy-start.14
  533.3 4.1 copy-start.31
  533.3 4.1 copy-start.36
  537.3 3.7 copy-start.12
  537.3 3.7 copy-start.27
  537.4 3.7 copy-start.53
  541.0 2.6 copy-start.45
  544.3 180.6 %copy-start.48 = (f32[128]{0:T(128)S(1)}, f32[128]{0:T(128)}, u32[]{:S(2)}) copy-start(f32[128]{0:T(128)} %copy-done.47) | copy-start | bytes 1540
  544.3 180.6 %copy-start.55 = (f32[128]{0:T(128)S(1)}, f32[128]{0:T(128)}, u32[]{:S(2)}) copy-start(f32[128]{0:T(128)} %copy-done.54) | copy-start | bytes 1540
  719.6 5.4 copy-start.7
  725.0 3.7 copy-start.44
  725.0 4.4 copy-start.41
  725.0 5.1 copy-start.40
  725.0 5.8 copy-start.39
  (16 other events, 20.9 us)

commit v2 on v1

--- a/solution.py
+++ b/solution.py
@@ -20,8 +20,17 @@
 SPAN = {"x": 4, "y": 4, "z": 4, "p": 2, "k": 2}
 GATHER_ORDERS = (("x", "y", "z"), ("y", "z", "x"), ("z", "x", "y"))
 SCATTER_ORDERS = (("z", "y", "x"), ("x", "z", "y"), ("y", "x", "z"))
+PLANE_DIMS = ("x", "y", "zh")
+PLANE_GATHER_ORDERS = (("x", "y"), ("y", "x"))
+PLANE_SCATTER_ORDERS = (("y", "x"), ("x", "y"))
 KEY_GATHER_ORDERS = (("p", "x", "y"), ("p", "y", "x"))
 KEY_SCATTER_ORDERS = (("y", "x", "p"), ("x", "y", "p"))
+
+
+def axis_of(dim, dims):
+    if dim == "zh" or (dim == "zl" and "zh" in dims):
+        return "z"
+    return "p" if dim == "zl" else dim
 
 
 class Spot:
@@ -51,24 +60,18 @@
     def turn(self, axis, by):
         return lax.rem(self.at[axis] + by, SPAN[axis])
 
-    def greet(self, reach):
+    def greet(self, reach, devices=()):
         barrier = pltpu.get_barrier_semaphore()
-        count = 0
-        for axis, steps in reach:
-            for by in steps:
-                pl.semaphore_signal(
-                    barrier,
-                    inc=1,
-                    device_id=self.device(axis, self.turn(axis, by)),
-                    device_id_type=MESH,
-                )
-                count += 1
-        pl.semaphore_wait(barrier, count)
+        devices = list(devices)
+        devices += [self.device(axis, self.turn(axis, by)) for axis, steps in reach for by in steps]
+        for device in devices:
+            pl.semaphore_signal(barrier, inc=1, device_id=device, device_id_type=MESH)
+        pl.semaphore_wait(barrier, len(devices))
 
     def slab(self, dims, full, axis, value):
         index = []
         for dim in dims:
-            name = "z" if dim == "zh" or (dim == "zl" and "zh" in dims) else "p" if dim == "zl" else dim
+            name = axis_of(dim, dims)
             if name in full:
                 index.append(slice(None))
             elif name == axis:
@@ -109,18 +112,24 @@
     return copies
 
 
-def run(threads):
+def in_turn(threads):
     threads = list(threads)
     while threads:
         for thread in list(threads):
             if next(thread, "end") == "end":
                 threads.remove(thread)
-
-
-def gather_lane(spot, wires, dims, order, parts, rows):
+        yield
+
+
+def run(threads):
+    for _ in in_turn(threads):
+        pass
+
+
+def gather_lane(spot, wires, dims, order, parts, rows, always=()):
     sent = []
     for phase, axis in enumerate(order):
-        full = order[:phase]
+        full = always + order[:phase]
         me = spot.at[axis]
 
         def slab(part, value, first, count):
@@ -177,14 +186,13 @@
 
 
 def slab_shape(dims, full):
-    names = {"zl": "z" if "zh" in dims else "p", "zh": "z", "x": "x", "y": "y"}
-    return tuple(SIZES[dim] if names[dim] in full else 1 for dim in dims)
-
-
-def landing_shapes(dims, order, rows, width):
+    return tuple(SIZES[dim] if axis_of(dim, dims) in full else 1 for dim in dims)
+
+
+def landing_shapes(dims, order, rows, width, always=()):
     shapes = []
     for phase, axis in enumerate(order):
-        lead = slab_shape(dims, order[phase + 1 :])
+        lead = slab_shape(dims, always + order[phase + 1 :])
         if SPAN[axis] == 2:
             shapes.append(lead + (rows, width))
         else:
@@ -192,18 +200,18 @@
     return shapes
 
 
-def scatter_lane(spot, wires, dims, order, source, held, landing, final, rows):
+def scatter_lane(spot, wires, dims, order, source, held, landing, final, rows, always=()):
     landing = list(landing)
     sent = []
     half = rows // 2
-    first_axis, first_full = order[0], order[1:]
+    first_axis, first_full = order[0], always + order[1:]
     loads = []
     for by in [0, 1, 3] if SPAN[first_axis] == 4 else [0]:
         index = spot.slab(dims, first_full, first_axis, spot.turn(first_axis, by))
         loads.append(wires.copy(source.at[index], held.at[index]))
     start(loads)
     for phase, axis in enumerate(order):
-        full = order[phase + 1 :]
+        full = always + order[phase + 1 :]
         lead = slab_shape(dims, full)
         flat = tuple(slice(None) if size > 1 else 0 for size in lead)
         me = spot.at[axis]
@@ -281,7 +289,7 @@
             for piece in arrived:
                 value = value + piece[index].astype(F32)
             if last:
-                final[...] = value
+                final[index] = value
             else:
                 held[place] = value.astype(BF16)
 
@@ -293,65 +301,104 @@
 RING = (1, 2, 3)
 
 
+def line_columns(z, core):
+    return core * 2432 + 640 * z - 128 * lax.div(z, 3)
+
+
+def line_devices(spot):
+    found = []
+    for dz in range(4):
+        for dk in range(2):
+            if dz or dk:
+                z, core = spot.turn("z", dz), spot.turn("k", dk)
+                place = Spot.__new__(Spot)
+                place.at = dict(spot.at, k=core)
+                found.append((z, core, place.device("z", z)))
+    return found
+
+
+def ffn_gather_lanes(spot, wires, sources, outs):
+    rows = pl.ds(pl.multiple_of(spot.at["k"] * 16, 16), 16)
+    own = tuple(spot.at[dim] for dim in WEIGHT_DIMS) + (rows,)
+    remote, local = [], []
+    for source, out in zip(sources, outs):
+        for z, core, device in line_devices(spot):
+            columns = pl.ds(pl.multiple_of(line_columns(z, core), 128), 640)
+            remote.append(wires.remote(source.at[:, columns], out.at[own], device))
+        columns = pl.ds(pl.multiple_of(line_columns(spot.at["z"], spot.at["k"]), 128), 640)
+        local.append(wires.copy(source.at[:, columns], out.at[own]))
+    start(remote + local)
+    yield
+    for copy in remote + local:
+        copy.wait()
+    threads = [
+        gather_lane(spot, wires, PLANE_DIMS, order, [(out.at[low], pl.ds(0, 640))], 32, ("z",))
+        for out in outs
+        for low, order in enumerate(PLANE_GATHER_ORDERS)
+    ]
+    yield from in_turn(threads)
+
+
 def weight_gather_kernel(widths, lanes, *refs):
+    refs = list(refs)
+
+    def take(count):
+        taken = refs[:count]
+        del refs[:count]
+        return taken
+
     count = len(widths)
-    sources, pairs_in = refs[:count], refs[count : count + 2]
-    outs, pairs_out = refs[count + 2 : 2 * count + 2], refs[2 * count + 2 : 2 * count + 4]
-    spot, wires = Spot(), Wires(*refs[2 * count + 4 :])
-    spot.greet((("x", (1, 3)), ("y", (1, 3)), ("z", (1, 3)), ("k", (1,))))
+    sources, ffn_in, (tokens,) = take(count), take(3), take(1)
+    outs, ffn_out, (tokens_all,) = take(count), take(3), take(1)
+    spot, wires = Spot(), Wires(*refs)
+    spot.greet((("x", (1, 3)), ("y", (1, 3))), [device for _, _, device in line_devices(spot)])
     core = spot.at["k"]
     sibling = spot.device("k", 1 - core)
     rows = pl.ds(pl.multiple_of(core * 16, 16), 16)
     own = tuple(spot.at[dim] for dim in WEIGHT_DIMS)
-    local, remote, swaps = [], [], []
+    local, remote = [], []
     for source, out, width in zip(sources, outs, widths):
         target = out.at[own + (rows,)]
         mine = pl.ds(pl.multiple_of(core * width, 128), width)
         theirs = pl.ds(pl.multiple_of((1 - core) * width, 128), width)
         local.append(wires.copy(source.at[:, mine], target))
         remote.append(wires.remote(source.at[:, theirs], target, sibling))
-    for source, out in zip(pairs_in, pairs_out):
-        local.append(wires.copy(source, out.at[core]))
-        swaps.append(wires.remote(source, out.at[core], sibling))
-    start(local + remote + swaps)
-    for copy in local:
+    local.append(wires.copy(tokens, tokens_all.at[core]))
+    swap_tokens = wires.remote(tokens, tokens_all.at[core], sibling)
+    start(local + remote + [swap_tokens])
+    ffn = ffn_gather_lanes(spot, wires, ffn_in, ffn_out)
+    next(ffn)
+    for copy in local + remote:
         copy.wait()
-    for copy in remote:
-        copy.wait()
-    run(
-        gather_lane(
-            spot,
-            wires,
-            WEIGHT_DIMS,
-            order,
-            [(outs[at], pl.ds(first, wide)) for at, first, wide in parts],
-            32,
-        )
-        for order, parts in zip(GATHER_ORDERS, lanes)
-    )
-    for copy in swaps:
-        copy.wait()
-
-
-def gather_weights(sources, pairs, lanes):
+    threads = [
+        gather_lane(spot, wires, WEIGHT_DIMS, order, [(outs[at], pl.ds(first, wide))], 32)
+        for number in range(count)
+        for order, (at, first, wide) in zip(GATHER_ORDERS, [lane[number] for lane in lanes])
+    ]
+    run(threads + [ffn])
+    swap_tokens.wait()
+
+
+def gather_weights(sources, ffn, tokens, lanes):
     widths = [source.shape[1] // 2 for source in sources]
-    remotes = len(sources) + 2 + sum(len(parts) for parts in lanes) * 12
+    count = len(sources)
+    remotes = count + 1 + sum(len(parts) for parts in lanes) * 12 + 21 + 6 * 8
     out = [jax.ShapeDtypeStruct((2, 4, 4, 2, 32, width), BF16) for width in widths]
-    out += [jax.ShapeDtypeStruct((2,) + pair.shape, pair.dtype) for pair in pairs]
-    gathered = pl.pallas_call(
+    out += [jax.ShapeDtypeStruct((2, 4, 4, 2, 32, 640), BF16)] * 3
+    out += [jax.ShapeDtypeStruct((2,) + tokens.shape, tokens.dtype)]
+    *gathered, tokens_all = pl.pallas_call(
         functools.partial(weight_gather_kernel, widths, lanes),
         out_shape=out,
-        in_specs=[ANY] * (len(sources) + 2),
+        in_specs=[ANY] * (count + 4),
         out_specs=[ANY] * len(out),
         scratch_shapes=[
             pltpu.SemaphoreType.DMA((remotes,)),
             pltpu.SemaphoreType.DMA((remotes,)),
-            pltpu.SemaphoreType.DMA((len(sources) + 2,)),
+            pltpu.SemaphoreType.DMA((count + 4,)),
         ],
         compiler_params=pltpu.CompilerParams(collective_id=0, has_side_effects=True),
-    )(*sources, *pairs)
-    weights = [g.reshape(2048, g.shape[-1]) for g in gathered[: len(sources)]]
-    return weights, gathered[len(sources) :]
+    )(*sources, *ffn, tokens)
+    return [g.reshape(2048, g.shape[-1]) for g in gathered], tokens_all
 
 
 def key_gather_kernel(source, out, send, recv, local):
@@ -382,7 +429,7 @@
         ],
         compiler_params=pltpu.CompilerParams(collective_id=1, has_side_effects=True),
     )(packed)
-    return out.reshape(2, 32 * rows, width)
+    return out
 
 
 def key_scatter_kernel(source, out, *refs):
@@ -416,7 +463,7 @@
         scratch += [pltpu.VMEM(shape, BF16) for shape in shapes]
     return pl.pallas_call(
         key_scatter_kernel,
-        out_shape=jax.ShapeDtypeStruct((2, rows, width), F32),
+        out_shape=jax.ShapeDtypeStruct((2, 1, 1, 1, rows, width), F32),
         in_specs=[ANY],
         out_specs=pl.BlockSpec(memory_space=pltpu.VMEM),
         scratch_shapes=scratch,
@@ -454,7 +501,7 @@
         copy.wait_send()
 
 
-def weight_scatter_kernel(widths, chunks, *refs):
+def weight_scatter_kernel(widths, lanes, *refs):
     refs = list(refs)
 
     def take(count):
@@ -463,111 +510,139 @@
         return taken
 
     count = len(widths)
-    sources, (vector,) = take(count), take(1)
-    outs, (vector_out,) = take(count), take(1)
+    sources, ffn_in, (vector,) = take(count), take(3), take(1)
+    outs, ffn_out, (vector_out,) = take(count), take(3), take(1)
     send, recv, local, slots = take(4)
-    held = [take(3), take(3)]
     spot, wires = Spot(), Wires(send, recv, local)
-    spot.greet((("x", RING), ("y", RING), ("z", RING), ("k", (1,))))
+    line = line_devices(spot)
+    spot.greet((("x", RING), ("y", RING)), [device for _, _, device in line])
     core = spot.at["k"]
     sibling = spot.device("k", 1 - core)
-    mine = pl.ds(pl.multiple_of(core * 16, 16), 16)
-    theirs = pl.ds(pl.multiple_of((1 - core) * 16, 16), 16)
-
-    def finish(at, first, wide, final):
+
+    def half_rows(which):
+        return pl.ds(pl.multiple_of(which * 16, 16), 16)
+
+    def part(lane, at, first, wide):
+        order = SCATTER_ORDERS[lane]
+        (held,) = take(1)
+        landing = take(len(landing_shapes(WEIGHT_DIMS, order, 32, wide)))
+        (final,) = take(1)
+        source = sources[at].at[(slice(None),) * 5 + (pl.ds(first, wide),)]
+        yield from scatter_lane(
+            spot, wires, WEIGHT_DIMS, order, source, held, landing, final, 32
+        )
         columns = pl.ds(pl.multiple_of(core * widths[at] + first, 128), wide)
+        done = final.at[0, 0, 0, 0]
         copies = [
-            wires.copy(final.at[mine], outs[at].at[:, columns]),
-            wires.remote(final.at[theirs], outs[at].at[:, columns], sibling),
+            wires.copy(done.at[half_rows(core)], outs[at].at[:, columns]),
+            wires.remote(done.at[half_rows(1 - core)], outs[at].at[:, columns], sibling),
         ]
         start(copies)
         yield
         for copy in copies:
             copy.wait()
 
-    def chunk(lane, part, buffer):
-        order = SCATTER_ORDERS[lane]
-        at, first, wide = part
-        landing = take(len(landing_shapes(WEIGHT_DIMS, order, 32, wide)))
-        (final,) = take(1)
-        lead = (slice(None),) * 5
-        yield from scatter_lane(
-            spot,
-            wires,
-            WEIGHT_DIMS,
-            order,
-            sources[at].at[lead + (pl.ds(first, wide),)],
-            buffer.at[lead + (pl.ds(0, wide),)],
-            landing,
-            final,
-            32,
-        )
-        yield from finish(at, first, wide, final)
-
-    def series(parity):
-        for number in range(parity, len(chunks), 2):
-            threads = [
-                chunk(lane, part, held[parity][lane]) for lane, part in enumerate(chunks[number])
-            ]
-            while threads:
-                for thread in list(threads):
-                    if next(thread, "end") == "end":
-                        threads.remove(thread)
-                yield
-
-    run([series(0), series(1), total_lane(spot, wires, vector, slots, vector_out)])
-
-
-def scatter_weights(sources, vector, chunks):
+    def ffn(source, out):
+        threads, finals = [], take(1)[0]
+        for low, order in enumerate(PLANE_SCATTER_ORDERS):
+            (held,) = take(1)
+            landing = take(len(landing_shapes(PLANE_DIMS, order, 32, 640, ("z",))))
+            threads.append(
+                scatter_lane(
+                    spot,
+                    wires,
+                    PLANE_DIMS,
+                    order,
+                    source.at[low],
+                    held,
+                    landing,
+                    finals.at[low],
+                    32,
+                    ("z",),
+                )
+            )
+        yield from in_turn(threads)
+        me = spot.at["z"]
+        shared = lax.div(me, 3)
+        spans = []
+        for first, target, wide in ((128 * shared, 0, 512), (512 - 512 * shared, 512, 128)):
+            target = core * 2560 + me * 640 + target
+            spans.append(
+                (
+                    pl.ds(pl.multiple_of(first, 128), wide),
+                    pl.ds(pl.multiple_of(target, 128), wide),
+                )
+            )
+        copies = []
+        for span, columns in spans:
+
+            def piece(z, k):
+                return finals.at[lax.rem(z, 2), 0, 0, lax.div(z, 2), half_rows(k), span]
+
+            slot = out.at[:, columns]
+            copies.append(wires.copy(piece(me, core), slot))
+            copies += [wires.remote(piece(z, k), slot, device) for z, k, device in line]
+        start(copies)
+        yield
+        for copy in copies:
+            copy.wait()
+
+    threads = [ffn(source, out) for source, out in zip(ffn_in, ffn_out)]
+    threads += [
+        part(number, *parts) for chunk in zip(*lanes) for number, parts in enumerate(chunk)
+    ]
+    run(threads + [total_lane(spot, wires, vector, slots, vector_out)])
+
+
+def scatter_weights(sources, ffn, vector, lanes):
     widths = [source.shape[1] for source in sources]
-    sources = [source.reshape(2, 4, 4, 2, 32, source.shape[1]) for source in sources]
-    remotes = 10 + sum(13 * len(parts) for parts in chunks)
-    locals_ = sum(4 * len(parts) for parts in chunks)
+    blocks = [g.reshape(2, 4, 4, 2, 32, g.shape[1]) for g in sources + ffn]
+    parts = sum(len(lane) for lane in lanes)
+    remotes = 10 + 13 * parts + 3 * (16 + 14)
     scratch = [
         pltpu.SemaphoreType.DMA((remotes,)),
         pltpu.SemaphoreType.DMA((remotes,)),
-        pltpu.SemaphoreType.DMA((locals_,)),
+        pltpu.SemaphoreType.DMA((4 * parts + 24,)),
         pltpu.VMEM((4, 4) + vector.shape, F32),
     ]
-    for parity in range(2):
-        for lane in range(3):
-            wide = max(parts[lane][2] for parts in chunks[parity::2])
-            scratch.append(pltpu.VMEM((2, 4, 4, 2, 32, wide), BF16))
-    order = []
-    waves = [list(range(0, len(chunks), 2)), list(range(1, len(chunks), 2))]
-    order = [n for pair in zip(*waves) for n in pair]
-    order += waves[0][len(waves[1]) :]
-    for number in order:
-        for lane, (_, _, wide) in enumerate(chunks[number]):
-            shapes = landing_shapes(WEIGHT_DIMS, SCATTER_ORDERS[lane], 32, wide)
+    for _ in ffn:
+        scratch.append(pltpu.VMEM((2, 1, 1, 2, 32, 640), F32))
+        for order in PLANE_SCATTER_ORDERS:
+            shapes = [(4, 4, 2, 32, 640)]
+            shapes += landing_shapes(PLANE_DIMS, order, 32, 640, ("z",))
             scratch += [pltpu.VMEM(shape, BF16) for shape in shapes]
-            scratch.append(pltpu.VMEM((32, wide), F32))
-    in_vmem = pl.BlockSpec(memory_space=pltpu.VMEM)
+    for chunk in zip(*lanes):
+        for lane, (_, _, wide) in enumerate(chunk):
+            shapes = [(2, 4, 4, 2, 32, wide)]
+            shapes += landing_shapes(WEIGHT_DIMS, SCATTER_ORDERS[lane], 32, wide)
+            scratch += [pltpu.VMEM(shape, BF16) for shape in shapes]
+            scratch.append(pltpu.VMEM((1, 1, 1, 1, 32, wide), F32))
+    out = [jax.ShapeDtypeStruct((16, 2 * width), F32) for width in widths]
+    out += [jax.ShapeDtypeStruct((16, 5120), F32)] * 3
     return pl.pallas_call(
-        functools.partial(weight_scatter_kernel, widths, chunks),
-        out_shape=[jax.ShapeDtypeStruct((16, 2 * width), F32) for width in widths]
-        + [jax.ShapeDtypeStruct(vector.shape, F32)],
-        in_specs=[ANY] * len(sources) + [in_vmem],
-        out_specs=[ANY] * len(sources) + [in_vmem],
+        functools.partial(weight_scatter_kernel, widths, lanes),
+        out_shape=out + [jax.ShapeDtypeStruct(vector.shape, F32)],
+        in_specs=[ANY] * len(blocks) + [IN_VMEM],
+        out_specs=[ANY] * len(blocks) + [IN_VMEM],
         scratch_shapes=scratch,
         compiler_params=pltpu.CompilerParams(
-            collective_id=3, has_side_effects=True, vmem_limit_bytes=62 << 20
+            collective_id=3, has_side_effects=True, vmem_limit_bytes=56 << 20
         ),
-    )(*sources, vector)
+    )(*blocks, vector)
 
 
 def contract(left, right, dims):
     return lax.dot_general(left, right, (dims, ((), ())), preferred_element_type=F32)
 
 
-def key_chunk(slot_ref, kv_ref, chunk):
-    return jnp.concatenate(
-        [
-            kv_ref[pl.ds(pl.multiple_of(slot_ref[chunk * 4 + n] * 64, 64), 64), :]
-            for n in range(4)
-        ],
-        axis=0,
-    )
+def key_chunk(slot_ref, kv, s, h, chunk):
+    pieces = []
+    for n in range(4):
+        slot = slot_ref[chunk * 4 + n]
+        rows = pl.ds(pl.multiple_of(lax.rem(slot, 2) * 64, 64), 64)
+        place = (lax.div(slot, 32), lax.rem(lax.div(slot, 8), 4), lax.rem(lax.div(slot, 2), 4))
+        pieces.append(kv[(s,) + place + (rows, slice(h * 128, h * 128 + 128))])
+    return jnp.concatenate(pieces, axis=0)
 
 
 def allowed_in(chunk, anchor, first):
@@ -575,117 +650,137 @@
     return (key <= anchor) & (key >= first)
 
 
-def attention_kernel(slot_ref, low_ref, kv_ref, q_ref, anchor_ref, first_ref, o_ref, lse_ref, acc, norm):
-    acc[...] = jnp.zeros_like(acc)
-    norm[...] = jnp.zeros_like(norm)
-    low_chunks = lax.div(low_ref[0], 4) + 1
-
-    def step(item, _):
-        is_low = item < low_chunks
-        block = jnp.where(is_low, 0, 1)
-        chunk = jnp.where(is_low, item, item - low_chunks)
-        kv = key_chunk(slot_ref, kv_ref, chunk)
-        scores = contract(kv, q_ref[block], ((1,), (1,)))
-        weights = jnp.where(
-            allowed_in(chunk, anchor_ref[block], first_ref[block]), jnp.exp(scores), 0.0
-        )
-        norm[block] += jnp.sum(weights, axis=0, keepdims=True)
-        acc[block] += contract(kv, weights.astype(BF16), ((0,), (0,)))
-        return 0
-
-    lax.fori_loop(0, 17, step, 0)
-    for block in range(2):
-        total = norm[block]
-        o_ref[block] = acc[block, 64:, :] / total
-        lse_ref[block] = jnp.log(total)
-
-
-def attention_specs():
-    per_head = pl.BlockSpec((None, None, 2, 256, 128), lambda s, h, *_: (s, h, 0, 0, 0))
-    row = pl.BlockSpec((None, None, 2, 1, 256), lambda s, h, *_: (s, h, 0, 0, 0))
-    tall = pl.BlockSpec((None, None, 2, 64, 256), lambda s, h, *_: (s, h, 0, 0, 0))
-    keys = pl.BlockSpec((None, 4096, 128), lambda s, h, *_: (s, 0, h))
-    places = pl.BlockSpec((None, 2, 1, 256), lambda s, h, *_: (s, 0, 0, 0))
-    return per_head, row, tall, keys, places
+def attention_kernel(slot_ref, low_ref, kv, q_ref, anchor_ref, first_ref, o_ref, lse_ref, acc, norm):
+    low = low_ref[0]
+    for s in range(2):
+        for h in range(3):
+
+            def item(chunk, block):
+                kv_rows = key_chunk(slot_ref, kv, s, h, chunk)
+                scores = contract(kv_rows, q_ref[s, h, block], ((1,), (1,)))
+                allowed = allowed_in(chunk, anchor_ref[s, block], first_ref[s, block])
+                weights = jnp.where(allowed, jnp.exp(scores), 0.0)
+                return (
+                    jnp.sum(weights, axis=0, keepdims=True),
+                    contract(kv_rows, weights.astype(BF16), ((0,), (0,))),
+                )
+
+            def early(chunk, carry):
+                total, out = item(chunk, 1)
+                return carry[0] + total, carry[1] + out
+
+            norm[1], acc[1] = lax.fori_loop(
+                0, 8, early, item(15 - lax.div(low, 4), 1), unroll=True
+            )
+            norm[0] = jnp.zeros((1, 256), F32)
+            acc[0] = jnp.zeros((128, 256), F32)
+
+            def either(chunk, _):
+                is_low = low >= 4 * chunk
+                total, out = item(jnp.where(is_low, chunk, 15 - chunk), jnp.where(is_low, 0, 1))
+                share = jnp.where(is_low, 1.0, 0.0)
+                norm[0] += total * share
+                norm[1] += total * (1.0 - share)
+                acc[0] += out * share
+                acc[1] += out * (1.0 - share)
+                return 0
+
+            lax.fori_loop(0, 8, either, 0, unroll=True)
+            for block in range(2):
+                o_ref[s, h, block] = acc[block, 64:, :] / norm[block]
+                lse_ref[s, h, block] = jnp.log(norm[block])
+
+
+IN_VMEM = pl.BlockSpec(memory_space=pltpu.VMEM)
+IN_SMEM = pl.BlockSpec(memory_space=pltpu.SMEM)
 
 
 def attention(slots, low, kv, q, anchor, first):
-    per_head, row, tall, keys, places = attention_specs()
     return pl.pallas_call(
         attention_kernel,
-        grid_spec=pltpu.PrefetchScalarGridSpec(
-            num_scalar_prefetch=2,
-            grid=(2, 3),
-            in_specs=[keys, per_head, places, places],
-            out_specs=[tall, row],
-            scratch_shapes=[pltpu.VMEM((2, 128, 256), F32), pltpu.VMEM((2, 1, 256), F32)],
-        ),
+        in_specs=[IN_SMEM] * 2 + [IN_VMEM] * 4,
+        out_specs=[IN_VMEM] * 2,
         out_shape=[
             jax.ShapeDtypeStruct((2, 3, 2, 64, 256), F32),
             jax.ShapeDtypeStruct((2, 3, 2, 1, 256), F32),
         ],
-        compiler_params=pltpu.CompilerParams(vmem_limit_bytes=32 << 20),
+        scratch_shapes=[pltpu.VMEM((2, 128, 256), F32), pltpu.VMEM((2, 1, 256), F32)],
+        compiler_params=pltpu.CompilerParams(vmem_limit_bytes=40 << 20),
     )(slots, low, kv, q, anchor, first)
 
 
 def attention_back_kernel(
-    slot_ref, low_ref, map_ref, kv_ref, q_ref, d_ref, anchor_ref, first_ref, lse_ref, delta_ref, dq_ref, dkv_ref, acc, sums
+    slot_ref, low_ref, map_ref, kv, q_ref, d_ref, anchor_ref, first_ref, lse_ref, delta_ref, dq_ref, dkv_ref, acc, sums
 ):
-    acc[...] = jnp.zeros_like(acc)
-    sums[...] = jnp.zeros_like(sums)
-    low_chunks = lax.div(low_ref[0], 4) + 1
-
-    def step(item, _):
-        is_low = item < low_chunks
-        block = jnp.where(is_low, 0, 1)
-        chunk = jnp.where(is_low, item, item - low_chunks)
-        kv = key_chunk(slot_ref, kv_ref, chunk)
-        q, d = q_ref[block], d_ref[block]
-        scores = contract(kv, q, ((1,), (1,)))
-        toward = contract(kv, d, ((1,), (1,)))
-        weights = jnp.where(
-            allowed_in(chunk, anchor_ref[block], first_ref[block]),
-            jnp.exp(scores - lse_ref[block]),
-            0.0,
-        )
-        grads = (weights * (toward - delta_ref[block])).astype(BF16)
-        acc[block] += contract(kv, grads, ((0,), (0,)))
-        sums[chunk] += contract(grads, q, ((1,), (0,))) + contract(
-            weights.astype(BF16), d, ((1,), (0,))
-        )
-        return 0
-
-    lax.fori_loop(0, 17, step, 0)
-    for block in range(2):
-        dq_ref[block] = acc[block, :64, :]
-
-    def place(slot, _):
-        block = map_ref[slot]
-        rows = pl.ds(pl.multiple_of(lax.rem(block, 4) * 64, 64), 64)
-        dkv_ref[pl.ds(pl.multiple_of(slot * 64, 64), 64), :] = sums[
-            lax.div(block, 4), rows, :
-        ].astype(BF16)
-        return 0
-
-    lax.fori_loop(0, 64, place, 0)
+    low = low_ref[0]
+    edge = lax.div(low, 4)
+    for s in range(2):
+        for h in range(3):
+
+            def item(chunk, block):
+                kv_rows = key_chunk(slot_ref, kv, s, h, chunk)
+                q, d = q_ref[s, h, block], d_ref[s, h, block]
+                scores = contract(kv_rows, q, ((1,), (1,)))
+                toward = contract(kv_rows, d, ((1,), (1,)))
+                allowed = allowed_in(chunk, anchor_ref[s, block], first_ref[s, block])
+                weights = jnp.where(allowed, jnp.exp(scores - lse_ref[s, h, block]), 0.0)
+                grads = (weights * (toward - delta_ref[s, h, block])).astype(BF16)
+                return (
+                    contract(kv_rows, grads, ((0,), (0,))),
+                    contract(grads, q, ((1,), (0,)))
+                    + contract(weights.astype(BF16), d, ((1,), (0,))),
+                )
+
+            acc[0] = jnp.zeros((128, 256), F32)
+            acc[1], late = item(15 - edge, 1)
+            for chunk in range(8):
+                sums[15 - chunk] = late * jnp.where(edge == chunk, 1.0, 0.0)
+
+            def early(chunk, _):
+                dq, sums[chunk] = item(chunk, 1)
+                acc[1] += dq
+                return 0
+
+            lax.fori_loop(0, 8, early, 0, unroll=True)
+
+            def either(chunk, _):
+                is_low = low >= 4 * chunk
+                dq, dkv = item(jnp.where(is_low, chunk, 15 - chunk), jnp.where(is_low, 0, 1))
+                share = jnp.where(is_low, 1.0, 0.0)
+                acc[0] += dq * share
+                acc[1] += dq * (1.0 - share)
+                sums[chunk] += dkv * share
+                sums[15 - chunk] += dkv * (1.0 - share)
+                return 0
+
+            lax.fori_loop(0, 8, either, 0, unroll=True)
+            for block in range(2):
+                dq_ref[s, h, block] = acc[block, :64, :]
+
+            def put(slot, _):
+                block = map_ref[slot]
+                rows = pl.ds(pl.multiple_of(lax.rem(block, 4) * 64, 64), 64)
+                to = pl.ds(pl.multiple_of(lax.rem(slot, 2) * 64, 64), 64)
+                place = (lax.div(slot, 32), lax.rem(lax.div(slot, 8), 4), lax.rem(lax.div(slot, 2), 4))
+                dkv_ref[(s,) + place + (to, slice(h * 128, h * 128 + 128))] = sums[
+                    lax.div(block, 4), rows, :
+                ].astype(BF16)
+                return 0
+
+            lax.fori_loop(0, 64, put, 0, unroll=4)
 
 
 def attention_back(slots, low, block_map, kv, q, d, anchor, first, lse, delta):
-    per_head, row, tall, keys, places = attention_specs()
     return pl.pallas_call(
         attention_back_kernel,
-        grid_spec=pltpu.PrefetchScalarGridSpec(
-            num_scalar_prefetch=3,
-            grid=(2, 3),
-            in_specs=[keys, per_head, per_head, places, places, row, row],
-            out_specs=[tall, keys],
-            scratch_shapes=[pltpu.VMEM((2, 128, 256), F32), pltpu.VMEM((16, 256, 128), F32)],
-        ),
+        in_specs=[IN_SMEM] * 3 + [IN_VMEM] * 7,
+        out_specs=[IN_VMEM] * 2,
         out_shape=[
             jax.ShapeDtypeStruct((2, 3, 2, 64, 256), F32),
             jax.ShapeDtypeStruct(kv.shape, BF16),
         ],
-        compiler_params=pltpu.CompilerParams(vmem_limit_bytes=32 << 20),
+        scratch_shapes=[pltpu.VMEM((2, 128, 256), F32), pltpu.VMEM((16, 256, 128), F32)],
+        compiler_params=pltpu.CompilerParams(vmem_limit_bytes=48 << 20),
     )(slots, low, block_map, kv, q, d, anchor, first, lse, delta)
 
 
@@ -706,6 +801,39 @@
     mine = lax.dynamic_slice_in_dim(partial, core * half, half)
     theirs = lax.dynamic_slice_in_dim(partial, (1 - core) * half, half)
     return mine + swap(theirs)
+
+
+def along_z(array, by):
+    pairs = []
+    for x in range(4):
+        for y in range(4):
+            for z in range(4):
+                for k in range(2):
+                    to = (z + by) % 4
+                    pairs.append(
+                        (
+                            ((z % 2) * 16 + x * 4 + y) * 4 + (z // 2) * 2 + k,
+                            ((to % 2) * 16 + x * 4 + y) * 4 + (to // 2) * 2 + k,
+                        )
+                    )
+    return lax.ppermute(array, ("ctx", "wt"), pairs)
+
+
+FAR = (1, 3, 2)
+
+
+def spread(array, core):
+    far = [along_z(array, by) for by in FAR]
+    return share(array, core), jnp.concatenate([share(rows, core) for rows in far], axis=0)
+
+
+def collect(partials, core):
+    near, far = partials
+    own = total_rows(near, core)
+    for number, by in enumerate(FAR):
+        rows = total_rows(far[number * 256 : (number + 1) * 256], core).astype(BF16)
+        own = own + along_z(rows, 4 - by).astype(F32)
+    return own
 
 
 def norm_forward(values, gain):
@@ -773,15 +901,11 @@
         [key_weight.reshape(16, 2, 3, 64), value_weight.reshape(16, 2, 3, 64)], axis=3
     ).reshape(16, 2, 384)
     qkv_pack = jnp.concatenate([halves(query_weight), kv_halves], axis=2).reshape(16, 2304)
-    lanes = [
-        [(0, lane * 384, 384), (1, lane * 256, 256), (2 + lane, 0, 2432)] for lane in range(3)
-    ]
-    (qkv_w, out_w, gate_w, up_w, down_w), (tokens_all, grad_out_all) = gather_weights(
-        [qkv_pack, out_weight, gate_weight, up_weight, down_weight],
-        [tokens[0], cotangent[0]],
-        lanes,
+    lanes = [[(0, lane * 384, 384), (1, lane * 256, 256)] for lane in range(3)]
+    grad_out_line = spread(cotangent[0], core)
+    (qkv_w, out_w, gate_w, up_w, down_w), tokens_all = gather_weights(
+        [qkv_pack, out_weight], [gate_weight, up_weight, down_weight], tokens[0], lanes
     )
-    grad_out_all = grad_out_all.reshape(256, 2048)
     rows = tokens[0].astype(F32)
 
     offsets = jnp.arange(64, dtype=jnp.int32)
@@ -831,23 +955,41 @@
     mixed = rows + total_rows(contract(merged, out_w, ((1,), (1,))), core)
 
     second_out, second_hat, second_inv = norm_forward(mixed, second_gain)
-    second_low = share(second_out.astype(BF16), core)
-    gate = jnp.dot(second_low, gate_w, preferred_element_type=F32)
-    upward = jnp.dot(second_low, up_w, preferred_element_type=F32)
-    sigmoid_gate = jax.nn.sigmoid(gate)
-    product = (gate * sigmoid_gate * upward).astype(BF16)
-    activations = (
-        mixed + total_rows(contract(product, down_w, ((1,), (1,))), core)
-    ).astype(BF16)[None]
-
-    grad_product = jnp.dot(grad_out_all, down_w, preferred_element_type=F32)
-    grad_gate = (grad_product * upward * sigmoid_gate * (1.0 + gate * (1.0 - sigmoid_gate))).astype(
-        BF16
-    )
-    grad_upward = (grad_product * gate * sigmoid_gate).astype(BF16)
-    grad_second = total_rows(
-        contract(grad_gate, gate_w, ((1,), (1,))) + contract(grad_upward, up_w, ((1,), (1,))), core
-    )
+    second_line = spread(second_out.astype(BF16), core)
+    z = lax.div(lax.axis_index("wt"), 2) * 2 + lax.div(ctx, 16)
+    unit = jnp.arange(640, dtype=jnp.int32)
+    held = jnp.where((z == 3) & (unit < 128), 0.0, 1.0).astype(F32)[None, :]
+    gate_w, up_w, down_w = (w.reshape(2048, 640) for w in (gate_w, up_w, down_w))
+
+    def feed_forward(second, grad_out):
+        gate = jnp.dot(second, gate_w, preferred_element_type=F32)
+        upward = jnp.dot(second, up_w, preferred_element_type=F32) * held
+        grad_product = jnp.dot(grad_out, down_w, preferred_element_type=F32) * held
+        sigmoid = jax.nn.sigmoid(gate)
+        product = (gate * sigmoid * upward).astype(BF16)
+        grad_gate = (
+            grad_product * upward * sigmoid * (1.0 + gate * (1.0 - sigmoid))
+        ).astype(BF16)
+        grad_upward = (grad_product * gate * sigmoid).astype(BF16)
+        grad_second = contract(grad_gate, gate_w, ((1,), (1,))) + contract(
+            grad_upward, up_w, ((1,), (1,))
+        )
+        branch = contract(product, down_w, ((1,), (1,)))
+        return product, grad_gate, grad_upward, branch, grad_second
+
+    results = [feed_forward(*pair) for pair in zip(second_line, grad_out_line)]
+    grad_second = collect([result[4] for result in results], core)
+    activations = (mixed + collect([result[3] for result in results], core)).astype(BF16)[None]
+
+    def outer(left, right):
+        return contract(left, right, ((0,), (0,)))
+
+    def outer_line(left, right):
+        return sum(outer(*pair) for pair in zip(left, right)).astype(BF16)
+
+    gate_g = outer_line(second_line, [result[1] for result in results])
+    up_g = outer_line(second_line, [result[2] for result in results])
+    down_g = outer_line(grad_out_line, [result[0] for result in results])
     second_back, second_terms = norm_backward(grad_second, second_gain, second_hat, second_inv)
     grad_mixed = cotangent[0].astype(F32) + second_back
     grad_branch = share(grad_mixed.astype(BF16), core)
@@ -868,7 +1010,7 @@
         lse,
         delta_rows,
     )
-    own_kv = scatter_keys(grad_kv.reshape(2, 2, 4, 4, 128, 384)).reshape(256, 3, 2, 64)
+    own_kv = scatter_keys(grad_kv).reshape(256, 3, 2, 64)
     query_unrot = unrotate(from_blocks(grad_query_tall) * 0.125, cosine, sine)
     query_back, query_terms = norm_backward(query_unrot, query_gain, query_hat, query_inv)
     key_unrot = unrotate(own_kv[:, :, 0], cosine, sine)
@@ -879,9 +1021,6 @@
     first_back, first_terms = norm_backward(grad_first, first_gain, first_hat, first_inv)
     token_grad = (grad_mixed + first_back).astype(BF16)[None]
 
-    def outer(left, right):
-        return contract(left, right, ((0,), (0,))).astype(BF16)
-
     gains = jnp.concatenate(
         [
             jnp.sum(first_terms, axis=0),
@@ -891,25 +1030,25 @@
             jnp.zeros((896,), F32),
         ]
     ).reshape(8, 640)
-    ffn = [[(2 + lane, first, wide) for lane in range(3)] for first, wide in
-           ((0, 640), (640, 640), (1280, 640), (1920, 512))]
-    chunks = ffn + [[(at, lane * wide, wide) for lane in range(3)] for at, wide in ((0, 384), (1, 256))]
     qkv_g, out_g, gate_g, up_g, down_g, gains = scatter_weights(
         [
-            outer(first_low, grad_qkv),
-            outer(grad_branch, merged),
-            outer(second_low, grad_gate),
-            outer(second_low, grad_upward),
-            outer(grad_out_all, product),
+            outer(first_low, grad_qkv).astype(BF16),
+            outer(grad_branch, merged).astype(BF16),
         ],
+        [gate_g, up_g, down_g],
         gains,
-        chunks,
+        lanes,
     )
     gains = gains.reshape(5120)
     qkv_g = qkv_g.reshape(16, 2, 1152)
     query_g = qkv_g[:, :, :768].reshape(16, 1536)
     kv_g = qkv_g[:, :, 768:].reshape(16, 2, 3, 2, 64)
     key_g, value_g = kv_g[:, :, :, 0].reshape(16, 384), kv_g[:, :, :, 1].reshape(16, 384)
+
+    def whole_rows(pieces):
+        return jnp.concatenate([pieces[:, :2432], pieces[:, 2560:4992]], axis=1)
+
+    gate_g, up_g, down_g = (whole_rows(pieces) for pieces in (gate_g, up_g, down_g))
     return (
         activations,
         token_grad,

time: 742 us -> 580 us (0.78)
  Pallas kernels: 551 us -> 336 us
  starting transfers between devices: 16.5 us -> 41.8 us
  waiting for transfers between devices: 0.11 us -> 19.7 us
  other arithmetic: 28.6 us -> 45.3 us
  matrix products: 73.7 us -> 61.3 us
    pallas_call x4, Pallas kernels: 315 us -> 193 us  [the longest x1 92.5 us: scatter_weights(): pl.pallas_call(functools.partial(weight_scatter_kernel, widths, lanes), o...]
    pallas_call x1, Pallas kernels: 189 us -> 96 us  [gather_weights(): pl.pallas_call(functools.partial(weight_gather_kernel, widths, lanes), ou...]
    ppermute x0 -> x12, starting transfers between devices: none -> 22.1 us  [along_z(): return lax.ppermute(array, ('ctx', 'wt'), pairs)]
    ppermute x0 -> x12, waiting for transfers between devices: none -> 19 us  [along_z(): return lax.ppermute(array, ('ctx', 'wt'), pairs)]
    convert_element_type x1 -> x7, other arithmetic: 0.15 us -> 8.27 us  [the longest x6 8.12 us: collect(): rows = total_rows(far[number * 256:(number + 1) * 256], core).astype(BF16)]
    unnamed x123 -> x136, local copies, waits for them, and re-layouts: 18.8 us -> 11.3 us
    dot_general x3 -> x6, matrix products: 19.9 us -> 13.1 us  [the longest x2 5.68 us: feed_forward(): gate = jnp.dot(second, gate_w, preferred_element_type=F32)]
    dot_general x10 -> x16, matrix products: 48.1 us -> 42.6 us  [contract(): lax.dot_general(left, right, (dims, ((), ())), preferred_element_type=F32)]
  transfers between devices with their start and end apart: 7 -> 32, of which waited for: 1 -> 5; matrix products, arithmetic and copies ran while one was open for 13% -> 28% of each run, Pallas kernels for 63% -> 59%
where the time goes in v2:
time: 580 us; the launch traced here: 571 us
  Pallas kernels  336 us (58%)
  local copies, waits for them, and re-layouts  64.3 us (11%)
  matrix products  61.3 us (11%)
  other arithmetic  45.3 us (8%)
  starting transfers between devices  41.8 us (7%)
  waiting for transfers between devices  19.7 us (3%)
    pallas_call x1, Pallas kernels, gather_weights(): pl.pallas_call(functools.partial(weight_gather_kernel, widths, lanes), ou...  96 us
    pallas_call x1, Pallas kernels, scatter_weights(): pl.pallas_call(functools.partial(weight_scatter_kernel, widths, lanes), o...  92.5 us
    pallas_call x1, Pallas kernels, gather_keys(): pl.pallas_call(key_gather_kernel, out_shape=jax.ShapeDtypeStruct((2, 2, 4...  46.2 us
    pallas_call x1, Pallas kernels, attention_back(): pl.pallas_call(attention_back_kernel, in_specs=[IN_SMEM] * 3 + [IN_VMEM]...  43.1 us
    dot_general x16, matrix products, contract(): lax.dot_general(left, right, (dims, ((), ())), preferred_element_type=F32)  42.6 us
    pallas_call x1, Pallas kernels, scatter_keys(): pl.pallas_call(key_scatter_kernel, out_shape=jax.ShapeDtypeStruct((2, 1,...  41.1 us
    ppermute x12, starting transfers between devices, along_z(): return lax.ppermute(array, ('ctx', 'wt'), pairs)  22.1 us
    ppermute x20, starting transfers between devices, swap(): return lax.ppermute(array, 'wt', [(0, 1), (1, 0), (2, 3), (3, 2)])  19.7 us
  transfers between devices with their start and end apart: 32, of which 5 were waited for; matrix products, arithmetic and copies ran while one was open for 28% of the time, Pallas kernels for 59%

profile of v2, /device:TPU:1, one launch (start us, length us, event | category | flops | bytes accessed | tf_op | source)
XLA Modules:
  0.0 570.6 jit_solution(17101196525716496642)
XLA Ops:
  0.7 2.5 collective-permute-start.18
  3.2 2.2 collective-permute-start.20
  16.1 96.0 %shard_map.255 = (bf16[2,4,4,2,32,1152]{5,4,3,2,1,0:T(8,128)(2,1)}, bf16[2,4,4,2,32,768]{5,4,3,2,1,0:T(8,128)(2,1)}, bf16[2,4,4,2,32,640]{5,4,3,2,1,0:T(8,128)(2...) custom-call(bf16[16,2304]{1,0:T(8,128)(2,1)} %bitcast.211, ...), custom_call_target="tpu_custom_call" | custom-call | tf_op jit(solution)/shard_map/pallas_call | solution.py:389
  113.6 1.5 multiply_convert_fusion
  115.2 3.9 fusion.51
  128.5 46.2 %shard_map.256.kv = bf16[2,2,4,4,128,384]{5,4,3,2,1,0:T(8,128)(2,1)} custom-call(bf16[2,128,384]{2,1,0:T(8,128)(2,1)} %copy.111.source), custom_call_target="tpu_custom_call" | custom-call | tf_op jit(solution)/shard_map/pallas_call | solution.py:420
  178.2 2.8 copy-done
  181.0 16.7 %shard_map.257 = (f32[2,3,2,64,256]{4,3,2,1,0:T(8,128)S(1)}, f32[2,3,2,1,256]{4,3,2,1,0:T(1,128)S(1)}) custom-call(s32[64]{0:T(128)S(1)} %select_reduce_fusion.1.slot_ref, s32[1]{0:T(128)S(1)} %bitcast.163, bf16[2,2,4,4,128,384]{5,4,3,2,1,0:T(8,128)(2,1)S(1)} %copy-done, bf16[2,3,2,256,128]{4,3,2,1,0:T(8,128)(2,1)S(1)} %pad.8.q_ref, ...), custom_call_target="tpu_custom_call" | custom-call | tf_op jit(solution)/shard_map/pallas_call | solution.py:699
  197.7 1.8 reshape.416
  199.5 1.8 copy.114
  202.8 3.1 fusion.52
  205.9 4.0 collective-permute-start.19
  219.4 2.6 fusion.57
  222.0 4.3 collective-permute-start.4
  226.3 2.1 collective-permute-start.8
  242.4 7.3 %collective-permute-done.8 = bf16[128,2048]{1,0:T(8,128)(2,1)S(1)} collective-permute-done((bf16[128,2048]{1,0:T(8,128)(2,1)S(1)}, bf16[128,2048]{1,0:T(8,128)(2,1)S(1)}, u32[]{:S(2)}, u32[]{:S(2)}) %collective-permute-start.8) | collective-permute-done | bytes 524320 | tf_op jit(solution)/shard_map/ppermute | solution.py:819
  252.6 2.6 fusion.54
  255.3 4.7 multiply_convert_fusion.1
  259.9 2.6 fusion.58
  262.6 3.9 convolution_add_fusion
  271.5 2.6 fusion.55
  274.1 4.1 add_convert_fusion.2
  278.2 4.1 add_convert_fusion.1
  286.2 3.1 collective-permute-start.29
  290.8 1.5 collective-permute-start.27
  295.0 4.2 add_convert_fusion
  302.8 10.2 %collective-permute-done.27 = bf16[128,2048]{1,0:T(8,128)(2,1)S(1)} collective-permute-done((bf16[128,2048]{1,0:T(8,128)(2,1)S(1)}, bf16[128,2048]{1,0:T(8,128)(2,1)S(1)}, u32[]{:S(2)}, u32[]{:S(2)}) %collective-permute-start.27) | collective-permute-done | bytes 524320 | tf_op jit(solution)/shard_map/ppermute | solution.py:819
  313.9 2.4 multiply_reduce_fusion.1
  318.8 1.5 collective-permute-start.15
  323.7 1.7 convolution_convert_fusion.2
  325.4 2.7 reshape_reshape.7
  328.2 3.0 fusion.2
  333.1 43.1 %shard_map.258 = (f32[2,3,2,64,256]{4,3,2,1,0:T(8,128)S(1)}, bf16[2,2,4,4,128,384]{5,4,3,2,1,0:T(8,128)(2,1)}) custom-call(s32[64]{0:T(128)S(1)} %select_reduce_fusion.1.slot_ref, s32[1]{0:T(128)S(1)} %bitcast.164, s32[64]{0:T(128)S(1)} %copy-done.1, bf16[2,2,4,4,128,384]{5,4,3,2,1,0:T(8,128)(2,1)} %shard_map.256.kv, ...), custom_call_target="tpu_custom_call" | custom-call | tf_op jit(solution)/shard_map/pallas_call | solution.py:774
  376.2 41.1 %shard_map.259 = f32[2,1,1,1,128,384]{5,4,3,2,1,0:T(8,128)S(1)} custom-call(bf16[2,2,4,4,128,384]{5,4,3,2,1,0:T(8,128)(2,1)} %get-tuple-element.38.source), custom_call_target="tpu_custom_call" | custom-call | tf_op jit(solution)/shard_map/pallas_call | solution.py:464
  419.2 1.8 copy.138
  422.4 2.1 mul.596
  424.5 2.4 copy.142
  426.9 2.6 mul.598
  431.7 2.3 copy.118
  435.0 2.3 copy.120
  437.2 1.6 multiply_reduce_fusion.4
  438.9 4.0 fusion.17
  444.1 5.9 %collective-permute-start.31 = (f32[128,2048]{1,0:T(8,128)}, f32[128,2048]{1,0:T(8,128)S(1)}, u32[]{:S(2)}, u32[]{:S(2)}) collective-permute-start(f32[128,2048]{1,0:T(8,128)} %constant_dynamic-slice_fusion), channel_id=1, source_target_pairs={{0,1},{1,0},{2,3},{3,2},{4,5},{5,4},{6,7},{7,6},{8,9},{9,8},{10,11... | collective-permute-start | bytes 3145736 | tf_op jit(solution)/shard_map/ppermute | solution.py:788
  449.9 2.1 add_convert_fusion.9
  453.1 4.1 convolution_convert_fusion.1
  457.2 3.7 convolution_convert_fusion
  463.0 92.5 %shard_map.260 = (f32[16,2304]{1,0:T(8,128)}, f32[16,1536]{1,0:T(8,128)}, f32[16,5120]{1,0:T(8,128)}, f32[16,5120]{1,0:T(8,128)}, f32[16,5120]{1,0:T(8,128)}, /*index=5*/f32[8,640]{1,0:T(8,128)}) custom-call(bf16[2,4,4,2,32,1152]{5,4,3,2,1,0:T(8,128)(2,1)} %bitcast.165, bf16[2,4,4,2,32,768]{5,4,3,2,1,0:T(8,128)(2,1)} %bitcast.185, ...), custom_call_target="tpu_custom_call" | custom-call | tf_op jit(solution)/shard_map/pallas_call | solution.py:622
  565.6 3.9 fusion.16
  (332 shorter events, 98.7 us)
Async XLA Ops:
  0.6 113.0 %copy-start.41 = (f32[2048]{0:T(1024)S(1)}, f32[2048]{0:T(1024)}, u32[]{:S(2)}) copy-start(f32[2048]{0:T(1024)} %param.21) | copy-start | bytes 24580
  0.7 205.3 %collective-permute-start.18 = (bf16[128,2048]{1,0:T(8,128)(2,1)}, bf16[128,2048]{1,0:T(8,128)(2,1)}, u32[]{:S(2)}, u32[]{:S(2)}) collective-permute-start(bf16[128,2048]{1,0:T(8,128)(2,1)} %bitcast.176), channel_id=1, source_target_pairs={{0,64},{1,65},{64,2},{65,3},{2,66},{3,67},{66,0},{67,1},{4,68},{5,... | collective-permute-start | bytes 1572872 | tf_op jit(solution)/shard_map/ppermute | solution.py:819
  3.2 206.9 %collective-permute-start.20 = (bf16[128,2048]{1,0:T(8,128)(2,1)}, bf16[128,2048]{1,0:T(8,128)(2,1)}, u32[]{:S(2)}, u32[]{:S(2)}) collective-permute-start(bf16[128,2048]{1,0:T(8,128)(2,1)} %bitcast.177), channel_id=1, source_target_pairs={{0,66},{1,67},{64,0},{65,1},{2,64},{3,65},{66,2},{67,3},{4,70},{5,... | collective-permute-start | bytes 1572872 | tf_op jit(solution)/shard_map/ppermute | solution.py:819
  5.4 205.2 %collective-permute-start.22 = (bf16[128,2048]{1,0:T(8,128)(2,1)}, bf16[128,2048]{1,0:T(8,128)(2,1)}, u32[]{:S(2)}, u32[]{:S(2)}) collective-permute-start(bf16[128,2048]{1,0:T(8,128)(2,1)} %bitcast.178), channel_id=1, source_target_pairs={{0,2},{1,3},{64,66},{65,67},{2,0},{3,1},{66,64},{67,65},{4,6},{5,7... | collective-permute-start | bytes 1572872 | tf_op jit(solution)/shard_map/ppermute | solution.py:819
  6.6 204.1 %collective-permute-start.16 = (bf16[128,2048]{1,0:T(8,128)(2,1)}, bf16[128,2048]{1,0:T(8,128)(2,1)}, u32[]{:S(2)}, u32[]{:S(2)}) collective-permute-start(bf16[128,2048]{1,0:T(8,128)(2,1)} %bitcast.179), channel_id=1, source_target_pairs={{0,1},{1,0},{2,3},{3,2},{4,5},{5,4},{6,7},{7,6},{8,9},{9,8},{10,11... | collective-permute-start | bytes 1572872 | tf_op jit(solution)/shard_map/ppermute | solution.py:788
  11.9 115.4 %collective-permute-start = (s32[1,2,128]{2,1,0:T(2,128)S(1)}, s32[1,2,128]{2,1,0:T(2,128)S(1)}, u32[]{:S(2)}, u32[]{:S(2)}) collective-permute-start(s32[1,2,128]{2,1,0:T(2,128)S(1)} %add_bitcast_fusion), channel_id=1, source_target_pairs={{0,1},{1,0},{2,3},{3,2},{4,5},{5,4},{6,7},{7,6},{8,9},{9,8},{10,11... | collective-permute-start | bytes 3080 | tf_op jit(solution)/shard_map/ppermute | solution.py:788
  202.8 7.8 %copy-start.18 = (bf16[1,128,2048]{2,1,0:T(8,128)(2,1)S(1)}, bf16[1,128,2048]{2,1,0:T(8,128)(2,1)}, u32[]{:S(2)}) copy-start(bf16[1,128,2048]{2,1,0:T(8,128)(2,1)} %param.17) | copy-start | bytes 1572868
  205.9 5.9 %collective-permute-start.19 = (bf16[128,2048]{1,0:T(8,128)(2,1)}, bf16[128,2048]{1,0:T(8,128)(2,1)S(1)}, u32[]{:S(2)}, u32[]{:S(2)}) collective-permute-start(bf16[128,2048]{1,0:T(8,128)(2,1)} %collective-permute-done.18), channel_id=1, source_target_pairs={{0,1},{1,0},{2,3},{3,2},{4,5},{5,4},{6,7},{7,6},{8,9},{9,8},{10,11... | collective-permute-start | bytes 1572872 | tf_op jit(solution)/shard_map/ppermute | solution.py:788
  210.0 6.5 %collective-permute-start.1 = (f32[128,2048]{1,0:T(8,128)S(1)}, f32[128,2048]{1,0:T(8,128)S(1)}, u32[]{:S(2)}, u32[]{:S(2)}) collective-permute-start(f32[128,2048]{1,0:T(8,128)S(1)} %constant_dynamic-slice_fusion.9), channel_id=1, source_target_pairs={{0,1},{1,0},{2,3},{3,2},{4,5},{5,4},{6,7},{7,6},{8,9},{9,8},{10,11... | collective-permute-start | bytes 3145736 | tf_op jit(solution)/shard_map/ppermute | solution.py:788
  210.1 3.7 collective-permute-start.21
  210.6 4.6 collective-permute-start.23
  216.9 99.5 %copy-start.49 = (f32[128]{0:T(128)}, f32[128]{0:T(128)S(1)}, u32[]{:S(2)}) copy-start(f32[128]{0:T(128)S(1)} %add_rsqrt_fusion.4) | copy-start | bytes 1540
  217.1 11.8 %collective-permute-start.2 = (bf16[128,2048]{1,0:T(8,128)(2,1)S(1)}, bf16[128,2048]{1,0:T(8,128)(2,1)S(1)}, u32[]{:S(2)}, u32[]{:S(2)}) collective-permute-start(bf16[128,2048]{1,0:T(8,128)(2,1)S(1)} %multiply_convert_fusion.4), channel_id=1, source_target_pairs={{0,1},{1,0},{2,3},{3,2},{4,5},{5,4},{6,7},{7,6},{8,9},{9,8},{10,11... | collective-permute-start | bytes 1572872 | tf_op jit(solution)/shard_map/ppermute | solution.py:788
  222.0 7.2 %copy-start.31 = (bf16[2,4,4,2,32,640]{5,4,3,2,1,0:T(8,128)(2,1)S(1)}, bf16[2,4,4,2,32,640]{5,4,3,2,1,0:T(8,128)(2,1)}, u32[]{:S(2)}) copy-start(bf16[2,4,4,2,32,640]{5,4,3,2,1,0:T(8,128)(2,1)} %get-tuple-element.33) | copy-start | bytes 7864324
  222.0 17.6 %collective-permute-start.4 = (bf16[128,2048]{1,0:T(8,128)(2,1)S(1)}, bf16[128,2048]{1,0:T(8,128)(2,1)S(1)}, u32[]{:S(2)}, u32[]{:S(2)}) collective-permute-start(bf16[128,2048]{1,0:T(8,128)(2,1)S(1)} %multiply_convert_fusion.4), channel_id=1, source_target_pairs={{0,64},{1,65},{64,2},{65,3},{2,66},{3,67},{66,0},{67,1},{4,68},{5,... | collective-permute-start | bytes 1572872 | tf_op jit(solution)/shard_map/ppermute | solution.py:819
  226.3 16.1 %collective-permute-start.6 = (bf16[128,2048]{1,0:T(8,128)(2,1)S(1)}, bf16[128,2048]{1,0:T(8,128)(2,1)S(1)}, u32[]{:S(2)}, u32[]{:S(2)}) collective-permute-start(bf16[128,2048]{1,0:T(8,128)(2,1)S(1)} %multiply_convert_fusion.4), channel_id=1, source_target_pairs={{0,66},{1,67},{64,0},{65,1},{2,64},{3,65},{66,2},{67,3},{4,70},{5,... | collective-permute-start | bytes 1572872 | tf_op jit(solution)/shard_map/ppermute | solution.py:819
  226.3 23.4 %collective-permute-start.8 = (bf16[128,2048]{1,0:T(8,128)(2,1)S(1)}, bf16[128,2048]{1,0:T(8,128)(2,1)S(1)}, u32[]{:S(2)}, u32[]{:S(2)}) collective-permute-start(bf16[128,2048]{1,0:T(8,128)(2,1)S(1)} %multiply_convert_fusion.4), channel_id=1, source_target_pairs={{0,2},{1,3},{64,66},{65,67},{2,0},{3,1},{66,64},{67,65},{4,6},{5,7... | collective-permute-start | bytes 1572872 | tf_op jit(solution)/shard_map/ppermute | solution.py:819
  237.9 61.3 %collective-permute-start.17 = (f32[128,2048]{1,0:T(8,128)}, f32[128,2048]{1,0:T(8,128)}, u32[]{:S(2)}, u32[]{:S(2)}) collective-permute-start(f32[128,2048]{1,0:T(8,128)} %constant_dynamic-slice_fusion.4), channel_id=1, source_target_pairs={{0,1},{1,0},{2,3},{3,2},{4,5},{5,4},{6,7},{7,6},{8,9},{9,8},{10,11... | collective-permute-start | bytes 3145736 | tf_op jit(solution)/shard_map/ppermute | solution.py:788
  239.6 12.2 %collective-permute-start.5 = (bf16[128,2048]{1,0:T(8,128)(2,1)S(1)}, bf16[128,2048]{1,0:T(8,128)(2,1)S(1)}, u32[]{:S(2)}, u32[]{:S(2)}) collective-permute-start(bf16[128,2048]{1,0:T(8,128)(2,1)S(1)} %collective-permute-done.4), channel_id=1, source_target_pairs={{0,1},{1,0},{2,3},{3,2},{4,5},{5,4},{6,7},{7,6},{8,9},{9,8},{10,11... | collective-permute-start | bytes 1572872 | tf_op jit(solution)/shard_map/ppermute | solution.py:788
  240.7 11.0 %copy-start.10 = (f32[256,2048]{1,0:T(8,128)}, f32[256,2048]{1,0:T(8,128)S(1)}, u32[]{:S(2)}) copy-start(f32[256,2048]{1,0:T(8,128)S(1)} %fusion.53) | copy-start | bytes 6291460
  241.9 323.7 %collective-permute-start.3 = (f32[128,2048]{1,0:T(8,128)}, f32[128,2048]{1,0:T(8,128)}, u32[]{:S(2)}, u32[]{:S(2)}) collective-permute-start(f32[128,2048]{1,0:T(8,128)} %constant_dynamic-slice_fusion.8), channel_id=1, source_target_pairs={{0,1},{1,0},{2,3},{3,2},{4,5},{5,4},{6,7},{7,6},{8,9},{9,8},{10,11... | collective-permute-start | bytes 3145736 | tf_op jit(solution)/shard_map/ppermute | solution.py:788
  242.4 9.7 %collective-permute-start.7 = (bf16[128,2048]{1,0:T(8,128)(2,1)S(1)}, bf16[128,2048]{1,0:T(8,128)(2,1)S(1)}, u32[]{:S(2)}, u32[]{:S(2)}) collective-permute-start(bf16[128,2048]{1,0:T(8,128)(2,1)S(1)} %collective-permute-done.6), channel_id=1, source_target_pairs={{0,1},{1,0},{2,3},{3,2},{4,5},{5,4},{6,7},{7,6},{8,9},{9,8},{10,11... | collective-permute-start | bytes 1572872 | tf_op jit(solution)/shard_map/ppermute | solution.py:788
  249.7 2.7 collective-permute-start.9
  268.4 16.4 %collective-permute-start.28 = (f32[128,2048]{1,0:T(8,128)}, f32[128,2048]{1,0:T(8,128)}, u32[]{:S(2)}, u32[]{:S(2)}) collective-permute-start(f32[128,2048]{1,0:T(8,128)} %constant_dynamic-slice_fusion.1), channel_id=1, source_target_pairs={{0,1},{1,0},{2,3},{3,2},{4,5},{5,4},{6,7},{7,6},{8,9},{9,8},{10,11... | collective-permute-start | bytes 3145736 | tf_op jit(solution)/shard_map/ppermute | solution.py:788
  269.8 19.6 %collective-permute-start.26 = (f32[128,2048]{1,0:T(8,128)}, f32[128,2048]{1,0:T(8,128)}, u32[]{:S(2)}, u32[]{:S(2)}) collective-permute-start(f32[128,2048]{1,0:T(8,128)} %constant_dynamic-slice_fusion.2), channel_id=1, source_target_pairs={{0,1},{1,0},{2,3},{3,2},{4,5},{5,4},{6,7},{7,6},{8,9},{9,8},{10,11... | collective-permute-start | bytes 3145736 | tf_op jit(solution)/shard_map/ppermute | solution.py:788
  271.0 21.2 %collective-permute-start.24 = (f32[128,2048]{1,0:T(8,128)}, f32[128,2048]{1,0:T(8,128)}, u32[]{:S(2)}, u32[]{:S(2)}) collective-permute-start(f32[128,2048]{1,0:T(8,128)} %constant_dynamic-slice_fusion.3), channel_id=1, source_target_pairs={{0,1},{1,0},{2,3},{3,2},{4,5},{5,4},{6,7},{7,6},{8,9},{9,8},{10,11... | collective-permute-start | bytes 3145736 | tf_op jit(solution)/shard_map/ppermute | solution.py:788
  286.2 8.8 %copy-start.44 = (bf16[768,2048]{1,0:T(8,128)(2,1)S(1)}, bf16[768,2048]{1,0:T(8,128)(2,1)}, u32[]{:S(2)}) copy-start(bf16[768,2048]{1,0:T(8,128)(2,1)} %copy-done.43) | copy-start | bytes 9437188
  286.2 8.8 %copy-start.62 = (bf16[768,640]{1,0:T(8,128)(2,1)S(1)}, bf16[768,640]{1,0:T(8,128)(2,1)}, u32[]{:S(2)}) copy-start(bf16[768,640]{1,0:T(8,128)(2,1)} %get-tuple-element.65) | copy-start | bytes 2949124
  286.2 15.1 %collective-permute-start.29 = (bf16[128,2048]{1,0:T(8,128)(2,1)S(1)}, bf16[128,2048]{1,0:T(8,128)(2,1)S(1)}, u32[]{:S(2)}, u32[]{:S(2)}) collective-permute-start(bf16[128,2048]{1,0:T(8,128)(2,1)S(1)} %add_convert_fusion.3), channel_id=1, source_target_pairs={{0,2},{1,3},{64,66},{65,67},{2,0},{3,1},{66,64},{67,65},{4,6},{5,7... | collective-permute-start | bytes 1572872 | tf_op jit(solution)/shard_map/ppermute | solution.py:819
  290.8 22.2 %collective-permute-start.27 = (bf16[128,2048]{1,0:T(8,128)(2,1)S(1)}, bf16[128,2048]{1,0:T(8,128)(2,1)S(1)}, u32[]{:S(2)}, u32[]{:S(2)}) collective-permute-start(bf16[128,2048]{1,0:T(8,128)(2,1)S(1)} %add_convert_fusion.4), channel_id=1, source_target_pairs={{0,64},{1,65},{64,2},{65,3},{2,66},{3,67},{66,0},{67,1},{4,68},{5,... | collective-permute-start | bytes 1572872 | tf_op jit(solution)/shard_map/ppermute | solution.py:819
  293.7 20.3 %copy-start.9 = (f32[256,2048]{1,0:T(8,128)S(1)}, f32[256,2048]{1,0:T(8,128)}, u32[]{:S(2)}) copy-start(f32[256,2048]{1,0:T(8,128)} %copy-done.8) | copy-start | bytes 6291460
  293.7 20.3 %collective-permute-start.25 = (bf16[128,2048]{1,0:T(8,128)(2,1)S(1)}, bf16[128,2048]{1,0:T(8,128)(2,1)S(1)}, u32[]{:S(2)}, u32[]{:S(2)}) collective-permute-start(bf16[128,2048]{1,0:T(8,128)(2,1)S(1)} %add_convert_fusion.5), channel_id=1, source_target_pairs={{0,66},{1,67},{64,0},{65,1},{2,64},{3,65},{66,2},{67,3},{4,70},{5,... | collective-permute-start | bytes 1572872 | tf_op jit(solution)/shard_map/ppermute | solution.py:819
  299.2 17.2 %copy-start.19 = (bf16[1,128,2048]{2,1,0:T(8,128)(2,1)S(1)}, bf16[1,128,2048]{2,1,0:T(8,128)(2,1)}, u32[]{:S(2)}) copy-start(bf16[1,128,2048]{2,1,0:T(8,128)(2,1)} %param.17) | copy-start | bytes 1572868
  299.2 18.7 %collective-permute-start.14 = (f32[128,2048]{1,0:T(8,128)S(1)}, f32[128,2048]{1,0:T(8,128)S(1)}, u32[]{:S(2)}, u32[]{:S(2)}) collective-permute-start(f32[128,2048]{1,0:T(8,128)S(1)} %constant_dynamic-slice_fusion.5), channel_id=1, source_target_pairs={{0,1},{1,0},{2,3},{3,2},{4,5},{5,4},{6,7},{7,6},{8,9},{9,8},{10,11... | collective-permute-start | bytes 3145736 | tf_op jit(solution)/shard_map/ppermute | solution.py:788
  301.4 18.9 %collective-permute-start.12 = (f32[128,2048]{1,0:T(8,128)S(1)}, f32[128,2048]{1,0:T(8,128)S(1)}, u32[]{:S(2)}, u32[]{:S(2)}) collective-permute-start(f32[128,2048]{1,0:T(8,128)S(1)} %constant_dynamic-slice_fusion.6), channel_id=1, source_target_pairs={{0,1},{1,0},{2,3},{3,2},{4,5},{5,4},{6,7},{7,6},{8,9},{9,8},{10,11... | collective-permute-start | bytes 3145736 | tf_op jit(solution)/shard_map/ppermute | solution.py:788
  313.0 136.9 %collective-permute-start.10 = (f32[128,2048]{1,0:T(8,128)}, f32[128,2048]{1,0:T(8,128)}, u32[]{:S(2)}, u32[]{:S(2)}) collective-permute-start(f32[128,2048]{1,0:T(8,128)} %constant_dynamic-slice_fusion.7), channel_id=1, source_target_pairs={{0,1},{1,0},{2,3},{3,2},{4,5},{5,4},{6,7},{7,6},{8,9},{9,8},{10,11... | collective-permute-start | bytes 3145736 | tf_op jit(solution)/shard_map/ppermute | solution.py:788
  316.7 5.9 %collective-permute-start.30 = (bf16[128,2048]{1,0:T(8,128)(2,1)S(1)}, bf16[128,2048]{1,0:T(8,128)(2,1)S(1)}, u32[]{:S(2)}, u32[]{:S(2)}) collective-permute-start(bf16[128,2048]{1,0:T(8,128)(2,1)S(1)} %fusion.42), channel_id=1, source_target_pairs={{0,1},{1,0},{2,3},{3,2},{4,5},{5,4},{6,7},{7,6},{8,9},{9,8},{10,11... | collective-permute-start | bytes 1572872 | tf_op jit(solution)/shard_map/ppermute | solution.py:788
  318.8 246.8 %collective-permute-start.15 = (bf16[128,2048]{1,0:T(8,128)(2,1)}, bf16[128,2048]{1,0:T(8,128)(2,1)}, u32[]{:S(2)}, u32[]{:S(2)}) collective-permute-start(bf16[128,2048]{1,0:T(8,128)(2,1)} %add_convert_fusion.7), channel_id=1, source_target_pairs={{0,2},{1,3},{64,66},{65,67},{2,0},{3,1},{66,64},{67,65},{4,6},{5,7... | collective-permute-start | bytes 1572872 | tf_op jit(solution)/shard_map/ppermute | solution.py:819
  321.2 244.3 %collective-permute-start.13 = (bf16[128,2048]{1,0:T(8,128)(2,1)}, bf16[128,2048]{1,0:T(8,128)(2,1)}, u32[]{:S(2)}, u32[]{:S(2)}) collective-permute-start(bf16[128,2048]{1,0:T(8,128)(2,1)} %add_convert_fusion.8), channel_id=1, source_target_pairs={{0,64},{1,65},{64,2},{65,3},{2,66},{3,67},{66,0},{67,1},{4,68},{5,... | collective-permute-start | bytes 1572872 | tf_op jit(solution)/shard_map/ppermute | solution.py:819
  442.9 9.1 %copy-start.32 = (f32[256,2048]{1,0:T(8,128)}, f32[256,2048]{1,0:T(8,128)S(1)}, u32[]{:S(2)}) copy-start(f32[256,2048]{1,0:T(8,128)S(1)} %fusion.17) | copy-start | bytes 6291460
  442.9 7.0 %copy-start.15 = (f32[256,2048]{1,0:T(8,128)S(1)}, f32[256,2048]{1,0:T(8,128)}, u32[]{:S(2)}) copy-start(f32[256,2048]{1,0:T(8,128)} %copy-done.14) | copy-start | bytes 6291460
  443.0 10.1 %copy-start.34 = (bf16[256,768]{1,0:T(8,128)(2,1)S(1)}, bf16[256,768]{1,0:T(8,128)(2,1)}, u32[]{:S(2)}) copy-start(bf16[256,768]{1,0:T(8,128)(2,1)} %convert_element_type.157) | copy-start | bytes 1179652
  444.1 16.9 %collective-permute-start.31 = (f32[128,2048]{1,0:T(8,128)}, f32[128,2048]{1,0:T(8,128)S(1)}, u32[]{:S(2)}, u32[]{:S(2)}) collective-permute-start(f32[128,2048]{1,0:T(8,128)} %constant_dynamic-slice_fusion), channel_id=1, source_target_pairs={{0,1},{1,0},{2,3},{3,2},{4,5},{5,4},{6,7},{7,6},{8,9},{9,8},{10,11... | collective-permute-start | bytes 3145736 | tf_op jit(solution)/shard_map/ppermute | solution.py:788
  452.1 113.5 %collective-permute-start.11 = (bf16[128,2048]{1,0:T(8,128)(2,1)}, bf16[128,2048]{1,0:T(8,128)(2,1)}, u32[]{:S(2)}, u32[]{:S(2)}) collective-permute-start(bf16[128,2048]{1,0:T(8,128)(2,1)} %add_convert_fusion.9), channel_id=1, source_target_pairs={{0,66},{1,67},{64,0},{65,1},{2,64},{3,65},{66,2},{67,3},{4,70},{5,... | collective-permute-start | bytes 1572872 | tf_op jit(solution)/shard_map/ppermute | solution.py:819
  556.5 9.0 %copy-start.6 = (f32[128,2048]{1,0:T(8,128)S(1)}, f32[128,2048]{1,0:T(8,128)}, u32[]{:S(2)}) copy-start(f32[128,2048]{1,0:T(8,128)} %copy-done.5) | copy-start | bytes 3145732
  556.5 9.0 %copy-start.20 = (bf16[1,128,2048]{2,1,0:T(8,128)(2,1)S(1)}, bf16[1,128,2048]{2,1,0:T(8,128)(2,1)}, u32[]{:S(2)}) copy-start(bf16[1,128,2048]{2,1,0:T(8,128)(2,1)} %param.17) | copy-start | bytes 1572868
  556.6 9.0 %copy-start.50 = (f32[128]{0:T(128)S(1)}, f32[128]{0:T(128)}, u32[]{:S(2)}) copy-start(f32[128]{0:T(128)} %copy-done.49) | copy-start | bytes 1540
  556.6 9.0 %copy-start.58 = (f32[128]{0:T(128)S(1)}, f32[128]{0:T(128)}, u32[]{:S(2)}) copy-start(f32[128]{0:T(128)} %copy-done.57) | copy-start | bytes 1540
  (49 other events, 158.3 us)

commit v3 on v2

--- a/solution.py
+++ b/solution.py
@@ -20,9 +20,7 @@
 SPAN = {"x": 4, "y": 4, "z": 4, "p": 2, "k": 2}
 GATHER_ORDERS = (("x", "y", "z"), ("y", "z", "x"), ("z", "x", "y"))
 SCATTER_ORDERS = (("z", "y", "x"), ("x", "z", "y"), ("y", "x", "z"))
-PLANE_DIMS = ("x", "y", "zh")
-PLANE_GATHER_ORDERS = (("x", "y"), ("y", "x"))
-PLANE_SCATTER_ORDERS = (("y", "x"), ("x", "y"))
+PLANE_AXES = ("x", "y")
 KEY_GATHER_ORDERS = (("p", "x", "y"), ("p", "y", "x"))
 KEY_SCATTER_ORDERS = (("y", "x", "p"), ("x", "y", "p"))
 
@@ -126,7 +124,7 @@
         pass
 
 
-def gather_lane(spot, wires, dims, order, parts, rows, always=()):
+def gather_lane(spot, wires, dims, order, parts, rows, always=(), direct=0):
     sent = []
     for phase, axis in enumerate(order):
         full = always + order[:phase]
@@ -136,12 +134,13 @@
             ref, columns = part
             return ref.at[spot.slab(dims, full, axis, value) + (pl.ds(first, count), columns)]
 
-        if SPAN[axis] == 2:
-            other = spot.turn(axis, 1)
+        if SPAN[axis] == 2 or phase < direct:
             copies = []
             for part in parts:
                 mine = slab(part, me, 0, rows)
-                copies.append(wires.remote(mine, mine, spot.device(axis, other)))
+                for by in range(1, SPAN[axis]):
+                    other = spot.device(axis, spot.turn(axis, by))
+                    copies.append(wires.remote(mine, mine, other))
             sent += start(copies)
             yield
             for copy in copies:
@@ -189,18 +188,18 @@
     return tuple(SIZES[dim] if axis_of(dim, dims) in full else 1 for dim in dims)
 
 
-def landing_shapes(dims, order, rows, width, always=()):
+def landing_shapes(dims, order, rows, width, always=(), direct=0):
     shapes = []
     for phase, axis in enumerate(order):
         lead = slab_shape(dims, always + order[phase + 1 :])
-        if SPAN[axis] == 2:
-            shapes.append(lead + (rows, width))
+        if SPAN[axis] == 2 or phase >= len(order) - direct:
+            shapes += [lead + (rows, width)] * (SPAN[axis] - 1)
         else:
             shapes += [lead + (rows // 2, width)] * 2 + [lead + (rows, width)] * 2
     return shapes
 
 
-def scatter_lane(spot, wires, dims, order, source, held, landing, final, rows, always=()):
+def scatter_lane(spot, wires, dims, order, source, held, landing, final, rows, always=(), direct=0):
     landing = list(landing)
     sent = []
     half = rows // 2
@@ -224,21 +223,25 @@
             )
 
         last = phase == len(order) - 1
-        if SPAN[axis] == 2:
-            other = spot.turn(axis, 1)
-            (whole,) = [landing.pop(0)]
-            copy = wires.remote(
-                origin.at[spot.slab(dims, full, axis, other)],
-                whole.at[flat],
-                spot.device(axis, other),
-            )
-            sent += start([copy])
+        if SPAN[axis] == 2 or phase >= len(order) - direct:
+            copies, arrived = [], []
+            for by in range(1, SPAN[axis]):
+                other = spot.turn(axis, by)
+                arrived.append(landing.pop(0))
+                copies.append(
+                    wires.remote(
+                        origin.at[spot.slab(dims, full, axis, other)],
+                        arrived[-1].at[flat],
+                        spot.device(axis, other),
+                    )
+                )
+            sent += start(copies)
             yield
             if phase == 0:
                 for load in loads:
                     load.wait()
-            copy.wait_recv()
-            arrived = [whole]
+            for copy in copies:
+                copy.wait_recv()
         else:
             right, left = spot.turn(axis, 1), spot.turn(axis, 3)
             across = origin.at[spot.slab(dims, full, axis, spot.turn(axis, 2))]
@@ -319,22 +322,32 @@
 
 def ffn_gather_lanes(spot, wires, sources, outs):
     rows = pl.ds(pl.multiple_of(spot.at["k"] * 16, 16), 16)
-    own = tuple(spot.at[dim] for dim in WEIGHT_DIMS) + (rows,)
-    remote, local = [], []
-    for source, out in zip(sources, outs):
-        for z, core, device in line_devices(spot):
-            columns = pl.ds(pl.multiple_of(line_columns(z, core), 128), 640)
-            remote.append(wires.remote(source.at[:, columns], out.at[own], device))
-        columns = pl.ds(pl.multiple_of(line_columns(spot.at["z"], spot.at["k"]), 128), 640)
-        local.append(wires.copy(source.at[:, columns], out.at[own]))
-    start(remote + local)
+    line = line_devices(spot)
+    wires_at = wires.remotes, wires.locals
+    for low, axis in enumerate(PLANE_AXES):
+        wires.remotes, wires.locals = wires_at
+        remote, local = [], []
+        for matrix, source in enumerate(sources):
+            target = outs[low].at[matrix, spot.at[axis], spot.at["zh"], rows]
+            for z, core, device in line:
+                columns = pl.ds(pl.multiple_of(line_columns(z, core), 128), 640)
+                remote.append(wires.remote(source.at[:, columns], target, device))
+            columns = pl.ds(pl.multiple_of(line_columns(spot.at["z"], spot.at["k"]), 128), 640)
+            local.append(wires.copy(source.at[:, columns], target))
+
+        @pl.when(spot.at["zl"] == low)
+        def _():
+            start(remote + local)
+
     yield
     for copy in remote + local:
         copy.wait()
     threads = [
-        gather_lane(spot, wires, PLANE_DIMS, order, [(out.at[low], pl.ds(0, 640))], 32, ("z",))
-        for out in outs
-        for low, order in enumerate(PLANE_GATHER_ORDERS)
+        gather_lane(
+            spot, wires, (axis, "zh"), (axis,), [(out.at[m], pl.ds(0, 640))], 32, ("z",)
+        )
+        for m in range(3)
+        for out, axis in zip(outs, PLANE_AXES)
     ]
     yield from in_turn(threads)
 
@@ -349,9 +362,9 @@
 
     count = len(widths)
     sources, ffn_in, (tokens,) = take(count), take(3), take(1)
-    outs, ffn_out, (tokens_all,) = take(count), take(3), take(1)
+    outs, ffn_out, (tokens_all,) = take(count), take(2), take(1)
     spot, wires = Spot(), Wires(*refs)
-    spot.greet((("x", (1, 3)), ("y", (1, 3))), [device for _, _, device in line_devices(spot)])
+    spot.greet((("x", RING), ("y", RING)), [device for _, _, device in line_devices(spot)])
     core = spot.at["k"]
     sibling = spot.device("k", 1 - core)
     rows = pl.ds(pl.multiple_of(core * 16, 16), 16)
@@ -371,7 +384,9 @@
     for copy in local + remote:
         copy.wait()
     threads = [
-        gather_lane(spot, wires, WEIGHT_DIMS, order, [(outs[at], pl.ds(first, wide))], 32)
+        gather_lane(
+            spot, wires, WEIGHT_DIMS, order, [(outs[at], pl.ds(first, wide))], 32, direct=2
+        )
         for number in range(count)
         for order, (at, first, wide) in zip(GATHER_ORDERS, [lane[number] for lane in lanes])
     ]
@@ -382,9 +397,9 @@
 def gather_weights(sources, ffn, tokens, lanes):
     widths = [source.shape[1] // 2 for source in sources]
     count = len(sources)
-    remotes = count + 1 + sum(len(parts) for parts in lanes) * 12 + 21 + 6 * 8
+    remotes = count + 1 + sum(len(parts) for parts in lanes) * 12 + 21 + 6 * 4
     out = [jax.ShapeDtypeStruct((2, 4, 4, 2, 32, width), BF16) for width in widths]
-    out += [jax.ShapeDtypeStruct((2, 4, 4, 2, 32, 640), BF16)] * 3
+    out += [jax.ShapeDtypeStruct((3, 4, 2, 32, 640), BF16)] * 2
     out += [jax.ShapeDtypeStruct((2,) + tokens.shape, tokens.dtype)]
     *gathered, tokens_all = pl.pallas_call(
         functools.partial(weight_gather_kernel, widths, lanes),
@@ -398,38 +413,79 @@
         ],
         compiler_params=pltpu.CompilerParams(collective_id=0, has_side_effects=True),
     )(*sources, *ffn, tokens)
-    return [g.reshape(2048, g.shape[-1]) for g in gathered], tokens_all
-
-
-def key_gather_kernel(source, out, send, recv, local):
+    return [g.reshape(2048, g.shape[-1]) for g in gathered[:count]], gathered[count:], tokens_all
+
+
+def line_gather(spot, wires, source, line):
+    sibling = spot.device("k", 1 - spot.at["k"])
+    half = source.shape[0] // 2
+    after, before = (spot.device("z", spot.turn("z", by)) for by in (1, 3))
+    copies = [
+        wires.copy(source, line.at[0, 0]),
+        wires.remote(source, line.at[0, 1], sibling),
+        wires.remote(source, line.at[1, 0], after),
+        wires.remote(source, line.at[2, 0], before),
+    ]
+    start(copies)
+    yield
+    later = []
+    for copy, slot, onward in ((copies[2], 1, after), (copies[3], 2, before)):
+        copy.wait_recv()
+        rows = pl.ds(half * (slot - 1), half)
+        later += start(
+            [
+                wires.remote(line.at[slot, 0, rows], line.at[3, 0, rows], onward),
+                wires.remote(line.at[slot, 0], line.at[slot, 1], sibling),
+            ]
+        )
+    yield
+    later[0].wait_recv()
+    later[2].wait_recv()
+    last = wires.remote(line.at[3, 0], line.at[3, 1], sibling)
+    start([last])
+    yield
+    copies[0].wait()
+    copies[1].wait()
+    copies[2].wait_send()
+    copies[3].wait_send()
+    for copy in (later[0], later[2]):
+        copy.wait_send()
+    for copy in (later[1], later[3], last):
+        copy.wait()
+
+
+def key_gather_kernel(source, cotangent, out, line, send, recv, local):
     spot, wires = Spot(), Wires(send, recv, local)
-    spot.greet((("x", (1, 3)), ("y", (1, 3)), ("p", (1,))))
+    spot.greet((("x", (1, 3)), ("y", (1, 3)), ("z", (1, 3)), ("k", (1,))))
     own = tuple(spot.at[dim] for dim in KEY_DIMS)
     copies = start([wires.copy(source.at[s], out.at[(s,) + own]) for s in range(2)])
     for copy in copies:
         copy.wait()
     whole = pl.ds(0, source.shape[-1])
-    run(
+    threads = [
         gather_lane(spot, wires, KEY_DIMS, order, [(out.at[s], whole)], source.shape[1])
         for s, order in enumerate(KEY_GATHER_ORDERS)
-    )
-
-
-def gather_keys(packed):
+    ]
+    run(threads + [line_gather(spot, wires, cotangent, line)])
+
+
+def gather_keys(packed, cotangent):
     _, rows, width = packed.shape
-    out = pl.pallas_call(
+    return pl.pallas_call(
         key_gather_kernel,
-        out_shape=jax.ShapeDtypeStruct((2, 2, 4, 4, rows, width), BF16),
-        in_specs=[ANY],
-        out_specs=ANY,
+        out_shape=[
+            jax.ShapeDtypeStruct((2, 2, 4, 4, rows, width), BF16),
+            jax.ShapeDtypeStruct((4, 2) + cotangent.shape, BF16),
+        ],
+        in_specs=[ANY] * 2,
+        out_specs=[ANY] * 2,
         scratch_shapes=[
-            pltpu.SemaphoreType.DMA((18,)),
-            pltpu.SemaphoreType.DMA((18,)),
-            pltpu.SemaphoreType.DMA((2,)),
+            pltpu.SemaphoreType.DMA((26,)),
+            pltpu.SemaphoreType.DMA((26,)),
+            pltpu.SemaphoreType.DMA((3,)),
         ],
         compiler_params=pltpu.CompilerParams(collective_id=1, has_side_effects=True),
-    )(packed)
-    return out
+    )(packed, cotangent)
 
 
 def key_scatter_kernel(source, out, *refs):
@@ -510,7 +566,7 @@
         return taken
 
     count = len(widths)
-    sources, ffn_in, (vector,) = take(count), take(3), take(1)
+    sources, ffn_in, (vector,) = take(count), take(2), take(1)
     outs, ffn_out, (vector_out,) = take(count), take(3), take(1)
     send, recv, local, slots = take(4)
     spot, wires = Spot(), Wires(send, recv, local)
@@ -525,11 +581,11 @@
     def part(lane, at, first, wide):
         order = SCATTER_ORDERS[lane]
         (held,) = take(1)
-        landing = take(len(landing_shapes(WEIGHT_DIMS, order, 32, wide)))
+        landing = take(len(landing_shapes(WEIGHT_DIMS, order, 32, wide, direct=2)))
         (final,) = take(1)
         source = sources[at].at[(slice(None),) * 5 + (pl.ds(first, wide),)]
         yield from scatter_lane(
-            spot, wires, WEIGHT_DIMS, order, source, held, landing, final, 32
+            spot, wires, WEIGHT_DIMS, order, source, held, landing, final, 32, direct=2
         )
         columns = pl.ds(pl.multiple_of(core * widths[at] + first, 128), wide)
         done = final.at[0, 0, 0, 0]
@@ -542,18 +598,18 @@
         for copy in copies:
             copy.wait()
 
-    def ffn(source, out):
+    def ffn(matrix, out):
         threads, finals = [], take(1)[0]
-        for low, order in enumerate(PLANE_SCATTER_ORDERS):
+        for low, axis in enumerate(PLANE_AXES):
             (held,) = take(1)
-            landing = take(len(landing_shapes(PLANE_DIMS, order, 32, 640, ("z",))))
+            landing = take(len(landing_shapes((axis, "zh"), (axis,), 32, 640, ("z",))))
             threads.append(
                 scatter_lane(
                     spot,
                     wires,
-                    PLANE_DIMS,
-                    order,
-                    source.at[low],
+                    (axis, "zh"),
+                    (axis,),
+                    ffn_in[low].at[matrix],
                     held,
                     landing,
                     finals.at[low],
@@ -577,7 +633,7 @@
         for span, columns in spans:
 
             def piece(z, k):
-                return finals.at[lax.rem(z, 2), 0, 0, lax.div(z, 2), half_rows(k), span]
+                return finals.at[lax.rem(z, 2), 0, lax.div(z, 2), half_rows(k), span]
 
             slot = out.at[:, columns]
             copies.append(wires.copy(piece(me, core), slot))
@@ -587,7 +643,7 @@
         for copy in copies:
             copy.wait()
 
-    threads = [ffn(source, out) for source, out in zip(ffn_in, ffn_out)]
+    threads = [ffn(matrix, out) for matrix, out in enumerate(ffn_out)]
     threads += [
         part(number, *parts) for chunk in zip(*lanes) for number, parts in enumerate(chunk)
     ]
@@ -596,25 +652,25 @@
 
 def scatter_weights(sources, ffn, vector, lanes):
     widths = [source.shape[1] for source in sources]
-    blocks = [g.reshape(2, 4, 4, 2, 32, g.shape[1]) for g in sources + ffn]
+    blocks = [g.reshape(2, 4, 4, 2, 32, g.shape[1]) for g in sources] + ffn
     parts = sum(len(lane) for lane in lanes)
-    remotes = 10 + 13 * parts + 3 * (16 + 14)
+    remotes = 10 + 13 * parts + 3 * (8 + 14)
     scratch = [
         pltpu.SemaphoreType.DMA((remotes,)),
         pltpu.SemaphoreType.DMA((remotes,)),
         pltpu.SemaphoreType.DMA((4 * parts + 24,)),
         pltpu.VMEM((4, 4) + vector.shape, F32),
     ]
-    for _ in ffn:
-        scratch.append(pltpu.VMEM((2, 1, 1, 2, 32, 640), F32))
-        for order in PLANE_SCATTER_ORDERS:
-            shapes = [(4, 4, 2, 32, 640)]
-            shapes += landing_shapes(PLANE_DIMS, order, 32, 640, ("z",))
+    for _ in range(3):
+        scratch.append(pltpu.VMEM((2, 1, 2, 32, 640), F32))
+        for axis in PLANE_AXES:
+            shapes = [(4, 2, 32, 640)]
+            shapes += landing_shapes((axis, "zh"), (axis,), 32, 640, ("z",))
             scratch += [pltpu.VMEM(shape, BF16) for shape in shapes]
     for chunk in zip(*lanes):
         for lane, (_, _, wide) in enumerate(chunk):
             shapes = [(2, 4, 4, 2, 32, wide)]
-            shapes += landing_shapes(WEIGHT_DIMS, SCATTER_ORDERS[lane], 32, wide)
+            shapes += landing_shapes(WEIGHT_DIMS, SCATTER_ORDERS[lane], 32, wide, direct=2)
             scratch += [pltpu.VMEM(shape, BF16) for shape in shapes]
             scratch.append(pltpu.VMEM((1, 1, 1, 1, 32, wide), F32))
     out = [jax.ShapeDtypeStruct((16, 2 * width), F32) for width in widths]
@@ -623,7 +679,7 @@
         functools.partial(weight_scatter_kernel, widths, lanes),
         out_shape=out + [jax.ShapeDtypeStruct(vector.shape, F32)],
         in_specs=[ANY] * len(blocks) + [IN_VMEM],
-        out_specs=[ANY] * len(blocks) + [IN_VMEM],
+        out_specs=[ANY] * len(out) + [IN_VMEM],
         scratch_shapes=scratch,
         compiler_params=pltpu.CompilerParams(
             collective_id=3, has_side_effects=True, vmem_limit_bytes=56 << 20
@@ -782,6 +838,181 @@
         scratch_shapes=[pltpu.VMEM((2, 128, 256), F32), pltpu.VMEM((16, 256, 128), F32)],
         compiler_params=pltpu.CompilerParams(vmem_limit_bytes=48 << 20),
     )(slots, low, block_map, kv, q, d, anchor, first, lse, delta)
+
+
+def ffn_kernel(*refs):
+    refs = list(refs)
+
+    def take(count):
+        taken = refs[:count]
+        del refs[:count]
+        return taken
+
+    pieces = [take(4), take(4)]
+    second, mask = take(2)
+    (cotangent_line,) = take(1)
+    (back_out, branch_out), branch_away, grads_out, first_out = take(2), take(3), take(2), take(2)
+    weights, line, cotangent, product, grads, own = take(6)
+    side_out, side_in, away_out, away_in = take(4)
+    spot, wires = Spot(), Wires(*refs)
+    core = spot.at["k"]
+    sibling = spot.device("k", 1 - core)
+    loads = []
+    for low, axis in enumerate(("y", "x")):
+        for step, piece in enumerate(pieces[low]):
+            place = lax.rem(spot.at[axis] + 4 - step + 2 * step * core, 4)
+            target = weights.at[:, 0, :, place] if low == 0 else weights.at[:, 1, place]
+            loads.append(wires.copy(piece, target))
+    loads.append(wires.copy(cotangent_line, cotangent))
+    start(loads)
+    spot.greet((("z", RING), ("k", (1,))))
+    beside = wires.remote(second, line.at[0, 1], sibling)
+    sent = [
+        wires.remote(second, line.at[slot, 0], spot.device("z", spot.turn("z", by)))
+        for slot, by in ((1, 1), (2, 3))
+    ]
+    start([beside] + sent)
+    line[0, 0] = second[...]
+    pending = [beside] + sent
+
+    def pass_on(slot, arrivals):
+        for copy in arrivals:
+            copy.wait_recv()
+        copies = [wires.remote(line.at[slot, 0], line.at[slot, 1], sibling)]
+        if slot < 3:
+            half = line.at[slot, 0, pl.ds(64 * (slot - 1), 64)]
+            target = line.at[3, 0, pl.ds(64 * (slot - 1), 64)]
+            onward = spot.device("z", spot.turn("z", (1, 3)[slot - 1]))
+            copies.append(wires.remote(half, target, onward))
+        pending.extend(start(copies))
+        return copies
+
+    def compute(slot):
+        rows = line[slot].reshape(256, 2048)
+        held = mask[...]
+        gate = contract(rows, weights[0].reshape(2048, 640), ((1,), (0,)))
+        upward = contract(rows, weights[1].reshape(2048, 640), ((1,), (0,))) * held
+        grad = contract(cotangent[slot].reshape(256, 2048), weights[2].reshape(2048, 640), ((1,), (0,))) * held
+        sigmoid = jax.nn.sigmoid(gate)
+        product[slot] = (gate * sigmoid * upward).astype(BF16)
+        grads[slot, :, :640] = (
+            grad * upward * sigmoid * (1.0 + gate * (1.0 - sigmoid))
+        ).astype(BF16)
+        grads[slot, :, 640:] = (grad * gate * sigmoid).astype(BF16)
+
+        def one(block, _):
+            low, place = lax.div(block, 4), lax.rem(block, 4)
+            columns = pl.ds(pl.multiple_of(block * 256, 256), 256)
+            tiles = [weights[m, low, place].reshape(256, 640) for m in range(3)]
+            back = contract(grads[slot, :, :640], tiles[0], ((1,), (1,))) + contract(
+                grads[slot, :, 640:], tiles[1], ((1,), (1,))
+            )
+            branch = contract(product[slot], tiles[2], ((1,), (1,)))
+            for number, value in enumerate((back, branch)):
+                own[slot % 2, number, :, columns] = value[:128]
+                side_out[slot, number, :, columns] = value[128:].astype(BF16)
+            return 0
+
+        lax.fori_loop(0, 8, one, 0, unroll=2)
+        copies = [
+            wires.remote(side_out.at[slot, number], side_in.at[slot, number], sibling)
+            for number in range(2)
+        ]
+        pending.extend(start(copies))
+        return copies
+
+    returns = []
+
+    def finish(slot, copies):
+        for number, copy in enumerate(copies):
+            copy.wait_recv()
+            total = own[slot % 2, number] + side_in[slot, number].astype(F32)
+            if slot == 0:
+                (back_out, branch_out)[number][...] = total
+            elif number == 1:
+                branch_away[slot - 1][...] = total.astype(BF16)
+            else:
+                away_out[slot - 1] = total.astype(BF16)
+                owner = spot.device("z", spot.turn("z", (3, 1, 2)[slot - 1]))
+                copy = wires.remote(away_out.at[slot - 1], away_in.at[slot - 1], owner)
+                returns.extend(start([copy]))
+
+    for copy in loads:
+        copy.wait()
+    beside.wait_recv()
+    first = compute(0)
+    one, two = pass_on(1, sent[:1]), pass_on(2, sent[1:])
+    finish(0, first)
+    one[0].wait_recv()
+    first = compute(1)
+    (three,) = pass_on(3, [one[1], two[1]])
+    two[0].wait_recv()
+    latest = compute(2)
+    finish(1, first)
+    three.wait_recv()
+    first = compute(3)
+    finish(2, latest)
+    finish(3, first)
+
+    for low in range(2):
+
+        def outer(place, _):
+            columns = pl.ds(pl.multiple_of((low * 4 + place) * 256, 256), 256)
+            rows = line[:, :, :, columns].reshape(1024, 256)
+            both = contract(rows, grads[...].reshape(1024, 1280), ((0,), (0,))).astype(BF16)
+            grads_out[low][0, place] = both[:, :640].reshape(4, 2, 32, 640)
+            grads_out[low][1, place] = both[:, 640:].reshape(4, 2, 32, 640)
+            rows = cotangent[:, :, :, columns].reshape(1024, 256)
+            down = contract(rows, product[...].reshape(1024, 640), ((0,), (0,))).astype(BF16)
+            grads_out[low][2, place] = down.reshape(4, 2, 32, 640)
+            return 0
+
+        lax.fori_loop(0, 4, outer, 0)
+    firsts = []
+    for low, axis in enumerate(("y", "x")):
+        place = lax.rem(spot.at[axis] + 3 + 2 * core, 4)
+        slab = grads_out[low].at[:, :, place] if low == 0 else grads_out[low].at[:, place]
+        firsts.append(wires.copy(slab, first_out[low]))
+    start(firsts)
+    for slot, copy in enumerate(returns):
+        copy.wait_recv()
+        back_out[...] += away_in[slot].astype(F32)
+    for copy in pending + returns:
+        copy.wait_send()
+    for copy in firsts:
+        copy.wait()
+
+
+def feed_forward(pieces, second, mask, cotangent_line):
+    grads = jax.ShapeDtypeStruct((3, 4, 4, 2, 32, 640), BF16)
+    rows = jax.ShapeDtypeStruct((128, 2048), F32)
+    return pl.pallas_call(
+        ffn_kernel,
+        out_shape=[rows] * 2
+        + [jax.ShapeDtypeStruct((128, 2048), BF16)] * 3
+        + [grads] * 2
+        + [jax.ShapeDtypeStruct((3, 4, 2, 32, 640), BF16)] * 2,
+        in_specs=[ANY] * 8 + [IN_VMEM] * 2 + [ANY],
+        out_specs=[IN_VMEM] * 7 + [ANY] * 2,
+        scratch_shapes=[
+            pltpu.VMEM((3, 2, 4, 4, 2, 32, 640), BF16),
+            pltpu.VMEM((4, 2, 128, 2048), BF16),
+            pltpu.VMEM((4, 2, 128, 2048), BF16),
+            pltpu.VMEM((4, 256, 640), BF16),
+            pltpu.VMEM((4, 256, 1280), BF16),
+            pltpu.VMEM((2, 2, 128, 2048), F32),
+            pltpu.VMEM((4, 2, 128, 2048), BF16),
+            pltpu.VMEM((4, 2, 128, 2048), BF16),
+            pltpu.VMEM((3, 128, 2048), BF16),
+            pltpu.VMEM((3, 128, 2048), BF16),
+            pltpu.SemaphoreType.DMA((19,)),
+            pltpu.SemaphoreType.DMA((19,)),
+            pltpu.SemaphoreType.DMA((11,)),
+        ],
+        compiler_params=pltpu.CompilerParams(
+            collective_id=4, has_side_effects=True, vmem_limit_bytes=62 << 20
+        ),
+    )(*pieces[0], *pieces[1], second, mask, cotangent_line)
 
 
 def swap(array):
@@ -822,18 +1053,26 @@
 FAR = (1, 3, 2)
 
 
-def spread(array, core):
-    far = [along_z(array, by) for by in FAR]
-    return share(array, core), jnp.concatenate([share(rows, core) for rows in far], axis=0)
-
-
-def collect(partials, core):
-    near, far = partials
-    own = total_rows(near, core)
-    for number, by in enumerate(FAR):
-        rows = total_rows(far[number * 256 : (number + 1) * 256], core).astype(BF16)
-        own = own + along_z(rows, 4 - by).astype(F32)
-    return own
+def round_ring(array, axis):
+    pairs = []
+    for ctx in range(32):
+        low, x, y = ctx // 16, ctx // 4 % 4, ctx % 4
+        for wt in range(4):
+            by = 1 if wt % 2 == 0 else 3
+            to_x, to_y = ((x + by) % 4, y) if axis == "x" else (x, (y + by) % 4)
+            pairs.append((ctx * 4 + wt, (low * 16 + to_x * 4 + to_y) * 4 + wt))
+    return lax.ppermute(array, ("ctx", "wt"), pairs)
+
+
+RING_AXES = ("y", "x")
+
+
+def ring_total_step(arrived, grads, lane, step, core):
+    ctx = lax.axis_index("ctx")
+    me = lax.rem(ctx, 4) if lane == 0 else lax.rem(lax.div(ctx, 4), 4)
+    place = lax.rem(me + 4 - step + 2 * step * core, 4)
+    slab = lax.dynamic_index_in_dim(grads, place, 2 - lane, keepdims=False)
+    return (arrived.astype(F32) + slab.astype(F32)).astype(BF16)
 
 
 def norm_forward(values, gain):
@@ -859,10 +1098,6 @@
 
 def unrotate(grads, cosine, sine):
     return rotate(grads, cosine, -sine)
-
-
-def halves(array):
-    return array.reshape(array.shape[0], 2, array.shape[1] // 2)
 
 
 def to_blocks(heads):
@@ -897,13 +1132,16 @@
 ):
     core = lax.rem(lax.axis_index("wt"), 2)
     ctx = lax.axis_index("ctx")
-    kv_halves = jnp.stack(
-        [key_weight.reshape(16, 2, 3, 64), value_weight.reshape(16, 2, 3, 64)], axis=3
-    ).reshape(16, 2, 384)
-    qkv_pack = jnp.concatenate([halves(query_weight), kv_halves], axis=2).reshape(16, 2304)
+    qkv_pack = jnp.concatenate(
+        [
+            weight[:, half * width : (half + 1) * width]
+            for half in range(2)
+            for weight, width in ((query_weight, 768), (key_weight, 192), (value_weight, 192))
+        ],
+        axis=1,
+    )
     lanes = [[(0, lane * 384, 384), (1, lane * 256, 256)] for lane in range(3)]
-    grad_out_line = spread(cotangent[0], core)
-    (qkv_w, out_w, gate_w, up_w, down_w), tokens_all = gather_weights(
+    (qkv_w, out_w), ffn_first, tokens_all = gather_weights(
         [qkv_pack, out_weight], [gate_weight, up_weight, down_weight], tokens[0], lanes
     )
     rows = tokens[0].astype(F32)
@@ -941,55 +1179,54 @@
         qkv_pre[:, :768].reshape(256, 12, 64), query_gain
     )
     query_low = rotate(query_normed, cosine, sine).astype(BF16)
-    kv_pre = qkv_pre[:, 768:].reshape(256, 3, 2, 64)
-    key_normed, key_hat, key_inv = norm_forward(kv_pre[:, :, 0], key_gain)
+    key_normed, key_hat, key_inv = norm_forward(qkv_pre[:, 768:960].reshape(256, 3, 64), key_gain)
     key_low = rotate(key_normed, cosine, sine).astype(BF16)
-    kv_low = jnp.stack([key_low, kv_pre[:, :, 1].astype(BF16)], axis=2)
-    kv_all = gather_keys(kv_low.reshape(2, 128, 384))
+    value_low = qkv_pre[:, 960:].astype(BF16).reshape(256, 3, 64)
+    kv_low = jnp.concatenate([key_low, value_low], axis=2)
+    pieces = [[lane] for lane in ffn_first]
+
+    def next_pieces(*after):
+        moved = [round_ring(lane[-1], axis) for lane, axis in zip(pieces, RING_AXES)]
+        *moved, after = lax.optimization_barrier((*moved, after))
+        for lane, piece in zip(pieces, moved):
+            lane.append(piece)
+        return after
+
+    (kv_low,) = next_pieces(kv_low)
+    kv_all, grad_out_line = gather_keys(kv_low.reshape(2, 128, 384), cotangent[0])
     query_blocks = jnp.pad(
         to_blocks(query_low * jnp.asarray(0.125, BF16)), ((0, 0),) * 4 + ((0, 64),)
     )
     attended, lse = attention(slots, low_block, kv_all, query_blocks, anchor_rows, start_rows)
+    (attended,) = next_pieces(attended)
     attended = from_blocks(attended)
     merged = attended.reshape(256, 768).astype(BF16)
     mixed = rows + total_rows(contract(merged, out_w, ((1,), (1,))), core)
 
     second_out, second_hat, second_inv = norm_forward(mixed, second_gain)
-    second_line = spread(second_out.astype(BF16), core)
+    second_low = second_out.astype(BF16)
+    (second_low,) = next_pieces(second_low)
     z = lax.div(lax.axis_index("wt"), 2) * 2 + lax.div(ctx, 16)
     unit = jnp.arange(640, dtype=jnp.int32)
     held = jnp.where((z == 3) & (unit < 128), 0.0, 1.0).astype(F32)[None, :]
-    gate_w, up_w, down_w = (w.reshape(2048, 640) for w in (gate_w, up_w, down_w))
-
-    def feed_forward(second, grad_out):
-        gate = jnp.dot(second, gate_w, preferred_element_type=F32)
-        upward = jnp.dot(second, up_w, preferred_element_type=F32) * held
-        grad_product = jnp.dot(grad_out, down_w, preferred_element_type=F32) * held
-        sigmoid = jax.nn.sigmoid(gate)
-        product = (gate * sigmoid * upward).astype(BF16)
-        grad_gate = (
-            grad_product * upward * sigmoid * (1.0 + gate * (1.0 - sigmoid))
-        ).astype(BF16)
-        grad_upward = (grad_product * gate * sigmoid).astype(BF16)
-        grad_second = contract(grad_gate, gate_w, ((1,), (1,))) + contract(
-            grad_upward, up_w, ((1,), (1,))
-        )
-        branch = contract(product, down_w, ((1,), (1,)))
-        return product, grad_gate, grad_upward, branch, grad_second
-
-    results = [feed_forward(*pair) for pair in zip(second_line, grad_out_line)]
-    grad_second = collect([result[4] for result in results], core)
-    activations = (mixed + collect([result[3] for result in results], core)).astype(BF16)[None]
+    grad_second, branch, *rest = feed_forward(pieces, second_low, held, grad_out_line)
+    branch_away, ffn_grads, running = rest[:3], rest[3:5], rest[5:]
+    for part, by in zip(branch_away, FAR):
+        branch = branch + along_z(part, 4 - by).astype(F32)
+    activations = (mixed + branch).astype(BF16)[None]
+
+    def next_running(step, *after):
+        moved = [round_ring(part, axis) for part, axis in zip(running, RING_AXES)]
+        *moved, after = lax.optimization_barrier((*moved, after))
+        running[:] = [
+            ring_total_step(part, g, lane, step, core)
+            for lane, (part, g) in enumerate(zip(moved, ffn_grads))
+        ]
+        return after
 
     def outer(left, right):
         return contract(left, right, ((0,), (0,)))
 
-    def outer_line(left, right):
-        return sum(outer(*pair) for pair in zip(left, right)).astype(BF16)
-
-    gate_g = outer_line(second_line, [result[1] for result in results])
-    up_g = outer_line(second_line, [result[2] for result in results])
-    down_g = outer_line(grad_out_line, [result[0] for result in results])
     second_back, second_terms = norm_backward(grad_second, second_gain, second_hat, second_inv)
     grad_mixed = cotangent[0].astype(F32) + second_back
     grad_branch = share(grad_mixed.astype(BF16), core)
@@ -998,6 +1235,7 @@
     delta = jnp.sum(grad_heads.astype(F32) * attended, axis=-1, keepdims=True)
     delta_rows = to_blocks(delta).reshape(2, 3, 2, 1, 256)
     grad_blocks = jnp.pad(to_blocks(grad_heads), ((0, 0),) * 4 + ((64, 0),))
+    (grad_blocks,) = next_running(2, grad_blocks)
     grad_query_tall, grad_kv = attention_back(
         slots,
         low_block,
@@ -1010,13 +1248,20 @@
         lse,
         delta_rows,
     )
-    own_kv = scatter_keys(grad_kv).reshape(256, 3, 2, 64)
+    (grad_kv,) = next_running(3, grad_kv)
+    own_kv = scatter_keys(grad_kv).reshape(256, 3, 128)
     query_unrot = unrotate(from_blocks(grad_query_tall) * 0.125, cosine, sine)
     query_back, query_terms = norm_backward(query_unrot, query_gain, query_hat, query_inv)
-    key_unrot = unrotate(own_kv[:, :, 0], cosine, sine)
+    key_unrot = unrotate(own_kv[:, :, :64], cosine, sine)
     key_back, key_terms = norm_backward(key_unrot, key_gain, key_hat, key_inv)
-    grad_kv_low = jnp.stack([key_back, own_kv[:, :, 1]], axis=2).reshape(256, 384)
-    grad_qkv = jnp.concatenate([query_back.reshape(256, 768), grad_kv_low], axis=1).astype(BF16)
+    grad_qkv = jnp.concatenate(
+        [
+            query_back.reshape(256, 768),
+            key_back.reshape(256, 192),
+            own_kv[:, :, 64:].reshape(256, 192),
+        ],
+        axis=1,
+    ).astype(BF16)
     grad_first = total_rows(contract(grad_qkv, qkv_w, ((1,), (1,))), core)
     first_back, first_terms = norm_backward(grad_first, first_gain, first_hat, first_inv)
     token_grad = (grad_mixed + first_back).astype(BF16)[None]
@@ -1030,20 +1275,21 @@
             jnp.zeros((896,), F32),
         ]
     ).reshape(8, 640)
+    (gains,) = next_running(4, gains)
     qkv_g, out_g, gate_g, up_g, down_g, gains = scatter_weights(
         [
             outer(first_low, grad_qkv).astype(BF16),
             outer(grad_branch, merged).astype(BF16),
         ],
-        [gate_g, up_g, down_g],
+        running,
         gains,
         lanes,
     )
     gains = gains.reshape(5120)
-    qkv_g = qkv_g.reshape(16, 2, 1152)
-    query_g = qkv_g[:, :, :768].reshape(16, 1536)
-    kv_g = qkv_g[:, :, 768:].reshape(16, 2, 3, 2, 64)
-    key_g, value_g = kv_g[:, :, :, 0].reshape(16, 384), kv_g[:, :, :, 1].reshape(16, 384)
+    query_g, key_g, value_g = (
+        jnp.concatenate([qkv_g[:, first : first + wide], qkv_g[:, 1152 + first : 1152 + first + wide]], axis=1)
+        for first, wide in ((0, 768), (768, 192), (960, 192))
+    )
 
     def whole_rows(pieces):
         return jnp.concatenate([pieces[:, :2432], pieces[:, 2560:4992]], axis=1)

time: 580 us -> 528 us (0.910)
  matrix products: 61.3 us -> 18.2 us
  Pallas kernels: 336 us -> 357 us
  local copies, waits for them, and re-layouts: 64.3 us -> 45.5 us
  starting transfers between devices: 41.8 us -> 25.7 us
    pallas_call x1 -> x2, Pallas kernels: 46.2 us -> 126 us  [the longest x1 67.1 us: feed_forward(): pl.pallas_call(ffn_kernel, out_shape=[rows] * 2 + [jax.ShapeDtypeStruct((...]
    pallas_call x1, Pallas kernels: 92.5 us -> 59 us  [scatter_weights(): pl.pallas_call(functools.partial(weight_scatter_kernel, widths, lanes), o...]
    dot_general x16 -> x4, matrix products: 42.6 us -> 13.3 us  [contract(): lax.dot_general(left, right, (dims, ((), ())), preferred_element_type=F32)]
    pallas_call x1, Pallas kernels: 96 us -> 68 us  [gather_weights(): pl.pallas_call(functools.partial(weight_gather_kernel, widths, lanes), ou...]
    ppermute x12 -> x3, starting transfers between devices: 22.1 us -> 0.01 us  [along_z(): return lax.ppermute(array, ('ctx', 'wt'), pairs)]
    ppermute x0 -> x12, waiting for transfers between devices: none -> 20.9 us  [round_ring(): return lax.ppermute(array, ('ctx', 'wt'), pairs)]
    ppermute x12 -> x3, waiting for transfers between devices: 19 us -> 0.01 us  [along_z(): return lax.ppermute(array, ('ctx', 'wt'), pairs)]
    ppermute x0 -> x12, starting transfers between devices: none -> 17.7 us  [round_ring(): return lax.ppermute(array, ('ctx', 'wt'), pairs)]
  transfers between devices with their start and end apart: 32 -> 19, of which waited for: 5 -> 7; matrix products, arithmetic and copies ran while one was open for 28% -> 17% of each run, Pallas kernels for 59% -> 43%
where the time goes in v3:
time: 528 us; the launch traced here: 520 us
  Pallas kernels  357 us (68%)
  other arithmetic  50.4 us (10%)
  local copies, waits for them, and re-layouts  45.5 us (9%)
  starting transfers between devices  25.7 us (5%)
  waiting for transfers between devices  20.9 us (4%)
  matrix products  18.2 us (3%)
    pallas_call x1, Pallas kernels, gather_weights(): pl.pallas_call(functools.partial(weight_gather_kernel, widths, lanes), ou...  68 us
    pallas_call x1, Pallas kernels, feed_forward(): pl.pallas_call(ffn_kernel, out_shape=[rows] * 2 + [jax.ShapeDtypeStruct((...  67.1 us
    pallas_call x1, Pallas kernels, scatter_weights(): pl.pallas_call(functools.partial(weight_scatter_kernel, widths, lanes), o...  59 us
    pallas_call x1, Pallas kernels, gather_keys(): pl.pallas_call(key_gather_kernel, out_shape=[jax.ShapeDtypeStruct((2, 2,...  58.9 us
    pallas_call x1, Pallas kernels, scatter_keys(): pl.pallas_call(key_scatter_kernel, out_shape=jax.ShapeDtypeStruct((2, 1,...  43.7 us
    pallas_call x1, Pallas kernels, attention_back(): pl.pallas_call(attention_back_kernel, in_specs=[IN_SMEM] * 3 + [IN_VMEM]...  43.4 us
    ppermute x12, waiting for transfers between devices, round_ring(): return lax.ppermute(array, ('ctx', 'wt'), pairs)  20.9 us
    ppermute x12, starting transfers between devices, round_ring(): return lax.ppermute(array, ('ctx', 'wt'), pairs)  17.7 us
  transfers between devices with their start and end apart: 19, of which 7 were waited for; matrix products, arithmetic and copies ran while one was open for 17% of the time, Pallas kernels for 43%

profile of v3, /device:TPU:1, one launch (start us, length us, event | category | flops | bytes accessed | tf_op | source)
XLA Modules:
  0.0 519.7 jit_solution(3803711136891074443)
XLA Ops:
  3.0 68.0 %shard_map.255 = (bf16[2,4,4,2,32,1152]{5,4,3,2,1,0:T(8,128)(2,1)}, bf16[2,4,4,2,32,768]{5,4,3,2,1,0:T(8,128)(2,1)}, bf16[3,4,2,32,640]{4,3,2,1,0:T(8,128)(2,1)}...) custom-call(bf16[16,2304]{1,0:T(8,128)(2,1)} %concatenate.59.refs_0_, bf16[16,1536]{1,0:T(8,128)(2,1)} %refs_1_.1, ...), custom_call_target="tpu_custom_call" | custom-call | tf_op jit(solution)/shard_map/pallas_call | solution.py:404
  71.0 2.8 collective-permute-start
  77.8 1.5 multiply_reduce_fusion
  79.4 1.5 multiply_convert_fusion
  80.9 3.9 fusion.42
  87.4 2.1 collective-permute-start.3
  89.5 1.5 collective-permute-start.4
  95.4 58.9 %shard_map.256 = (bf16[2,2,4,4,128,384]{5,4,3,2,1,0:T(8,128)(2,1)}, bf16[4,2,128,2048]{3,2,1,0:T(8,128)(2,1)}) custom-call(bf16[2,128,384]{2,1,0:T(8,128)(2,1)} %copy.119.source, bf16[128,2048]{1,0:T(8,128)(2,1)} %bitcast.134), custom_call_target="tpu_custom_call" | custom-call | tf_op jit(solution)/shard_map/pallas_call | solution.py:474
  154.3 2.8 copy-done
  157.1 16.9 %shard_map.257 = (f32[2,3,2,64,256]{4,3,2,1,0:T(8,128)S(1)}, f32[2,3,2,1,256]{4,3,2,1,0:T(1,128)S(1)}) custom-call(s32[64]{0:T(128)S(1)} %select_reduce_fusion.1.slot_ref, s32[1]{0:T(128)S(1)} %bitcast.122, bf16[2,2,4,4,128,384]{5,4,3,2,1,0:T(8,128)(2,1)S(1)} %copy-done, bf16[2,3,2,256,128]{4,3,2,1,0:T(8,128)(2,1)S(1)} %pad.8.q_ref, ...), custom_call_target="tpu_custom_call" | custom-call | tf_op jit(solution)/shard_map/pallas_call | solution.py:755
  174.0 1.9 reshape.349
  175.9 2.6 copy.122
  178.5 1.7 bitcast_convert_fusion
  181.3 2.9 fusion.43
  184.3 1.3 copy-done.8
  185.7 2.7 collective-permute-start.5
  190.4 2.3 collective-permute-start.6
  193.1 1.9 multiply_reduce_fusion.3
  195.9 8.1 %collective-permute-done.6.refs_3_ = bf16[3,4,2,32,640]{4,3,2,1,0:T(8,128)(2,1)} collective-permute-done((bf16[3,4,2,32,640]{4,3,2,1,0:T(8,128)(2,1)}, bf16[3,4,2,32,640]{4,3,2,1,0:T(8,128)(2,1)}, u32[]{:S(2)}, u32[]{:S(2)}) %collective-permute-start.6) | collective-permute-done | bytes 983072 | tf_op jit(solution)/shard_map/ppermute | solution.py:1064
  204.0 2.2 collective-permute-done.7.refs_7_
  206.2 67.1 %shard_map.258 = (f32[128,2048]{1,0:T(8,128)}, f32[128,2048]{1,0:T(8,128)}, bf16[128,2048]{1,0:T(8,128)(2,1)}, bf16[128,2048]{1,0:T(8,128)(2,1)}, bf16[128,2048]...) custom-call(bf16[3,4,2,32,640]{4,3,2,1,0:T(8,128)(2,1)} %get-tuple-e, ...), custom_call_target="tpu_custom_call" | custom-call | tf_op jit(solution)/shard_map/pallas_call | solution.py:989
  273.4 1.7 multiply_reduce_fusion.1
  278.4 1.9 collective-permute-start.12
  286.4 4.8 collective-permute-done.11
  292.4 43.4 %shard_map.259 = (f32[2,3,2,64,256]{4,3,2,1,0:T(8,128)S(1)}, bf16[2,2,4,4,128,384]{5,4,3,2,1,0:T(8,128)(2,1)}) custom-call(s32[64]{0:T(128)S(1)} %select_reduce_fusion.1.slot_ref, s32[1]{0:T(128)S(1)} %bitcast.123, s32[64]{0:T(128)S(1)} %copy-done.1, bf16[2,2,4,4,128,384]{5,4,3,2,1,0:T(8,128)(2,1)} %get-tuple-element.64.kv, ...), custom_call_target="tpu_custom_call" | custom-call | tf_op jit(solution)/shard_map/pallas_call | solution.py:830
  336.7 1.9 mul.496
  338.6 2.4 copy.154
  341.0 2.6 mul.498
  343.6 2.7 fusion.7
  346.4 1.4 collective-permute-start.14
  347.8 2.9 fusion.6
  353.1 2.4 copy.126
  356.4 2.3 copy.128
  358.7 2.4 multiply_reduce_fusion.4
  361.1 3.1 collective-permute-done.15
  364.2 43.7 %shard_map.260 = f32[2,1,1,1,128,384]{5,4,3,2,1,0:T(8,128)S(1)} custom-call(bf16[2,2,4,4,128,384]{5,4,3,2,1,0:T(8,128)(2,1)} %get-tuple-element.89.source), custom_call_target="tpu_custom_call" | custom-call | tf_op jit(solution)/shard_map/pallas_call | solution.py:520
  409.6 3.9 fusion.44
  414.7 4.8 collective-permute-start.16
  419.5 2.7 fusion.5
  422.3 2.8 fusion.4
  425.1 3.0 collective-permute-start.18
  428.1 2.8 convolution_convert_fusion.1
  431.3 3.7 convolution_convert_fusion
  435.0 2.6 fusion.17
  439.5 2.8 fusion.3.refs_2_
  442.2 2.7 fusion.2.refs_3_
  445.0 59.0 %shard_map.261 = (f32[16,2304]{1,0:T(8,128)}, f32[16,1536]{1,0:T(8,128)}, f32[16,5120]{1,0:T(8,128)}, f32[16,5120]{1,0:T(8,128)}, f32[16,5120]{1,0:T(8,128)}, /*index=5*/f32[8,640]{1,0:T(8,128)}) custom-call(bf16[2,4,4,2,32,1152]{5,4,3,2,1,0:T(8,128)(2,1)} %bitcast.124, bf16[2,4,4,2,32,768]{5,4,3,2,1,0:T(8,128)(2,1)} %bitcast.142, ...), custom_call_target="tpu_custom_call" | custom-call | tf_op jit(solution)/shard_map/pallas_call | solution.py:678
  515.1 3.5 fusion.21
  (207 shorter events, 49.4 us)
Async XLA Ops:
  0.6 78.7 %copy-start.33 = (f32[2048]{0:T(1024)S(1)}, f32[2048]{0:T(1024)}, u32[]{:S(2)}) copy-start(f32[2048]{0:T(1024)} %param.21) | copy-start | bytes 24580
  71.0 16.1 %collective-permute-start = (bf16[3,4,2,32,640]{4,3,2,1,0:T(8,128)(2,1)}, bf16[3,4,2,32,640]{4,3,2,1,0:T(8,128)(2,1)}, u32[]{:S(2)}, u32[]{:S(2)}) collective-permute-start(bf16[3,4,2,32,640]{4,3,2,1,0:T(8,128)(2,1)} %get-tuple-element.57.refs_0_), channel_id=1, source_target_pairs={{0,4},{1,13},{2,6},{3,15},{4,8},{5,1},{6,10},{7,3},{8,12},{9,5},{1... | collective-permute-start | bytes 2949128 | tf_op jit(solution)/shard_map/ppermute | solution.py:1064
  73.8 13.6 %collective-permute-start.1 = (bf16[3,4,2,32,640]{4,3,2,1,0:T(8,128)(2,1)}, bf16[3,4,2,32,640]{4,3,2,1,0:T(8,128)(2,1)}, u32[]{:S(2)}, u32[]{:S(2)}) collective-permute-start(bf16[3,4,2,32,640]{4,3,2,1,0:T(8,128)(2,1)} %get-tuple-element.58.refs_4_), channel_id=1, source_target_pairs={{0,16},{1,49},{2,18},{3,51},{4,20},{5,53},{6,22},{7,55},{8,24},{9,... | collective-permute-start | bytes 2949128 | tf_op jit(solution)/shard_map/ppermute | solution.py:1064
  77.8 8.9 %collective-permute-start.2 = (s32[1,2,128]{2,1,0:T(2,128)S(1)}, s32[1,2,128]{2,1,0:T(2,128)S(1)}, u32[]{:S(2)}, u32[]{:S(2)}) collective-permute-start(s32[1,2,128]{2,1,0:T(2,128)S(1)} %add_bitcast_fusion), channel_id=1, source_target_pairs={{0,1},{1,0},{2,3},{3,2},{4,5},{5,4},{6,7},{7,6},{8,9},{9,8},{10,11... | collective-permute-start | bytes 3080 | tf_op jit(solution)/shard_map/ppermute | solution.py:1019
  86.0 5.3 %copy-start.14 = (f32[256,192]{0,1:T(8,128)}, f32[256,192]{0,1:T(8,128)S(1)}, u32[]{:S(2)}) copy-start(f32[256,192]{0,1:T(8,128)S(1)} %copy.140) | copy-start | bytes 589828
  86.0 4.9 copy-start.1
  86.0 5.0 copy-start.37
  86.4 5.0 copy-start.3
  87.4 86.6 %collective-permute-start.3 = (bf16[3,4,2,32,640]{4,3,2,1,0:T(8,128)(2,1)}, bf16[3,4,2,32,640]{4,3,2,1,0:T(8,128)(2,1)}, u32[]{:S(2)}, u32[]{:S(2)}) collective-permute-start(bf16[3,4,2,32,640]{4,3,2,1,0:T(8,128)(2,1)} %collective-permute-done.refs_1_), channel_id=1, source_target_pairs={{0,4},{1,13},{2,6},{3,15},{4,8},{5,1},{6,10},{7,3},{8,12},{9,5},{1... | collective-permute-start | bytes 2949128 | tf_op jit(solution)/shard_map/ppermute | solution.py:1064
  89.5 84.5 %collective-permute-start.4 = (bf16[3,4,2,32,640]{4,3,2,1,0:T(8,128)(2,1)}, bf16[3,4,2,32,640]{4,3,2,1,0:T(8,128)(2,1)}, u32[]{:S(2)}, u32[]{:S(2)}) collective-permute-start(bf16[3,4,2,32,640]{4,3,2,1,0:T(8,128)(2,1)} %collective-permute-done.1.refs_5_), channel_id=1, source_target_pairs={{0,16},{1,49},{2,18},{3,51},{4,20},{5,53},{6,22},{7,55},{8,24},{9,... | collective-permute-start | bytes 2949128 | tf_op jit(solution)/shard_map/ppermute | solution.py:1064
  154.3 2.8 copy-start
  184.2 1.3 copy-start.8
  185.6 7.5 %copy-start.9 = (bf16[1,128,2048]{2,1,0:T(8,128)(2,1)S(1)}, bf16[1,128,2048]{2,1,0:T(8,128)(2,1)}, u32[]{:S(2)}) copy-start(bf16[1,128,2048]{2,1,0:T(8,128)(2,1)} %param.16) | copy-start | bytes 1572868
  185.7 7.4 %collective-permute-start.5 = (f32[128,2048]{1,0:T(8,128)S(1)}, f32[128,2048]{1,0:T(8,128)}, u32[]{:S(2)}, u32[]{:S(2)}) collective-permute-start(f32[128,2048]{1,0:T(8,128)S(1)} %constant_dynamic-slice_fusion.1), channel_id=1, source_target_pairs={{0,1},{1,0},{2,3},{3,2},{4,5},{5,4},{6,7},{7,6},{8,9},{9,8},{10,11... | collective-permute-start | bytes 3145736 | tf_op jit(solution)/shard_map/ppermute | solution.py:1019
  189.6 5.3 %copy-start.34 = (f32[2048]{0:T(1024)S(1)}, f32[2048]{0:T(1024)}, u32[]{:S(2)}) copy-start(f32[2048]{0:T(1024)} %param.28) | copy-start | bytes 24580
  190.4 13.6 %collective-permute-start.6 = (bf16[3,4,2,32,640]{4,3,2,1,0:T(8,128)(2,1)}, bf16[3,4,2,32,640]{4,3,2,1,0:T(8,128)(2,1)}, u32[]{:S(2)}, u32[]{:S(2)}) collective-permute-start(bf16[3,4,2,32,640]{4,3,2,1,0:T(8,128)(2,1)} %collective-permute-done.3.refs_2_), channel_id=1, source_target_pairs={{0,4},{1,13},{2,6},{3,15},{4,8},{5,1},{6,10},{7,3},{8,12},{9,5},{1... | collective-permute-start | bytes 2949128 | tf_op jit(solution)/shard_map/ppermute | solution.py:1064
  192.7 13.6 %collective-permute-start.7 = (bf16[3,4,2,32,640]{4,3,2,1,0:T(8,128)(2,1)}, bf16[3,4,2,32,640]{4,3,2,1,0:T(8,128)(2,1)}, u32[]{:S(2)}, u32[]{:S(2)}) collective-permute-start(bf16[3,4,2,32,640]{4,3,2,1,0:T(8,128)(2,1)} %collective-permute-done.4.refs_6_), channel_id=1, source_target_pairs={{0,16},{1,49},{2,18},{3,51},{4,20},{5,53},{6,22},{7,55},{8,24},{9,... | collective-permute-start | bytes 2949128 | tf_op jit(solution)/shard_map/ppermute | solution.py:1064
  273.3 1.7 copy-start.5
  273.3 1.7 copy-start.16
  275.4 4.8 collective-permute-start.13
  276.3 5.1 copy-start.22
  277.6 13.6 %collective-permute-start.11 = (bf16[3,4,2,32,640]{4,3,2,1,0:T(8,128)(2,1)}, bf16[3,4,2,32,640]{4,3,2,1,0:T(8,128)(2,1)}, u32[]{:S(2)}, u32[]{:S(2)}) collective-permute-start(bf16[3,4,2,32,640]{4,3,2,1,0:T(8,128)(2,1)} %get-tuple-element.79), channel_id=1, source_target_pairs={{0,4},{1,13},{2,6},{3,15},{4,8},{5,1},{6,10},{7,3},{8,12},{9,5},{1... | collective-permute-start | bytes 2949128 | tf_op jit(solution)/shard_map/ppermute | solution.py:1064
  278.4 14.0 %collective-permute-start.12 = (bf16[3,4,2,32,640]{4,3,2,1,0:T(8,128)(2,1)}, bf16[3,4,2,32,640]{4,3,2,1,0:T(8,128)(2,1)}, u32[]{:S(2)}, u32[]{:S(2)}) collective-permute-start(bf16[3,4,2,32,640]{4,3,2,1,0:T(8,128)(2,1)} %get-tuple-element.80), channel_id=1, source_target_pairs={{0,16},{1,49},{2,18},{3,51},{4,20},{5,53},{6,22},{7,55},{8,24},{9,... | collective-permute-start | bytes 2949128 | tf_op jit(solution)/shard_map/ppermute | solution.py:1064
  280.3 234.8 %collective-permute-start.10 = (bf16[128,2048]{1,0:T(8,128)(2,1)}, bf16[128,2048]{1,0:T(8,128)(2,1)}, u32[]{:S(2)}, u32[]{:S(2)}) collective-permute-start(bf16[128,2048]{1,0:T(8,128)(2,1)} %get-tuple-element.77), channel_id=1, source_target_pairs={{0,2},{1,3},{64,66},{65,67},{2,0},{3,1},{66,64},{67,65},{4,6},{5,7... | collective-permute-start | bytes 1572872 | tf_op jit(solution)/shard_map/ppermute | solution.py:1050
  280.3 234.8 %collective-permute-start.9 = (bf16[128,2048]{1,0:T(8,128)(2,1)}, bf16[128,2048]{1,0:T(8,128)(2,1)}, u32[]{:S(2)}, u32[]{:S(2)}) collective-permute-start(bf16[128,2048]{1,0:T(8,128)(2,1)} %get-tuple-element.76), channel_id=1, source_target_pairs={{0,64},{1,65},{64,2},{65,3},{2,66},{3,67},{66,0},{67,1},{4,68},{5,... | collective-permute-start | bytes 1572872 | tf_op jit(solution)/shard_map/ppermute | solution.py:1050
  282.8 1.7 copy-start.2
  346.4 14.8 %collective-permute-start.14 = (bf16[3,4,2,32,640]{4,3,2,1,0:T(8,128)(2,1)}, bf16[3,4,2,32,640]{4,3,2,1,0:T(8,128)(2,1)}, u32[]{:S(2)}, u32[]{:S(2)}) collective-permute-start(bf16[3,4,2,32,640]{4,3,2,1,0:T(8,128)(2,1)} %fusion.7), channel_id=1, source_target_pairs={{0,4},{1,13},{2,6},{3,15},{4,8},{5,1},{6,10},{7,3},{8,12},{9,5},{1... | collective-permute-start | bytes 2949128 | tf_op jit(solution)/shard_map/ppermute | solution.py:1064
  347.8 4.2 copy-start.4
  350.7 13.6 %collective-permute-start.15 = (bf16[3,4,2,32,640]{4,3,2,1,0:T(8,128)(2,1)}, bf16[3,4,2,32,640]{4,3,2,1,0:T(8,128)(2,1)}, u32[]{:S(2)}, u32[]{:S(2)}) collective-permute-start(bf16[3,4,2,32,640]{4,3,2,1,0:T(8,128)(2,1)} %fusion.6), channel_id=1, source_target_pairs={{0,16},{1,49},{2,18},{3,51},{4,20},{5,53},{6,22},{7,55},{8,24},{9,... | collective-permute-start | bytes 2949128 | tf_op jit(solution)/shard_map/ppermute | solution.py:1064
  353.0 5.7 %copy-start.20 = (f32[256,1152]{1,0:T(8,128)S(1)}, f32[256,1152]{1,0:T(8,128)}, u32[]{:S(2)}) copy-start(f32[256,1152]{1,0:T(8,128)} %copy-done.19) | copy-start | bytes 3538948
  353.0 5.7 %copy-start.21 = (f32[256,768]{1,0:T(8,128)S(1)}, f32[256,768]{1,0:T(8,128)}, u32[]{:S(2)}) copy-start(f32[256,768]{1,0:T(8,128)} %copy.129) | copy-start | bytes 2359300
  407.9 1.4 copy-start.25
  413.5 8.7 %copy-start.23 = (f32[256,2048]{1,0:T(8,128)}, f32[256,2048]{1,0:T(8,128)S(1)}, u32[]{:S(2)}) copy-start(f32[256,2048]{1,0:T(8,128)S(1)} %fusion.44) | copy-start | bytes 6291460
  414.7 20.3 %collective-permute-start.16 = (f32[128,2048]{1,0:T(8,128)}, f32[128,2048]{1,0:T(8,128)}, u32[]{:S(2)}, u32[]{:S(2)}) collective-permute-start(f32[128,2048]{1,0:T(8,128)} %constant_dynamic-slice_fusion), channel_id=1, source_target_pairs={{0,1},{1,0},{2,3},{3,2},{4,5},{5,4},{6,7},{7,6},{8,9},{9,8},{10,11... | collective-permute-start | bytes 3145736 | tf_op jit(solution)/shard_map/ppermute | solution.py:1019
  422.2 5.9 %copy-start.27 = (bf16[256,768]{1,0:T(8,128)(2,1)S(1)}, bf16[256,768]{1,0:T(8,128)(2,1)}, u32[]{:S(2)}) copy-start(bf16[256,768]{1,0:T(8,128)(2,1)} %copy-done.26) | copy-start | bytes 1179652
  422.2 5.9 %copy-start.30 = (bf16[128,2048]{1,0:T(8,128)(2,1)S(1)}, bf16[128,2048]{1,0:T(8,128)(2,1)}, u32[]{:S(2)}) copy-start(bf16[128,2048]{1,0:T(8,128)(2,1)} %copy-done.29) | copy-start | bytes 1572868
  422.2 5.9 %copy-start.32 = (bf16[128,2048]{1,0:T(8,128)(2,1)S(1)}, bf16[128,2048]{1,0:T(8,128)(2,1)}, u32[]{:S(2)}) copy-start(bf16[128,2048]{1,0:T(8,128)(2,1)} %copy-done.31) | copy-start | bytes 1572868
  422.2 16.1 %collective-permute-start.17 = (bf16[3,4,2,32,640]{4,3,2,1,0:T(8,128)(2,1)}, bf16[3,4,2,32,640]{4,3,2,1,0:T(8,128)(2,1)}, u32[]{:S(2)}, u32[]{:S(2)}) collective-permute-start(bf16[3,4,2,32,640]{4,3,2,1,0:T(8,128)(2,1)} %fusion.5), channel_id=1, source_target_pairs={{0,4},{1,13},{2,6},{3,15},{4,8},{5,1},{6,10},{7,3},{8,12},{9,5},{1... | collective-permute-start | bytes 2949128 | tf_op jit(solution)/shard_map/ppermute | solution.py:1064
  425.1 6.1 %copy-start.13 = (bf16[256,2048]{1,0:T(8,128)(2,1)S(1)}, bf16[256,2048]{1,0:T(8,128)(2,1)}, u32[]{:S(2)}) copy-start(bf16[256,2048]{1,0:T(8,128)(2,1)} %fusion.1) | copy-start | bytes 3145732
  425.1 14.3 %collective-permute-start.18 = (bf16[3,4,2,32,640]{4,3,2,1,0:T(8,128)(2,1)}, bf16[3,4,2,32,640]{4,3,2,1,0:T(8,128)(2,1)}, u32[]{:S(2)}, u32[]{:S(2)}) collective-permute-start(bf16[3,4,2,32,640]{4,3,2,1,0:T(8,128)(2,1)} %fusion.4), channel_id=1, source_target_pairs={{0,16},{1,49},{2,18},{3,51},{4,20},{5,53},{6,22},{7,55},{8,24},{9,... | collective-permute-start | bytes 2949128 | tf_op jit(solution)/shard_map/ppermute | solution.py:1064
  431.2 3.8 copy-start.10
  431.3 3.8 copy-start.24
  435.0 80.0 %collective-permute-start.8 = (bf16[128,2048]{1,0:T(8,128)(2,1)}, bf16[128,2048]{1,0:T(8,128)(2,1)}, u32[]{:S(2)}, u32[]{:S(2)}) collective-permute-start(bf16[128,2048]{1,0:T(8,128)(2,1)} %get-tuple-element.75), channel_id=1, source_target_pairs={{0,66},{1,67},{64,0},{65,1},{2,64},{3,65},{66,2},{67,3},{4,70},{5,... | collective-permute-start | bytes 1572872 | tf_op jit(solution)/shard_map/ppermute | solution.py:1050
  505.7 9.3 %copy-start.6 = (f32[128,2048]{1,0:T(8,128)S(1)}, f32[128,2048]{1,0:T(8,128)}, u32[]{:S(2)}) copy-start(f32[128,2048]{1,0:T(8,128)} %get-tuple-element.78) | copy-start | bytes 3145732
  505.7 9.3 %copy-start.17 = (bf16[1,128,2048]{2,1,0:T(8,128)(2,1)S(1)}, bf16[1,128,2048]{2,1,0:T(8,128)(2,1)}, u32[]{:S(2)}) copy-start(bf16[1,128,2048]{2,1,0:T(8,128)(2,1)} %param.17) | copy-start | bytes 1572868
  506.6 8.5 %copy-start.18 = (f32[128,2048]{1,0:T(8,128)S(1)}, f32[128,2048]{1,0:T(8,128)}, u32[]{:S(2)}) copy-start(f32[128,2048]{1,0:T(8,128)} %get-tuple-element.105) | copy-start | bytes 3145732
  506.6 8.5 %copy-start.28 = (f32[128,2048]{1,0:T(8,128)S(1)}, f32[128,2048]{1,0:T(8,128)}, u32[]{:S(2)}) copy-start(f32[128,2048]{1,0:T(8,128)} %get-tuple-element.74) | copy-start | bytes 3145732
  515.1 3.5 copy-start.35
  (10 other events, 9.4 us)

commit v4 on v3

--- a/solution.py
+++ b/solution.py
@@ -188,14 +188,15 @@
     return tuple(SIZES[dim] if axis_of(dim, dims) in full else 1 for dim in dims)
 
 
-def landing_shapes(dims, order, rows, width, always=(), direct=0):
+def landing_shapes(dims, order, rows, width, always=(), direct=0, beneath=()):
     shapes = []
     for phase, axis in enumerate(order):
         lead = slab_shape(dims, always + order[phase + 1 :])
         if SPAN[axis] == 2 or phase >= len(order) - direct:
-            shapes += [lead + (rows, width)] * (SPAN[axis] - 1)
+            shapes += [lead + (rows, width) + beneath] * (SPAN[axis] - 1)
         else:
-            shapes += [lead + (rows // 2, width)] * 2 + [lead + (rows, width)] * 2
+            shapes += [lead + (rows // 2, width) + beneath] * 2
+            shapes += [lead + (rows, width) + beneath] * 2
     return shapes
 
 
@@ -205,7 +206,7 @@
     half = rows // 2
     first_axis, first_full = order[0], always + order[1:]
     loads = []
-    for by in [0, 1, 3] if SPAN[first_axis] == 4 else [0]:
+    for by in () if source is None else (0, 1, 3):
         index = spot.slab(dims, first_full, first_axis, spot.turn(first_axis, by))
         loads.append(wires.copy(source.at[index], held.at[index]))
     start(loads)
@@ -214,7 +215,7 @@
         lead = slab_shape(dims, full)
         flat = tuple(slice(None) if size > 1 else 0 for size in lead)
         me = spot.at[axis]
-        origin = source if phase == 0 else held
+        origin = source if phase == 0 and source is not None else held
 
         def at(value, index):
             spots = spot.slab(dims, full, axis, value)
@@ -454,81 +455,6 @@
         copy.wait()
 
 
-def key_gather_kernel(source, cotangent, out, line, send, recv, local):
-    spot, wires = Spot(), Wires(send, recv, local)
-    spot.greet((("x", (1, 3)), ("y", (1, 3)), ("z", (1, 3)), ("k", (1,))))
-    own = tuple(spot.at[dim] for dim in KEY_DIMS)
-    copies = start([wires.copy(source.at[s], out.at[(s,) + own]) for s in range(2)])
-    for copy in copies:
-        copy.wait()
-    whole = pl.ds(0, source.shape[-1])
-    threads = [
-        gather_lane(spot, wires, KEY_DIMS, order, [(out.at[s], whole)], source.shape[1])
-        for s, order in enumerate(KEY_GATHER_ORDERS)
-    ]
-    run(threads + [line_gather(spot, wires, cotangent, line)])
-
-
-def gather_keys(packed, cotangent):
-    _, rows, width = packed.shape
-    return pl.pallas_call(
-        key_gather_kernel,
-        out_shape=[
-            jax.ShapeDtypeStruct((2, 2, 4, 4, rows, width), BF16),
-            jax.ShapeDtypeStruct((4, 2) + cotangent.shape, BF16),
-        ],
-        in_specs=[ANY] * 2,
-        out_specs=[ANY] * 2,
-        scratch_shapes=[
-            pltpu.SemaphoreType.DMA((26,)),
-            pltpu.SemaphoreType.DMA((26,)),
-            pltpu.SemaphoreType.DMA((3,)),
-        ],
-        compiler_params=pltpu.CompilerParams(collective_id=1, has_side_effects=True),
-    )(packed, cotangent)
-
-
-def key_scatter_kernel(source, out, *refs):
-    send, recv, local = refs[:3]
-    buffers = list(refs[3:])
-    spot, wires = Spot(), Wires(send, recv, local)
-    spot.greet((("x", (1, 3)), ("y", (1, 3)), ("p", (1,))))
-    rows, width = source.shape[-2:]
-    lanes = []
-    for s, order in enumerate(KEY_SCATTER_ORDERS):
-        count = len(landing_shapes(KEY_DIMS, order, rows, width))
-        held, landing = buffers[0], buffers[1 : 1 + count]
-        del buffers[: 1 + count]
-        lanes.append(
-            scatter_lane(
-                spot, wires, KEY_DIMS, order, source.at[s], held, landing, out.at[s], rows
-            )
-        )
-    run(lanes)
-
-
-def scatter_keys(grads):
-    rows, width = grads.shape[-2:]
-    scratch = [
-        pltpu.SemaphoreType.DMA((18,)),
-        pltpu.SemaphoreType.DMA((18,)),
-        pltpu.SemaphoreType.DMA((6,)),
-    ]
-    for order in KEY_SCATTER_ORDERS:
-        shapes = [(2, 4, 4, rows, width)] + landing_shapes(KEY_DIMS, order, rows, width)
-        scratch += [pltpu.VMEM(shape, BF16) for shape in shapes]
-    return pl.pallas_call(
-        key_scatter_kernel,
-        out_shape=jax.ShapeDtypeStruct((2, 1, 1, 1, rows, width), F32),
-        in_specs=[ANY],
-        out_specs=pl.BlockSpec(memory_space=pltpu.VMEM),
-        scratch_shapes=scratch,
-        compiler_params=pltpu.CompilerParams(
-            collective_id=2, has_side_effects=True, vmem_limit_bytes=48 << 20
-        ),
-    )(grads)
-
-
 def total_lane(spot, wires, vector, slots, out):
     value = vector[...]
     sent = []
@@ -691,14 +617,40 @@
     return lax.dot_general(left, right, (dims, ((), ())), preferred_element_type=F32)
 
 
-def key_chunk(slot_ref, kv, s, h, chunk):
-    pieces = []
-    for n in range(4):
-        slot = slot_ref[chunk * 4 + n]
-        rows = pl.ds(pl.multiple_of(lax.rem(slot, 2) * 64, 64), 64)
-        place = (lax.div(slot, 32), lax.rem(lax.div(slot, 8), 4), lax.rem(lax.div(slot, 2), 4))
-        pieces.append(kv[(s,) + place + (rows, slice(h * 128, h * 128 + 128))])
-    return jnp.concatenate(pieces, axis=0)
+def slot_place(slot):
+    places = (lax.div(slot, 32), lax.rem(lax.div(slot, 8), 4), lax.rem(lax.div(slot, 2), 4))
+    return places + (lax.rem(slot, 2),)
+
+
+def key_chunk(slot_ref, kv, chunk):
+    return jnp.concatenate([kv[slot_place(slot_ref[chunk * 4 + n])] for n in range(4)], axis=0)
+
+
+def head_norm(values):
+    inverse = lax.rsqrt(jnp.mean(values * values, axis=0, keepdims=True) + EPSILON)
+    return values * inverse, inverse
+
+
+def rotate(values, cosine, sine):
+    first, second = values[:32], values[32:]
+    return jnp.concatenate([first * cosine - second * sine, second * cosine + first * sine], axis=0)
+
+
+def to_block(heads, s, block):
+    first = s * 128 + block * 64
+    return jnp.concatenate([head[:, first : first + 64] for head in heads], axis=1)
+
+
+def from_blocks(blocks, head):
+    return jnp.concatenate([block[:, head * 64 : head * 64 + 64] for block in blocks], axis=1)
+
+
+def head_back(grads, values, gain, cosine, sine):
+    normed, inverse = head_norm(values)
+    grads = rotate(grads, cosine, -sine)
+    scaled = grads * gain
+    back = inverse * (scaled - normed * jnp.mean(scaled * normed, axis=0, keepdims=True))
+    return back, jnp.sum(grads * normed, axis=1, keepdims=True)
 
 
 def allowed_in(chunk, anchor, first):
@@ -706,138 +658,387 @@
     return (key <= anchor) & (key >= first)
 
 
-def attention_kernel(slot_ref, low_ref, kv, q_ref, anchor_ref, first_ref, o_ref, lse_ref, acc, norm):
+def attend(s, h, slot_ref, low, kv, q_ref, anchor_ref, first_ref, out_ref, lse_ref, acc, norm):
+    def item(chunk, block):
+        kv_rows = key_chunk(slot_ref, kv, chunk)
+        scores = contract(kv_rows, q_ref[s, h, block], ((1,), (0,)))
+        allowed = allowed_in(chunk, anchor_ref[s, block], first_ref[s, block])
+        weights = jnp.where(allowed, jnp.exp(scores), 0.0)
+        return (
+            jnp.sum(weights, axis=0, keepdims=True),
+            contract(kv_rows, weights.astype(BF16), ((0,), (0,))),
+        )
+
+    def early(chunk, carry):
+        total, out = item(chunk, 1)
+        return carry[0] + total, carry[1] + out
+
+    norm[1], acc[1] = lax.fori_loop(0, 8, early, item(15 - lax.div(low, 4), 1), unroll=True)
+    norm[0] = jnp.zeros((1, 256), F32)
+    acc[0] = jnp.zeros((128, 256), F32)
+
+    def either(chunk, _):
+        is_low = low >= 4 * chunk
+        total, out = item(jnp.where(is_low, chunk, 15 - chunk), jnp.where(is_low, 0, 1))
+        share = jnp.where(is_low, 1.0, 0.0)
+        norm[0] += total * share
+        norm[1] += total * (1.0 - share)
+        acc[0] += out * share
+        acc[1] += out * (1.0 - share)
+        return 0
+
+    lax.fori_loop(0, 8, either, 0, unroll=True)
+    outs = [acc[block, 64:, :] / norm[block] for block in range(2)]
+    for head in range(4):
+        out_ref[pl.ds((4 * h + head) * 64, 64), pl.ds(s * 128, 128)] = from_blocks(outs, head)
+    for block in range(2):
+        lse_ref[s, h, block] = jnp.log(norm[block])
+
+
+HEADS = [(s, h) for s in range(2) for h in range(3)]
+
+
+def attention_kernel(*refs):
+    refs = list(refs)
+
+    def take(count):
+        taken = refs[:count]
+        del refs[:count]
+        return taken
+
+    slot_ref, low_ref, qkv, cosine_ref, sine_ref, q_gain, k_gain = take(7)
+    anchor_ref, first_ref, cotangent = take(3)
+    out_ref, lse_ref, q_out, kv_out, line = take(5)
+    buffers, (acc, norm) = take(6), take(2)
+    spot, wires = Spot(), Wires(*refs)
+    own = tuple(spot.at[dim] for dim in KEY_DIMS)
+    cosine, sine = cosine_ref[...], sine_ref[...]
+    for h in range(3):
+        keys = rotate(head_norm(qkv[768 + 64 * h : 832 + 64 * h])[0] * k_gain[...], cosine, sine)
+        both = jnp.concatenate([keys, qkv[960 + 64 * h : 1024 + 64 * h]], axis=0).T.astype(BF16)
+        for s in range(2):
+            buffers[s * 3 + h][own] = both[s * 128 : s * 128 + 128].reshape(2, 64, 128)
+    spot.greet((("x", RING), ("y", RING), ("z", (1, 3)), ("k", (1,))))
     low = low_ref[0]
-    for s in range(2):
-        for h in range(3):
-
-            def item(chunk, block):
-                kv_rows = key_chunk(slot_ref, kv, s, h, chunk)
-                scores = contract(kv_rows, q_ref[s, h, block], ((1,), (1,)))
-                allowed = allowed_in(chunk, anchor_ref[s, block], first_ref[s, block])
-                weights = jnp.where(allowed, jnp.exp(scores), 0.0)
-                return (
-                    jnp.sum(weights, axis=0, keepdims=True),
-                    contract(kv_rows, weights.astype(BF16), ((0,), (0,))),
-                )
-
-            def early(chunk, carry):
-                total, out = item(chunk, 1)
-                return carry[0] + total, carry[1] + out
-
-            norm[1], acc[1] = lax.fori_loop(
-                0, 8, early, item(15 - lax.div(low, 4), 1), unroll=True
+    streams = [
+        gather_lane(
+            spot, wires, KEY_DIMS, KEY_GATHER_ORDERS[n % 2], [(buffer, pl.ds(0, 64))], 2, direct=2
+        )
+        for n, buffer in enumerate(buffers)
+    ]
+    rows = line_gather(spot, wires, cotangent, line)
+    kept = []
+
+    def go_on(pair):
+        for n in (2 * pair, 2 * pair + 1):
+            next(streams[n], None)
+
+    def work(pair):
+        for n in (2 * pair, 2 * pair + 1):
+            kept.append(wires.copy(buffers[n], kv_out.at[n]))
+            start(kept[-1:])
+            attend(
+                *HEADS[n], slot_ref, low, buffers[n], q_out, anchor_ref, first_ref, out_ref, lse_ref, acc, norm
             )
-            norm[0] = jnp.zeros((1, 256), F32)
-            acc[0] = jnp.zeros((128, 256), F32)
-
-            def either(chunk, _):
-                is_low = low >= 4 * chunk
-                total, out = item(jnp.where(is_low, chunk, 15 - chunk), jnp.where(is_low, 0, 1))
-                share = jnp.where(is_low, 1.0, 0.0)
-                norm[0] += total * share
-                norm[1] += total * (1.0 - share)
-                acc[0] += out * share
-                acc[1] += out * (1.0 - share)
-                return 0
-
-            lax.fori_loop(0, 8, either, 0, unroll=True)
+
+    def queries(h):
+        heads = []
+        for head in range(4 * h, 4 * h + 4):
+            values = head_norm(qkv[64 * head : 64 * head + 64])[0] * q_gain[...]
+            values = rotate(values, cosine, sine).astype(BF16)
+            heads.append(values.astype(F32) * 0.125)
+        for s in range(2):
             for block in range(2):
-                o_ref[s, h, block] = acc[block, 64:, :] / norm[block]
-                lse_ref[s, h, block] = jnp.log(norm[block])
+                q_out[s, h, block, :64] = to_block(heads, s, block).astype(BF16)
+                q_out[s, h, block, 64:] = jnp.zeros((64, 256), BF16)
+
+    for pair in range(3):
+        go_on(pair)
+    next(rows, None)
+    queries(0)
+    for pair in range(3):
+        go_on(pair)
+    next(rows, None)
+    queries(1)
+    for pair in (0, 1):
+        go_on(pair)
+    queries(2)
+    next(rows, None)
+    for pair in (0, 2, 1, 0):
+        go_on(pair)
+    work(0)
+    go_on(2)
+    go_on(1)
+    next(rows, None)
+    work(1)
+    go_on(2)
+    work(2)
+    for copy in kept:
+        copy.wait()
 
 
 IN_VMEM = pl.BlockSpec(memory_space=pltpu.VMEM)
 IN_SMEM = pl.BlockSpec(memory_space=pltpu.SMEM)
 
 
-def attention(slots, low, kv, q, anchor, first):
+def attention(slots, low, qkv, cosine, sine, q_gain, k_gain, anchor, first, cotangent):
+    remotes = 6 * (1 + 3 + 4) + 8
     return pl.pallas_call(
         attention_kernel,
-        in_specs=[IN_SMEM] * 2 + [IN_VMEM] * 4,
-        out_specs=[IN_VMEM] * 2,
+        in_specs=[IN_SMEM] * 2 + [IN_VMEM] * 7 + [ANY],
+        out_specs=[IN_VMEM] * 3 + [ANY] * 2,
         out_shape=[
-            jax.ShapeDtypeStruct((2, 3, 2, 64, 256), F32),
+            jax.ShapeDtypeStruct((768, 256), F32),
             jax.ShapeDtypeStruct((2, 3, 2, 1, 256), F32),
+            jax.ShapeDtypeStruct((2, 3, 2, 128, 256), BF16),
+            jax.ShapeDtypeStruct((6, 2, 4, 4, 2, 64, 128), BF16),
+            jax.ShapeDtypeStruct((4, 2) + cotangent.shape, BF16),
         ],
-        scratch_shapes=[pltpu.VMEM((2, 128, 256), F32), pltpu.VMEM((2, 1, 256), F32)],
-        compiler_params=pltpu.CompilerParams(vmem_limit_bytes=40 << 20),
-    )(slots, low, kv, q, anchor, first)
-
-
-def attention_back_kernel(
-    slot_ref, low_ref, map_ref, kv, q_ref, d_ref, anchor_ref, first_ref, lse_ref, delta_ref, dq_ref, dkv_ref, acc, sums
+        scratch_shapes=[pltpu.VMEM((2, 4, 4, 2, 64, 128), BF16)] * 6
+        + [
+            pltpu.VMEM((2, 128, 256), F32),
+            pltpu.VMEM((2, 1, 256), F32),
+            pltpu.SemaphoreType.DMA((remotes,)),
+            pltpu.SemaphoreType.DMA((remotes,)),
+            pltpu.SemaphoreType.DMA((7,)),
+        ],
+        compiler_params=pltpu.CompilerParams(
+            collective_id=1, has_side_effects=True, vmem_limit_bytes=40 << 20
+        ),
+    )(slots, low, qkv, cosine, sine, q_gain, k_gain, anchor, first, cotangent)
+
+
+def attend_back(
+    s, h, slot_ref, low, map_ref, kv, q_ref, d_ref, anchor_ref, first_ref, lse_ref, delta, dq_ref, dkv_ref, acc, sums
 ):
+    edge = lax.div(low, 4)
+
+    def item(chunk, block):
+        kv_rows = key_chunk(slot_ref, kv, chunk)
+        q, d = q_ref[s, h, block], d_ref[block]
+        scores = contract(kv_rows, q, ((1,), (0,)))
+        toward = contract(kv_rows, d, ((1,), (0,)))
+        allowed = allowed_in(chunk, anchor_ref[s, block], first_ref[s, block])
+        weights = jnp.where(allowed, jnp.exp(scores - lse_ref[s, h, block]), 0.0)
+        grads = (weights * (toward - delta[block])).astype(BF16)
+        return (
+            contract(kv_rows, grads, ((0,), (0,))),
+            (
+                contract(grads, q, ((1,), (1,))) + contract(weights.astype(BF16), d, ((1,), (1,)))
+            ).reshape(4, 64, 128),
+        )
+
+    acc[0] = jnp.zeros((128, 256), F32)
+    acc[1], late = item(15 - edge, 1)
+    for chunk in range(8):
+        sums[15 - chunk] = late * jnp.where(edge == chunk, 1.0, 0.0)
+
+    def early(chunk, _):
+        dq, sums[chunk] = item(chunk, 1)
+        acc[1] += dq
+        return 0
+
+    lax.fori_loop(0, 8, early, 0, unroll=True)
+
+    def either(chunk, _):
+        is_low = low >= 4 * chunk
+        dq, dkv = item(jnp.where(is_low, chunk, 15 - chunk), jnp.where(is_low, 0, 1))
+        share = jnp.where(is_low, 1.0, 0.0)
+        acc[0] += dq * share
+        acc[1] += dq * (1.0 - share)
+        sums[chunk] += dkv * share
+        sums[15 - chunk] += dkv * (1.0 - share)
+        return 0
+
+    lax.fori_loop(0, 8, either, 0, unroll=True)
+    blocks = [acc[block, :64, :] * 0.125 for block in range(2)]
+    for head in range(4):
+        dq_ref[pl.ds((4 * h + head) * 64, 64), pl.ds(s * 128, 128)] = from_blocks(blocks, head)
+
+    def put(slot, _):
+        block = map_ref[slot]
+        dkv_ref[slot_place(slot)] = sums[lax.div(block, 4), lax.rem(block, 4)].astype(BF16)
+        return 0
+
+    lax.fori_loop(0, 64, put, 0, unroll=4)
+
+
+PIECE = (3, 4, 2, 32, 640)
+
+
+def ring_place(spot, axis, step):
+    return lax.rem(spot.at[axis] + 4 - step + 2 * step * spot.at["k"], 4)
+
+
+def ring_device(spot, axis):
+    return spot.device(axis, spot.turn(axis, 1 + 2 * spot.at["k"]))
+
+
+def ring_lane(spot, wires, lane, arrived, grads, out, held, terms, landing):
+    axis = ("y", "x")[lane]
+
+    def load(step, target):
+        place = ring_place(spot, axis, step)
+        return wires.copy(grads.at[:, :, place] if lane == 0 else grads.at[:, place], target)
+
+    def add(running, term):
+        def one(index):
+            total = running[index].astype(F32) + term[index].astype(F32)
+            running[index] = total.astype(BF16)
+
+        each_block(PIECE[:3], one)
+
+    loads = start([wires.copy(arrived, held), load(2, terms[0])])
+    yield
+    for copy in loads:
+        copy.wait()
+    running, sent = held, []
+    for step in (2, 3):
+        add(running, terms[step % 2])
+        copy = wires.remote(running, landing[step - 2], ring_device(spot, axis))
+        sent += start([copy])
+        running = landing[step - 2]
+        following = load(step + 1, terms[(step + 1) % 2])
+        start([following])
+        yield
+        following.wait()
+        copy.wait_recv()
+    add(running, terms[0])
+    last = wires.copy(running, out)
+    start([last])
+    yield
+    last.wait()
+    for copy in sent:
+        copy.wait_send()
+
+
+def attention_back_kernel(*refs):
+    refs = list(refs)
+
+    def take(count):
+        taken = refs[:count]
+        del refs[:count]
+        return taken
+
+    slot_ref, low_ref, map_ref, kv_all = take(4)
+    arrived, ffn_grads = take(2), take(2)
+    qkv, cosine_ref, sine_ref, q_gain, k_gain = take(5)
+    q_ref, d_rows, attended, anchor_ref, first_ref, lse_ref = take(6)
+    grad_ref, q_terms, k_terms = take(3)
+    ffn_out = take(2)
+    buffers, held, finals = take(6), take(6), take(6)
+    acc, sums, d_blocks, delta, dq = take(5)
+    landings = [take(len(key_landing(n))) for n in range(6)]
+    ring_buffers = [take(5), take(5)]
+    spot, wires = Spot(), Wires(*refs)
+    loads = start([wires.copy(kv_all.at[n], buffer) for n, buffer in enumerate(buffers)])
+    rings = [
+        ring_lane(spot, wires, lane, arrived[lane], ffn_grads[lane], ffn_out[lane], b[0], b[1:3], b[3:])
+        for lane, b in enumerate(ring_buffers)
+    ]
+
+    def turn_rings():
+        for ring in rings:
+            next(ring, None)
+
+    turn_rings()
+    spot.greet((("x", RING), ("y", RING), ("p", (1,))))
+    turn_rings()
     low = low_ref[0]
-    edge = lax.div(low, 4)
-    for s in range(2):
-        for h in range(3):
-
-            def item(chunk, block):
-                kv_rows = key_chunk(slot_ref, kv, s, h, chunk)
-                q, d = q_ref[s, h, block], d_ref[s, h, block]
-                scores = contract(kv_rows, q, ((1,), (1,)))
-                toward = contract(kv_rows, d, ((1,), (1,)))
-                allowed = allowed_in(chunk, anchor_ref[s, block], first_ref[s, block])
-                weights = jnp.where(allowed, jnp.exp(scores - lse_ref[s, h, block]), 0.0)
-                grads = (weights * (toward - delta_ref[s, h, block])).astype(BF16)
-                return (
-                    contract(kv_rows, grads, ((0,), (0,))),
-                    contract(grads, q, ((1,), (0,)))
-                    + contract(weights.astype(BF16), d, ((1,), (0,))),
-                )
-
-            acc[0] = jnp.zeros((128, 256), F32)
-            acc[1], late = item(15 - edge, 1)
-            for chunk in range(8):
-                sums[15 - chunk] = late * jnp.where(edge == chunk, 1.0, 0.0)
-
-            def early(chunk, _):
-                dq, sums[chunk] = item(chunk, 1)
-                acc[1] += dq
-                return 0
-
-            lax.fori_loop(0, 8, early, 0, unroll=True)
-
-            def either(chunk, _):
-                is_low = low >= 4 * chunk
-                dq, dkv = item(jnp.where(is_low, chunk, 15 - chunk), jnp.where(is_low, 0, 1))
-                share = jnp.where(is_low, 1.0, 0.0)
-                acc[0] += dq * share
-                acc[1] += dq * (1.0 - share)
-                sums[chunk] += dkv * share
-                sums[15 - chunk] += dkv * (1.0 - share)
-                return 0
-
-            lax.fori_loop(0, 8, either, 0, unroll=True)
-            for block in range(2):
-                dq_ref[s, h, block] = acc[block, :64, :]
-
-            def put(slot, _):
-                block = map_ref[slot]
-                rows = pl.ds(pl.multiple_of(lax.rem(block, 4) * 64, 64), 64)
-                to = pl.ds(pl.multiple_of(lax.rem(slot, 2) * 64, 64), 64)
-                place = (lax.div(slot, 32), lax.rem(lax.div(slot, 8), 4), lax.rem(lax.div(slot, 2), 4))
-                dkv_ref[(s,) + place + (to, slice(h * 128, h * 128 + 128))] = sums[
-                    lax.div(block, 4), rows, :
-                ].astype(BF16)
-                return 0
-
-            lax.fori_loop(0, 64, put, 0, unroll=4)
-
-
-def attention_back(slots, low, block_map, kv, q, d, anchor, first, lse, delta):
+    cosine, sine = cosine_ref[...], sine_ref[...]
+    streams = []
+    for n, (s, h) in enumerate(HEADS):
+        heads = [pl.ds(64 * head, 64) for head in range(4 * h, 4 * h + 4)]
+        for block in range(2):
+            d = to_block([d_rows[head].astype(F32) for head in heads], s, block)
+            out = to_block([attended[head] for head in heads], s, block)
+            delta[block] = jnp.sum(d * out, axis=0, keepdims=True)
+            d_blocks[block, :64] = jnp.zeros((64, 256), BF16)
+            d_blocks[block, 64:] = d.astype(BF16)
+        loads[n].wait()
+        attend_back(
+            s, h, slot_ref, low, map_ref, buffers[n], q_ref, d_blocks, anchor_ref, first_ref, lse_ref, delta, dq, held[n], acc, sums
+        )
+        streams.append(
+            scatter_lane(
+                spot,
+                wires,
+                KEY_DIMS,
+                KEY_SCATTER_ORDERS[n % 2],
+                None,
+                held[n],
+                landings[n],
+                finals[n],
+                2,
+                direct=2,
+            )
+        )
+        for stream in streams:
+            next(stream, None)
+        if n in (1, 3, 4):
+            turn_rings()
+    for stream in streams:
+        next(stream, None)
+    total = jnp.zeros((64, 1), F32)
+    for head in range(12):
+        rows = pl.ds(64 * head, 64)
+        back, terms = head_back(dq[rows], qkv[rows], q_gain[...], cosine, sine)
+        grad_ref[rows] = back.astype(BF16)
+        total = total + terms
+        if head % 4 == 3:
+            for stream in streams:
+                next(stream, None)
+    q_terms[...] = total
+    run(streams)
+    run(rings)
+    total = jnp.zeros((64, 1), F32)
+    for h in range(3):
+        both = [finals[s * 3 + h][0, 0, 0].reshape(128, 128).T for s in range(2)]
+        both = jnp.concatenate(both, axis=1)
+        rows = pl.ds(768 + 64 * h, 64)
+        back, terms = head_back(both[:64], qkv[rows], k_gain[...], cosine, sine)
+        grad_ref[rows] = back.astype(BF16)
+        grad_ref[pl.ds(960 + 64 * h, 64)] = both[64:].astype(BF16)
+        total = total + terms
+    k_terms[...] = total
+
+
+def key_landing(n):
+    return landing_shapes(KEY_DIMS, KEY_SCATTER_ORDERS[n % 2], 2, 64, direct=2, beneath=(128,))
+
+
+def attention_back(slots, low, block_map, kv, ffn, heads, rows):
+    remotes = 6 * (4 + 3 + 1) + 4
     return pl.pallas_call(
         attention_back_kernel,
-        in_specs=[IN_SMEM] * 3 + [IN_VMEM] * 7,
-        out_specs=[IN_VMEM] * 2,
+        in_specs=[IN_SMEM] * 3 + [ANY] * 5 + [IN_VMEM] * 11,
+        out_specs=[IN_VMEM] * 3 + [ANY] * 2,
         out_shape=[
-            jax.ShapeDtypeStruct((2, 3, 2, 64, 256), F32),
-            jax.ShapeDtypeStruct(kv.shape, BF16),
+            jax.ShapeDtypeStruct((1152, 256), BF16),
+            jax.ShapeDtypeStruct((64, 1), F32),
+            jax.ShapeDtypeStruct((64, 1), F32),
+        ]
+        + [jax.ShapeDtypeStruct(PIECE, BF16)] * 2,
+        scratch_shapes=[pltpu.VMEM((2, 4, 4, 2, 64, 128), BF16)] * 12
+        + [pltpu.VMEM((1, 1, 1, 2, 64, 128), F32)] * 6
+        + [
+            pltpu.VMEM((2, 128, 256), F32),
+            pltpu.VMEM((16, 4, 64, 128), F32),
+            pltpu.VMEM((2, 128, 256), BF16),
+            pltpu.VMEM((2, 1, 256), F32),
+            pltpu.VMEM((768, 256), F32),
+        ]
+        + [pltpu.VMEM(shape, BF16) for n in range(6) for shape in key_landing(n)]
+        + [pltpu.VMEM(PIECE, BF16)] * 10
+        + [
+            pltpu.SemaphoreType.DMA((remotes,)),
+            pltpu.SemaphoreType.DMA((remotes,)),
+            pltpu.SemaphoreType.DMA((16,)),
         ],
-        scratch_shapes=[pltpu.VMEM((2, 128, 256), F32), pltpu.VMEM((16, 256, 128), F32)],
-        compiler_params=pltpu.CompilerParams(vmem_limit_bytes=48 << 20),
-    )(slots, low, block_map, kv, q, d, anchor, first, lse, delta)
+        compiler_params=pltpu.CompilerParams(
+            collective_id=2, has_side_effects=True, vmem_limit_bytes=60 << 20
+        ),
+    )(slots, low, block_map, kv, *ffn, *heads, *rows)
 
 
 def ffn_kernel(*refs):
@@ -865,7 +1066,7 @@
             loads.append(wires.copy(piece, target))
     loads.append(wires.copy(cotangent_line, cotangent))
     start(loads)
-    spot.greet((("z", RING), ("k", (1,))))
+    spot.greet((("x", (1, 3)), ("y", (1, 3)), ("z", RING), ("k", (1,))))
     beside = wires.remote(second, line.at[0, 1], sibling)
     sent = [
         wires.remote(second, line.at[slot, 0], spot.device("z", spot.turn("z", by)))
@@ -954,33 +1155,41 @@
     finish(2, latest)
     finish(3, first)
 
-    for low in range(2):
-
-        def outer(place, _):
-            columns = pl.ds(pl.multiple_of((low * 4 + place) * 256, 256), 256)
-            rows = line[:, :, :, columns].reshape(1024, 256)
-            both = contract(rows, grads[...].reshape(1024, 1280), ((0,), (0,))).astype(BF16)
-            grads_out[low][0, place] = both[:, :640].reshape(4, 2, 32, 640)
-            grads_out[low][1, place] = both[:, 640:].reshape(4, 2, 32, 640)
-            rows = cotangent[:, :, :, columns].reshape(1024, 256)
-            down = contract(rows, product[...].reshape(1024, 640), ((0,), (0,))).astype(BF16)
-            grads_out[low][2, place] = down.reshape(4, 2, 32, 640)
+    def outer(low, place):
+        columns = pl.ds(pl.multiple_of((low * 4 + place) * 256, 256), 256)
+        rows = line[:, :, :, columns].reshape(1024, 256)
+        both = contract(rows, grads[...].reshape(1024, 1280), ((0,), (0,))).astype(BF16)
+        grads_out[low][0, place] = both[:, :640].reshape(4, 2, 32, 640)
+        grads_out[low][1, place] = both[:, 640:].reshape(4, 2, 32, 640)
+        rows = cotangent[:, :, :, columns].reshape(1024, 256)
+        down = contract(rows, product[...].reshape(1024, 640), ((0,), (0,))).astype(BF16)
+        grads_out[low][2, place] = down.reshape(4, 2, 32, 640)
+
+    def first_step(low, axis):
+        place = ring_place(spot, axis, 1)
+        slab = grads_out[low].at[:, :, place] if low == 0 else grads_out[low].at[:, place]
+        returns.extend(start([wires.remote(slab, first_out[low], ring_device(spot, axis))]))
+
+    def outers(low, first):
+        def one(number, _):
+            outer(low, lax.rem(first + number, 4))
             return 0
 
-        lax.fori_loop(0, 4, outer, 0)
-    firsts = []
-    for low, axis in enumerate(("y", "x")):
-        place = lax.rem(spot.at[axis] + 3 + 2 * core, 4)
-        slab = grads_out[low].at[:, :, place] if low == 0 else grads_out[low].at[:, place]
-        firsts.append(wires.copy(slab, first_out[low]))
-    start(firsts)
-    for slot, copy in enumerate(returns):
+        return one
+
+    lax.fori_loop(0, 4, outers(0, 0), 0)
+    first_step(0, "y")
+    first = ring_place(spot, "x", 1)
+    outer(1, first)
+    first_step(1, "x")
+    lax.fori_loop(1, 4, outers(1, first), 0)
+    for slot, copy in enumerate(returns[:3]):
         copy.wait_recv()
         back_out[...] += away_in[slot].astype(F32)
+    for copy in returns[3:]:
+        copy.wait_recv()
     for copy in pending + returns:
         copy.wait_send()
-    for copy in firsts:
-        copy.wait()
 
 
 def feed_forward(pieces, second, mask, cotangent_line):
@@ -991,7 +1200,7 @@
         out_shape=[rows] * 2
         + [jax.ShapeDtypeStruct((128, 2048), BF16)] * 3
         + [grads] * 2
-        + [jax.ShapeDtypeStruct((3, 4, 2, 32, 640), BF16)] * 2,
+        + [jax.ShapeDtypeStruct(PIECE, BF16)] * 2,
         in_specs=[ANY] * 8 + [IN_VMEM] * 2 + [ANY],
         out_specs=[IN_VMEM] * 7 + [ANY] * 2,
         scratch_shapes=[
@@ -1005,9 +1214,9 @@
             pltpu.VMEM((4, 2, 128, 2048), BF16),
             pltpu.VMEM((3, 128, 2048), BF16),
             pltpu.VMEM((3, 128, 2048), BF16),
-            pltpu.SemaphoreType.DMA((19,)),
-            pltpu.SemaphoreType.DMA((19,)),
-            pltpu.SemaphoreType.DMA((11,)),
+            pltpu.SemaphoreType.DMA((21,)),
+            pltpu.SemaphoreType.DMA((21,)),
+            pltpu.SemaphoreType.DMA((9,)),
         ],
         compiler_params=pltpu.CompilerParams(
             collective_id=4, has_side_effects=True, vmem_limit_bytes=62 << 20
@@ -1067,14 +1276,6 @@
 RING_AXES = ("y", "x")
 
 
-def ring_total_step(arrived, grads, lane, step, core):
-    ctx = lax.axis_index("ctx")
-    me = lax.rem(ctx, 4) if lane == 0 else lax.rem(lax.div(ctx, 4), 4)
-    place = lax.rem(me + 4 - step + 2 * step * core, 4)
-    slab = lax.dynamic_index_in_dim(grads, place, 2 - lane, keepdims=False)
-    return (arrived.astype(F32) + slab.astype(F32)).astype(BF16)
-
-
 def norm_forward(values, gain):
     inverse = lax.rsqrt(jnp.mean(values * values, axis=-1, keepdims=True) + EPSILON)
     normed = values * inverse
@@ -1085,31 +1286,6 @@
     scaled = grads * gain
     back = inverse * (scaled - normed * jnp.mean(scaled * normed, axis=-1, keepdims=True))
     return (back, grads * normed)
-
-
-def rotate(values, cosine, sine):
-    halfway = values.shape[-1] // 2
-    first = values[..., :halfway]
-    second = values[..., halfway:]
-    return jnp.concatenate(
-        [first * cosine - second * sine, second * cosine + first * sine], axis=-1
-    )
-
-
-def unrotate(grads, cosine, sine):
-    return rotate(grads, cosine, -sine)
-
-
-def to_blocks(heads):
-    depth = heads.shape[-1]
-    split = heads.reshape(2, 2, 64, 3, 4, depth)
-    return split.transpose(0, 3, 1, 4, 2, 5).reshape(2, 3, 2, 256, depth)
-
-
-def from_blocks(tall):
-    depth = tall.shape[3]
-    split = tall.reshape(2, 3, 2, depth, 4, 64)
-    return split.transpose(0, 2, 5, 1, 4, 3).reshape(256, 12, depth)
 
 
 def body(
@@ -1168,21 +1344,13 @@
     low_block = own_blocks[:1]
 
     inverse_freq = ROPE_BASE ** (-(jnp.arange(32, dtype=F32) * 2.0) / 64)
-    angle = position_all.reshape(256).astype(F32)[:, None] * inverse_freq[None, :]
-    cosine, sine = jnp.cos(angle)[:, None, :], jnp.sin(angle)[:, None, :]
+    angle = position_all.reshape(256).astype(F32)[None, :] * inverse_freq[:, None]
+    tables = (jnp.cos(angle), jnp.sin(angle), query_gain[:, None], key_gain[:, None])
 
     first_all, _, _ = norm_forward(tokens_all.reshape(256, 2048).astype(F32), first_gain)
     first_low = first_all.astype(BF16)
     _, first_hat, first_inv = norm_forward(rows, first_gain)
-    qkv_pre = jnp.dot(first_low, qkv_w, preferred_element_type=F32)
-    query_normed, query_hat, query_inv = norm_forward(
-        qkv_pre[:, :768].reshape(256, 12, 64), query_gain
-    )
-    query_low = rotate(query_normed, cosine, sine).astype(BF16)
-    key_normed, key_hat, key_inv = norm_forward(qkv_pre[:, 768:960].reshape(256, 3, 64), key_gain)
-    key_low = rotate(key_normed, cosine, sine).astype(BF16)
-    value_low = qkv_pre[:, 960:].astype(BF16).reshape(256, 3, 64)
-    kv_low = jnp.concatenate([key_low, value_low], axis=2)
+    qkv = contract(qkv_w, first_low, ((0,), (1,)))
     pieces = [[lane] for lane in ffn_first]
 
     def next_pieces(*after):
@@ -1192,16 +1360,13 @@
             lane.append(piece)
         return after
 
-    (kv_low,) = next_pieces(kv_low)
-    kv_all, grad_out_line = gather_keys(kv_low.reshape(2, 128, 384), cotangent[0])
-    query_blocks = jnp.pad(
-        to_blocks(query_low * jnp.asarray(0.125, BF16)), ((0, 0),) * 4 + ((0, 64),)
+    (qkv,) = next_pieces(qkv)
+    attended, lse, query_blocks, kv_all, grad_out_line = attention(
+        slots, low_block, qkv, *tables, anchor_rows, start_rows, cotangent[0]
     )
-    attended, lse = attention(slots, low_block, kv_all, query_blocks, anchor_rows, start_rows)
     (attended,) = next_pieces(attended)
-    attended = from_blocks(attended)
-    merged = attended.reshape(256, 768).astype(BF16)
-    mixed = rows + total_rows(contract(merged, out_w, ((1,), (1,))), core)
+    merged = attended.astype(BF16)
+    mixed = rows + total_rows(contract(merged, out_w, ((0,), (1,))), core)
 
     second_out, second_hat, second_inv = norm_forward(mixed, second_gain)
     second_low = second_out.astype(BF16)
@@ -1210,59 +1375,25 @@
     unit = jnp.arange(640, dtype=jnp.int32)
     held = jnp.where((z == 3) & (unit < 128), 0.0, 1.0).astype(F32)[None, :]
     grad_second, branch, *rest = feed_forward(pieces, second_low, held, grad_out_line)
-    branch_away, ffn_grads, running = rest[:3], rest[3:5], rest[5:]
+    branch_away, ffn_grads, arrived = rest[:3], rest[3:5], rest[5:]
     for part, by in zip(branch_away, FAR):
         branch = branch + along_z(part, 4 - by).astype(F32)
     activations = (mixed + branch).astype(BF16)[None]
 
-    def next_running(step, *after):
-        moved = [round_ring(part, axis) for part, axis in zip(running, RING_AXES)]
-        *moved, after = lax.optimization_barrier((*moved, after))
-        running[:] = [
-            ring_total_step(part, g, lane, step, core)
-            for lane, (part, g) in enumerate(zip(moved, ffn_grads))
-        ]
-        return after
-
-    def outer(left, right):
-        return contract(left, right, ((0,), (0,)))
-
     second_back, second_terms = norm_backward(grad_second, second_gain, second_hat, second_inv)
     grad_mixed = cotangent[0].astype(F32) + second_back
     grad_branch = share(grad_mixed.astype(BF16), core)
-    grad_merged = jnp.dot(grad_branch, out_w, preferred_element_type=F32).astype(BF16)
-    grad_heads = grad_merged.reshape(256, 12, 64)
-    delta = jnp.sum(grad_heads.astype(F32) * attended, axis=-1, keepdims=True)
-    delta_rows = to_blocks(delta).reshape(2, 3, 2, 1, 256)
-    grad_blocks = jnp.pad(to_blocks(grad_heads), ((0, 0),) * 4 + ((64, 0),))
-    (grad_blocks,) = next_running(2, grad_blocks)
-    grad_query_tall, grad_kv = attention_back(
+    grad_merged = contract(out_w, grad_branch, ((0,), (1,))).astype(BF16)
+    grad_qkv, query_terms, key_terms, *running = attention_back(
         slots,
         low_block,
         block_map,
         kv_all,
-        query_blocks,
-        grad_blocks,
-        anchor_rows,
-        start_rows,
-        lse,
-        delta_rows,
+        (*arrived, *ffn_grads),
+        (qkv, *tables),
+        (query_blocks, grad_merged, attended, anchor_rows, start_rows, lse),
     )
-    (grad_kv,) = next_running(3, grad_kv)
-    own_kv = scatter_keys(grad_kv).reshape(256, 3, 128)
-    query_unrot = unrotate(from_blocks(grad_query_tall) * 0.125, cosine, sine)
-    query_back, query_terms = norm_backward(query_unrot, query_gain, query_hat, query_inv)
-    key_unrot = unrotate(own_kv[:, :, :64], cosine, sine)
-    key_back, key_terms = norm_backward(key_unrot, key_gain, key_hat, key_inv)
-    grad_qkv = jnp.concatenate(
-        [
-            query_back.reshape(256, 768),
-            key_back.reshape(256, 192),
-            own_kv[:, :, 64:].reshape(256, 192),
-        ],
-        axis=1,
-    ).astype(BF16)
-    grad_first = total_rows(contract(grad_qkv, qkv_w, ((1,), (1,))), core)
+    grad_first = total_rows(contract(grad_qkv, qkv_w, ((0,), (1,))), core)
     first_back, first_terms = norm_backward(grad_first, first_gain, first_hat, first_inv)
     token_grad = (grad_mixed + first_back).astype(BF16)[None]
 
@@ -1270,16 +1401,15 @@
         [
             jnp.sum(first_terms, axis=0),
             jnp.sum(second_terms, axis=0),
-            jnp.sum(query_terms, axis=(0, 1)),
-            jnp.sum(key_terms, axis=(0, 1)),
+            query_terms[:, 0],
+            key_terms[:, 0],
             jnp.zeros((896,), F32),
         ]
     ).reshape(8, 640)
-    (gains,) = next_running(4, gains)
     qkv_g, out_g, gate_g, up_g, down_g, gains = scatter_weights(
         [
-            outer(first_low, grad_qkv).astype(BF16),
-            outer(grad_branch, merged).astype(BF16),
+            contract(first_low, grad_qkv, ((0,), (1,))).astype(BF16),
+            contract(grad_branch, merged, ((0,), (1,))).astype(BF16),
         ],
         running,
         gains,

time: 528 us -> 452 us (0.86)
  local copies, waits for them, and re-layouts: 45.5 us -> 16 us
  other arithmetic: 50.4 us -> 22.2 us
  Pallas kernels: 357 us -> 346 us
  starting transfers between devices: 25.7 us -> 18.1 us
    convert_element_type x7 -> x0, other arithmetic: 18.3 us -> none  [the longest x6 16.6 us: ring_total_step(): return (arrived.astype(F32) + slab.astype(F32)).astype(BF16)]
    mul x11 -> x0, local copies, waits for them, and re-layouts: 11.5 us -> none  [the longest x3 6.88 us: body(): query_unrot = unrotate(from_blocks(grad_query_tall) * 0.125, cosine, sine)]
    ppermute x12 -> x6, starting transfers between devices: 17.7 us -> 7.61 us  [round_ring(): return lax.ppermute(array, ('ctx', 'wt'), pairs)]
    dot_general x4 -> x6, matrix products: 13.3 us -> 22.5 us  [contract(): lax.dot_general(left, right, (dims, ((), ())), preferred_element_type=F32)]
    pallas_call x4 -> x2, Pallas kernels: 163 us -> 155 us  [the longest x1 97 us: attention_back(): pl.pallas_call(attention_back_kernel, in_specs=[IN_SMEM] * 3 + [ANY] * 5...]
    reshape x6 -> x0, local copies, waits for them, and re-layouts: 5.75 us -> none  [the longest x2 4.45 us: from_blocks(): split = tall.reshape(2, 3, 2, depth, 4, 64)]
    ppermute x12 -> x6, waiting for transfers between devices: 20.9 us -> 16.6 us  [round_ring(): return lax.ppermute(array, ('ctx', 'wt'), pairs)]
  transfers between devices with their start and end apart: 19 -> 13, of which waited for: 7 -> 6; matrix products, arithmetic and copies ran while one was open for 17% -> 8% of each run, Pallas kernels for 43% -> 26%
where the time goes in v4:
time: 452 us; the launch traced here: 446 us
  Pallas kernels  346 us (77%)
  matrix products  22.5 us (5%)
  other arithmetic  22.2 us (5%)
  waiting for transfers between devices  18.9 us (4%)
  starting transfers between devices  18.1 us (4%)
  local copies, waits for them, and re-layouts  16 us (4%)
    pallas_call x1, Pallas kernels, attention_back(): pl.pallas_call(attention_back_kernel, in_specs=[IN_SMEM] * 3 + [ANY] * 5...  97 us
    pallas_call x1, Pallas kernels, gather_weights(): pl.pallas_call(functools.partial(weight_gather_kernel, widths, lanes), ou...  68 us
    pallas_call x1, Pallas kernels, feed_forward(): pl.pallas_call(ffn_kernel, out_shape=[rows] * 2 + [jax.ShapeDtypeStruct((...  66.2 us
    pallas_call x1, Pallas kernels, attention(): pl.pallas_call(attention_kernel, in_specs=[IN_SMEM] * 2 + [IN_VMEM] * 7 +...  57.7 us
    pallas_call x1, Pallas kernels, scatter_weights(): pl.pallas_call(functools.partial(weight_scatter_kernel, widths, lanes), o...  57.5 us
    dot_general x6, matrix products, contract(): lax.dot_general(left, right, (dims, ((), ())), preferred_element_type=F32)  22.5 us
    ppermute x6, waiting for transfers between devices, round_ring(): return lax.ppermute(array, ('ctx', 'wt'), pairs)  16.6 us
  transfers between devices with their start and end apart: 13, of which 6 were waited for; matrix products, arithmetic and copies ran while one was open for 8% of the time, Pallas kernels for 26%

profile of v4, /device:TPU:1, one launch (start us, length us, event | category | flops | bytes accessed | tf_op | source)
XLA Modules:
  0.0 445.7 jit_solution(3024607216250759819)
XLA Ops:
  0.7 0.8 fusion.29
  1.5 0.9 fusion.32
  3.0 68.0 %shard_map.255 = (bf16[2,4,4,2,32,1152]{5,4,3,2,1,0:T(8,128)(2,1)}, bf16[2,4,4,2,32,768]{5,4,3,2,1,0:T(8,128)(2,1)}, bf16[3,4,2,32,640]{4,3,2,1,0:T(8,128)(2,1)}...) custom-call(bf16[16,2304]{1,0:T(8,128)(2,1)} %concatenate.30.refs_0_, bf16[16,1536]{1,0:T(8,128)(2,1)} %refs_1_.1, ...), custom_call_target="tpu_custom_call" | custom-call | tf_op jit(solution)/shard_map/pallas_call | solution.py:405
  71.0 2.8 collective-permute-start
  74.1 1.5 multiply_reduce_fusion
  76.3 1.5 multiply_convert_fusion
  77.9 3.9 fusion.34.refs_2_.refs_8_
  81.8 3.4 collective-permute-done.refs_1_
  85.2 2.2 collective-permute-done.1.refs_5_
  87.4 1.2 collective-permute-start.2
  88.6 0.9 collective-permute-start.3
  89.9 1.6 collective-permute-start.4
  92.8 57.7 %shard_map.256 = (f32[768,256]{1,0:T(8,128)S(1)}, f32[2,3,2,1,256]{4,3,2,1,0:T(1,128)S(1)}, bf16[2,3,2,128,256]{4,3,2,1,0:T(8,128)(2,1)S(1)}, bf16[6,2,4,4,2,64,...) custom-call(s32[64]{0:T(128)S(1)} %select_reduce_fusion.1.refs_0_, s32[1]{0:T(128)S(1)} %bitcast.51, ...), custom_call_target="tpu_custom_call" | custom-call | tf_op jit(solution)/shard_map/pallas_call | solution.py:786
  150.5 2.6 copy-done.2
  153.2 5.0 %fusion.15 = f32[256,2048]{1,0:T(8,128)S(1)} fusion(bf16[2048,768]{1,0:T(8,128)(2,1)} %bitcast.56, f32[768,256]{1,0:T(8,128)S(1)} %get-tuple-element.60.refs_15_), kind=kOutput, calls=%fused_computation.40 | convolution fusion | flops 805502976 | bytes 6029312 | tf_op jit(solution)/shard_map/dot_general | solution.py:617
  158.4 1.2 copy-done.19
  159.6 2.7 collective-permute-start.5
  162.8 2.4 collective-permute-start.6
  165.3 1.6 multiply_reduce_fusion.3
  166.9 0.9 multiply_convert_fusion.1.refs_8_
  167.8 8.8 %collective-permute-done.6.refs_3_ = bf16[3,4,2,32,640]{4,3,2,1,0:T(8,128)(2,1)} collective-permute-done((bf16[3,4,2,32,640]{4,3,2,1,0:T(8,128)(2,1)}, bf16[3,4,2,32,640]{4,3,2,1,0:T(8,128)(2,1)}, u32[]{:S(2)}, u32[]{:S(2)}) %collective-permute-start.6) | collective-permute-done | bytes 983072 | tf_op jit(solution)/shard_map/ppermute | solution.py:1273
  176.6 2.2 collective-permute-done.7.refs_7_
  178.8 66.2 %shard_map.257 = (f32[128,2048]{1,0:T(8,128)}, f32[128,2048]{1,0:T(8,128)}, bf16[128,2048]{1,0:T(8,128)(2,1)}, bf16[128,2048]{1,0:T(8,128)(2,1)}, bf16[128,2048]...) custom-call(bf16[3,4,2,32,640]{4,3,2,1,0:T(8,128)(2,1)} %get-tuple-e, ...), custom_call_target="tpu_custom_call" | custom-call | tf_op jit(solution)/shard_map/pallas_call | solution.py:1198
  245.0 1.7 multiply_reduce_fusion.1
  247.2 1.9 collective-permute-done.11
  249.3 1.8 convolution_convert_fusion.2.refs_14_
  251.0 97.0 %shard_map.258 = (bf16[1152,256]{1,0:T(8,128)(2,1)}, f32[64,1]{1,0:T(8,128)}, f32[64,1]{1,0:T(8,128)}, bf16[3,4,2,32,640]{4,3,2,1,0:T(8,128)(2,1)}, bf16[3,4,2,32,640]{4,3,2,1,0:T(8,128)(2,1)}) custom-call(s32[64]{0:T(128)} %copy-done.16, s32[1]{0:T(128)} %bitcast.52, s32[64]{0:T(128)} %refs_2_.3, bf16[6,2,4,4,2,64,128]{6,5,4,3,2,1,0:T(8,128)(2,1)} %copy-done.2, ...), custom_call_target="tpu_custom_call" | custom-call | tf_op jit(solution)/shard_map/pallas_call | solution.py:1012
  348.0 4.1 fusion.35
  352.2 1.1 constant_dynamic-slice_fusion
  353.2 1.6 collective-permute-start.12
  354.8 1.3 fusion.1
  356.1 0.8 collective-permute-start.10
  357.0 1.4 collective-permute-start.9
  358.4 2.2 collective-permute-start.8
  360.9 4.0 convolution_convert_fusion.1
  364.9 3.7 convolution_convert_fusion
  368.6 2.6 fusion.10
  371.9 57.5 %shard_map.259 = (f32[16,2304]{1,0:T(8,128)}, f32[16,1536]{1,0:T(8,128)}, f32[16,5120]{1,0:T(8,128)}, f32[16,5120]{1,0:T(8,128)}, f32[16,5120]{1,0:T(8,128)}, /*index=5*/f32[8,640]{1,0:T(8,128)}) custom-call(bf16[2,4,4,2,32,1152]{5,4,3,2,1,0:T(8,128)(2,1)} %bitcast.53, bf16[2,4,4,2,32,768]{5,4,3,2,1,0:T(8,128)(2,1)} %bitcast.54, ...), custom_call_target="tpu_custom_call" | custom-call | tf_op jit(solution)/shard_map/pallas_call | solution.py:604
  429.4 0.8 fusion.28
  430.3 0.9 fusion.27
  431.1 0.7 reshape.175
  433.1 1.0 fusion.26
  434.1 1.0 fusion.25
  435.1 1.0 fusion.24
  438.1 0.7 pad_maximum_fusion.3
  438.9 0.7 pad_maximum_fusion.4
  439.6 0.7 pad_maximum_fusion.5
  440.4 4.3 fusion.13
  (127 shorter events, 9.4 us)
Async XLA Ops:
  0.6 75.0 %copy-start.35 = (s32[64]{0:T(128)S(1)}, s32[64]{0:T(128)}, u32[]{:S(2)}) copy-start(s32[64]{0:T(128)} %refs_2_.3) | copy-start | bytes 772
  0.7 75.2 %copy-start.32 = (s32[1,4096]{1,0:T(1,128)S(1)}, s32[1,4096]{1,0:T(1,128)}, u32[]{:S(2)}) copy-start(s32[1,4096]{1,0:T(1,128)} %param.19) | copy-start | bytes 49156
  0.7 75.6 %copy-start.29 = (f32[2048]{0:T(1024)S(1)}, f32[2048]{0:T(1024)}, u32[]{:S(2)}) copy-start(f32[2048]{0:T(1024)} %param.21) | copy-start | bytes 24580
  71.0 14.2 %collective-permute-start = (bf16[3,4,2,32,640]{4,3,2,1,0:T(8,128)(2,1)}, bf16[3,4,2,32,640]{4,3,2,1,0:T(8,128)(2,1)S(1)}, u32[]{:S(2)}, u32[]{:S(2)}) collective-permute-start(bf16[3,4,2,32,640]{4,3,2,1,0:T(8,128)(2,1)} %get-tuple-element.52.refs_0_), channel_id=1, source_target_pairs={{0,4},{1,13},{2,6},{3,15},{4,8},{5,1},{6,10},{7,3},{8,12},{9,5},{1... | collective-permute-start | bytes 2949128 | tf_op jit(solution)/shard_map/ppermute | solution.py:1273
  73.8 13.6 %collective-permute-start.1 = (bf16[3,4,2,32,640]{4,3,2,1,0:T(8,128)(2,1)}, bf16[3,4,2,32,640]{4,3,2,1,0:T(8,128)(2,1)}, u32[]{:S(2)}, u32[]{:S(2)}) collective-permute-start(bf16[3,4,2,32,640]{4,3,2,1,0:T(8,128)(2,1)} %get-tuple-element.53.refs_4_), channel_id=1, source_target_pairs={{0,16},{1,49},{2,18},{3,51},{4,20},{5,53},{6,22},{7,55},{8,24},{9,... | collective-permute-start | bytes 2949128 | tf_op jit(solution)/shard_map/ppermute | solution.py:1273
  75.7 17.1 %copy-start.15 = (s32[2]{0:T(128)}, s32[2]{0:T(128)S(1)}, u32[]{:S(2)}) copy-start(s32[2]{0:T(128)S(1)} %get-tuple-element.99) | copy-start | bytes 28
  77.8 12.0 %copy-start.36 = (s32[1,128]{1,0:T(1,128)S(1)}, s32[1,128]{1,0:T(1,128)}, u32[]{:S(2)}) copy-start(s32[1,128]{1,0:T(1,128)} %param.20) | copy-start | bytes 1540
  77.9 13.8 %copy-start.37 = (f32[64]{0:T(128)S(1)}, f32[64]{0:T(128)}, u32[]{:S(2)}) copy-start(f32[64]{0:T(128)} %param.26) | copy-start | bytes 772
  77.9 13.9 %copy-start.38 = (f32[64]{0:T(128)S(1)}, f32[64]{0:T(128)}, u32[]{:S(2)}) copy-start(f32[64]{0:T(128)} %param.27) | copy-start | bytes 772
  77.9 14.9 %copy-start.4 = (bf16[1,128,2048]{2,1,0:T(8,128)(2,1)S(1)}, bf16[1,128,2048]{2,1,0:T(8,128)(2,1)}, u32[]{:S(2)}) copy-start(bf16[1,128,2048]{2,1,0:T(8,128)(2,1)} %param.17) | copy-start | bytes 1572868
  81.8 76.4 %copy-start.3 = (f32[1152,256]{1,0:T(8,128)}, f32[1152,256]{1,0:T(8,128)S(1)}, u32[]{:S(2)}) copy-start(f32[1152,256]{1,0:T(8,128)S(1)} %fusion.34.refs_2_.refs_8_) | copy-start | bytes 3538948
  85.2 68.0 %copy-start.27 = (bf16[3,4,2,32,640]{4,3,2,1,0:T(8,128)(2,1)}, bf16[3,4,2,32,640]{4,3,2,1,0:T(8,128)(2,1)S(1)}, u32[]{:S(2)}) copy-start(bf16[3,4,2,32,640]{4,3,2,1,0:T(8,128)(2,1)S(1)} %collective-permute-done.refs_1_) | copy-start | bytes 2949124
  87.4 65.8 %collective-permute-start.2 = (bf16[3,4,2,32,640]{4,3,2,1,0:T(8,128)(2,1)S(1)}, bf16[3,4,2,32,640]{4,3,2,1,0:T(8,128)(2,1)}, u32[]{:S(2)}, u32[]{:S(2)}) collective-permute-start(bf16[3,4,2,32,640]{4,3,2,1,0:T(8,128)(2,1)S(1)} %collective-permute-done.refs_1_), channel_id=1, source_target_pairs={{0,4},{1,13},{2,6},{3,15},{4,8},{5,1},{6,10},{7,3},{8,12},{9,5},{1... | collective-permute-start | bytes 2949128 | tf_op jit(solution)/shard_map/ppermute | solution.py:1273
  88.6 64.6 %collective-permute-start.3 = (bf16[3,4,2,32,640]{4,3,2,1,0:T(8,128)(2,1)}, bf16[3,4,2,32,640]{4,3,2,1,0:T(8,128)(2,1)}, u32[]{:S(2)}, u32[]{:S(2)}) collective-permute-start(bf16[3,4,2,32,640]{4,3,2,1,0:T(8,128)(2,1)} %collective-permute-done.1.refs_5_), channel_id=1, source_target_pairs={{0,16},{1,49},{2,18},{3,51},{4,20},{5,53},{6,22},{7,55},{8,24},{9,... | collective-permute-start | bytes 2949128 | tf_op jit(solution)/shard_map/ppermute | solution.py:1273
  89.9 2.4 collective-permute-start.4
  91.6 66.5 %copy-start.16 = (s32[64]{0:T(128)}, s32[64]{0:T(128)S(1)}, u32[]{:S(2)}) copy-start(s32[64]{0:T(128)S(1)} %select_reduce_fusion.1.refs_0_) | copy-start | bytes 772
  91.8 66.4 %copy-start.8 = (f32[64,1]{1,0:T(8,128)}, f32[64,1]{1,0:T(8,128)S(1)}, u32[]{:S(2)}) copy-start(f32[64,1]{1,0:T(8,128)S(1)} %copy.37.refs_5_.refs_11_) | copy-start | bytes 772
  91.9 66.3 %copy-start.9 = (f32[64,1]{1,0:T(8,128)}, f32[64,1]{1,0:T(8,128)S(1)}, u32[]{:S(2)}) copy-start(f32[64,1]{1,0:T(8,128)S(1)} %copy.38.refs_6_.refs_12_) | copy-start | bytes 772
  92.5 65.7 %copy-start.12 = (s32[2,2,1,256]{3,2,1,0:T(1,128)}, s32[2,2,1,256]{3,2,1,0:T(1,128)S(1)}, u32[]{:S(2)}) copy-start(s32[2,2,1,256]{3,2,1,0:T(1,128)S(1)} %broadcast_in_dim.93.refs_8_.refs_17_) | copy-start | bytes 12292
  92.7 65.5 %copy-start.10 = (f32[32,256]{1,0:T(8,128)}, f32[32,256]{1,0:T(8,128)S(1)}, u32[]{:S(2)}) copy-start(f32[32,256]{1,0:T(8,128)S(1)} %get-tuple-element.131.refs_4_.refs_10_) | copy-start | bytes 98308
  92.8 65.5 %copy-start.11 = (f32[32,256]{1,0:T(8,128)}, f32[32,256]{1,0:T(8,128)S(1)}, u32[]{:S(2)}) copy-start(f32[32,256]{1,0:T(8,128)S(1)} %get-tuple-element.132.refs_3_.refs_9_) | copy-start | bytes 98308
  92.8 65.5 %copy-start.13 = (s32[2,2,1,256]{3,2,1,0:T(1,128)}, s32[2,2,1,256]{3,2,1,0:T(1,128)S(1)}, u32[]{:S(2)}) copy-start(s32[2,2,1,256]{3,2,1,0:T(1,128)S(1)} %broadcast_in_dim.90.refs_7_.refs_16_) | copy-start | bytes 12292
  150.5 2.6 copy-start.2
  153.1 5.1 %copy-start = (f32[768,256]{1,0:T(8,128)}, f32[768,256]{1,0:T(8,128)S(1)}, u32[]{:S(2)}) copy-start(f32[768,256]{1,0:T(8,128)S(1)} %get-tuple-element.60.refs_15_) | copy-start | bytes 2359300
  153.1 5.1 %copy-start.6 = (bf16[4,2,128,2048]{3,2,1,0:T(8,128)(2,1)}, bf16[4,2,128,2048]{3,2,1,0:T(8,128)(2,1)S(1)}, u32[]{:S(2)}) copy-start(bf16[4,2,128,2048]{3,2,1,0:T(8,128)(2,1)S(1)} %get-tuple-element.67.refs_10_) | copy-start | bytes 12582916
  153.2 5.1 %copy-start.7 = (bf16[2,3,2,128,256]{4,3,2,1,0:T(8,128)(2,1)}, bf16[2,3,2,128,256]{4,3,2,1,0:T(8,128)(2,1)S(1)}, u32[]{:S(2)}) copy-start(bf16[2,3,2,128,256]{4,3,2,1,0:T(8,128)(2,1)S(1)} %get-tuple-element.78.refs_13_) | copy-start | bytes 2359300
  153.2 5.1 %copy-start.14 = (f32[2,3,2,1,256]{4,3,2,1,0:T(1,128)}, f32[2,3,2,1,256]{4,3,2,1,0:T(1,128)S(1)}, u32[]{:S(2)}) copy-start(f32[2,3,2,1,256]{4,3,2,1,0:T(1,128)S(1)} %get-tuple-element.79.refs_18_) | copy-start | bytes 36868
  158.3 7.0 %copy-start.20 = (bf16[1,128,2048]{2,1,0:T(8,128)(2,1)S(1)}, bf16[1,128,2048]{2,1,0:T(8,128)(2,1)}, u32[]{:S(2)}) copy-start(bf16[1,128,2048]{2,1,0:T(8,128)(2,1)} %param.16) | copy-start | bytes 1572868
  159.6 7.3 %copy-start.30 = (f32[2048]{0:T(1024)S(1)}, f32[2048]{0:T(1024)}, u32[]{:S(2)}) copy-start(f32[2048]{0:T(1024)} %param.28) | copy-start | bytes 24580
  159.6 5.7 %collective-permute-start.5 = (f32[128,2048]{1,0:T(8,128)S(1)}, f32[128,2048]{1,0:T(8,128)S(1)}, u32[]{:S(2)}, u32[]{:S(2)}) collective-permute-start(f32[128,2048]{1,0:T(8,128)S(1)} %constant_dynamic-slice_fusion.1), channel_id=1, source_target_pairs={{0,1},{1,0},{2,3},{3,2},{4,5},{5,4},{6,7},{7,6},{8,9},{9,8},{10,11... | collective-permute-start | bytes 3145736 | tf_op jit(solution)/shard_map/ppermute | solution.py:1228
  162.8 13.8 %collective-permute-start.6 = (bf16[3,4,2,32,640]{4,3,2,1,0:T(8,128)(2,1)}, bf16[3,4,2,32,640]{4,3,2,1,0:T(8,128)(2,1)}, u32[]{:S(2)}, u32[]{:S(2)}) collective-permute-start(bf16[3,4,2,32,640]{4,3,2,1,0:T(8,128)(2,1)} %collective-permute-done.2.refs_2_), channel_id=1, source_target_pairs={{0,4},{1,13},{2,6},{3,15},{4,8},{5,1},{6,10},{7,3},{8,12},{9,5},{1... | collective-permute-start | bytes 2949128 | tf_op jit(solution)/shard_map/ppermute | solution.py:1273
  165.3 13.6 %collective-permute-start.7 = (bf16[3,4,2,32,640]{4,3,2,1,0:T(8,128)(2,1)}, bf16[3,4,2,32,640]{4,3,2,1,0:T(8,128)(2,1)}, u32[]{:S(2)}, u32[]{:S(2)}) collective-permute-start(bf16[3,4,2,32,640]{4,3,2,1,0:T(8,128)(2,1)} %collective-permute-done.3.refs_6_), channel_id=1, source_target_pairs={{0,16},{1,49},{2,18},{3,51},{4,20},{5,53},{6,22},{7,55},{8,24},{9,... | collective-permute-start | bytes 2949128 | tf_op jit(solution)/shard_map/ppermute | solution.py:1273
  246.7 2.5 copy-start.22
  247.1 2.0 collective-permute-start.11
  249.2 1.8 copy-start.25
  352.1 4.0 copy-start.23
  352.1 2.7 copy-start.18
  352.1 8.5 %copy-start.34 = (f32[64,1]{1,0:T(8,128)S(1)}, f32[64,1]{1,0:T(8,128)}, u32[]{:S(2)}) copy-start(f32[64,1]{1,0:T(8,128)} %get-tuple-element.83) | copy-start | bytes 772
  352.1 8.6 %copy-start.33 = (f32[64,1]{1,0:T(8,128)S(1)}, f32[64,1]{1,0:T(8,128)}, u32[]{:S(2)}) copy-start(f32[64,1]{1,0:T(8,128)} %get-tuple-element.84) | copy-start | bytes 772
  352.1 8.7 %copy-start.1 = (f32[768,256]{1,0:T(8,128)S(1)}, f32[768,256]{1,0:T(8,128)}, u32[]{:S(2)}) copy-start(f32[768,256]{1,0:T(8,128)} %copy-done) | copy-start | bytes 2359300
  353.2 15.4 %collective-permute-start.12 = (f32[128,2048]{1,0:T(8,128)}, f32[128,2048]{1,0:T(8,128)}, u32[]{:S(2)}, u32[]{:S(2)}) collective-permute-start(f32[128,2048]{1,0:T(8,128)} %constant_dynamic-slice_fusion), channel_id=1, source_target_pairs={{0,1},{1,0},{2,3},{3,2},{4,5},{5,4},{6,7},{7,6},{8,9},{9,8},{10,11... | collective-permute-start | bytes 3145736 | tf_op jit(solution)/shard_map/ppermute | solution.py:1228
  356.1 84.2 %collective-permute-start.10 = (bf16[128,2048]{1,0:T(8,128)(2,1)}, bf16[128,2048]{1,0:T(8,128)(2,1)}, u32[]{:S(2)}, u32[]{:S(2)}) collective-permute-start(bf16[128,2048]{1,0:T(8,128)(2,1)} %get-tuple-element.71), channel_id=1, source_target_pairs={{0,2},{1,3},{64,66},{65,67},{2,0},{3,1},{66,64},{67,65},{4,6},{5,7... | collective-permute-start | bytes 1572872 | tf_op jit(solution)/shard_map/ppermute | solution.py:1259
  357.0 83.4 %collective-permute-start.9 = (bf16[128,2048]{1,0:T(8,128)(2,1)}, bf16[128,2048]{1,0:T(8,128)(2,1)}, u32[]{:S(2)}, u32[]{:S(2)}) collective-permute-start(bf16[128,2048]{1,0:T(8,128)(2,1)} %get-tuple-element.70), channel_id=1, source_target_pairs={{0,64},{1,65},{64,2},{65,3},{2,66},{3,67},{66,0},{67,1},{4,68},{5,... | collective-permute-start | bytes 1572872 | tf_op jit(solution)/shard_map/ppermute | solution.py:1259
  358.4 81.9 %collective-permute-start.8 = (bf16[128,2048]{1,0:T(8,128)(2,1)}, bf16[128,2048]{1,0:T(8,128)(2,1)}, u32[]{:S(2)}, u32[]{:S(2)}) collective-permute-start(bf16[128,2048]{1,0:T(8,128)(2,1)} %get-tuple-element.69), channel_id=1, source_target_pairs={{0,66},{1,67},{64,0},{65,1},{2,64},{3,65},{66,2},{67,3},{4,70},{5,... | collective-permute-start | bytes 1572872 | tf_op jit(solution)/shard_map/ppermute | solution.py:1259
  360.8 4.0 copy-start.21
  360.8 4.0 copy-start.28
  364.9 3.7 copy-start.24
  440.3 4.3 copy-start.31
  (4 other events, 6.5 us)
